TPU v7x, 32 devices: a whole 2x2x4 slice. The times are simulated.
32 devices in a mesh: rep: 16 (over z, y, core), shard: 2 (over x).
Axes of the slice: x: 2, y: 2, z: 4, core: 2. Of those that a mesh axis runs over, the one named last changes fastest.
Arguments:
- stream_in: bfloat16 [4096, 2048], P(('rep', 'shard')), may hold values from -6 to 6
- stream_grad: bfloat16 [4096, 2048], P(('rep', 'shard')), may hold values from -6 to 6
- prefix_len: int32 [16], replicated, may hold values from 1 to 256, as said below
- routes: int32 [4096, 6], P(('rep', 'shard')), may hold values from 0 to 15, all different within a row; in each aligned block of 128 rows (0 to 127, 128 to 255, ...) at most 56 rows name the same one
- route_weight: float32 [4096, 6], P(('rep', 'shard')), may hold values from 0.5 to 2
- attn_gain: bfloat16 [2048], P('shard'), may hold values from 0.5 to 1.5
- query_proj: bfloat16 [2048, 3072], P('shard'), may hold values from -0.125 to 0.125
- latent_proj: bfloat16 [2048, 512], P('shard'), may hold values from -0.125 to 0.125
- rope_key_proj: bfloat16 [2048, 64], P('shard'), may hold values from -0.125 to 0.125
- latent_gain: bfloat16 [512], P('shard'), may hold values from 0.5 to 1.5
- kv_up_proj: bfloat16 [512, 4096], P('shard'), may hold values from -0.25 to 0.25
- out_proj: bfloat16 [2048, 2048], P('shard'), may hold values from -0.75 to 0.75
- ffn_gain: bfloat16 [2048], P('shard'), may hold values from 0.5 to 1.5
- router_proj: bfloat16 [2048, 16], P('shard'), may hold values from -0.06591797 to 0.06591797
- shared_gate: bfloat16 [2048, 2816], P(('rep', 'shard')), may hold values from -0.125 to 0.125
- shared_up: bfloat16 [2048, 2816], P(('rep', 'shard')), may hold values from -0.125 to 0.125
- shared_down: bfloat16 [2816, 2048], P(('rep', 'shard')), may hold values from -0.109375 to 0.109375
- expert_gate: bfloat16 [16, 2048, 1408], P('rep', None, 'shard'), may hold values from -0.125 to 0.125
- expert_up: bfloat16 [16, 2048, 1408], P('rep', None, 'shard'), may hold values from -0.125 to 0.125
- expert_down: bfloat16 [16, 1408, 2048], P('rep', 'shard'), may hold values from -0.15625 to 0.15625
Outputs:
- stream_out: bfloat16 [4096, 2048], P(('rep', 'shard'))
- grad_stream: bfloat16 [4096, 2048], P(('rep', 'shard'))
- stats: float32 [5], replicated
- grad_attn_gain: float32 [2048], P(('rep', 'shard'))
- grad_query_proj: float32 [2048, 3072], P(('rep', 'shard'))
- grad_latent_proj: float32 [2048, 512], P(('rep', 'shard'))
- grad_rope_key_proj: float32 [2048, 64], P(('rep', 'shard'))
- grad_latent_gain: float32 [512], P(('rep', 'shard'))
- grad_kv_up_proj: float32 [512, 4096], P(('rep', 'shard'))
- grad_out_proj: float32 [2048, 2048], P(('rep', 'shard'))
- grad_ffn_gain: float32 [2048], P(('rep', 'shard'))
- grad_router_proj: float32 [2048, 16], P(('rep', 'shard'))
- grad_shared_gate: float32 [2048, 2816], P(('rep', 'shard'))
- grad_shared_up: float32 [2048, 2816], P(('rep', 'shard'))
- grad_shared_down: float32 [2816, 2048], P(('rep', 'shard'))
- grad_expert_gate: float32 [16, 2048, 1408], P('rep', None, 'shard')
- grad_expert_up: float32 [16, 2048, 1408], P('rep', None, 'shard')
- grad_expert_down: float32 [16, 1408, 2048], P('rep', 'shard')
Inputs may be any that keep to these rules, and one draw needn't show every extreme that they name: `prefix_len`: one sequence, drawn from the seed, has a prefix of 256. `routes`: each row names 6 different experts; among the rows of one device no expert is named more than 56 times.
All inputs are finite; a program needn't handle non-finite values.
Results may differ from a plain program's by a relative error of at most 0.018.
Values may be sent and summed in bfloat16 or wider, within the bound.
A program may use at most 384 MiB of HBM per device.

v0:
```python
import jax
import jax.numpy as jnp
from jax import lax
from jax.sharding import PartitionSpec as P

D = 2048
H = 16
DN = 128
DR = 64
DV = 128
TOP_K = 6


EPS = 1e-06
ROPE_BASE = 10000.0
MASKED = -1e30


def wide_product(left, right):
    return jnp.dot(left, right, preferred_element_type=jnp.float32)


def rms_scale(values):
    return lax.rsqrt(jnp.mean(values * values, axis=-1, keepdims=True) + EPS)


def norm_back(grad_out, inputs, row_scale, gain_vec):
    weighted = grad_out * gain_vec
    inner_mean = jnp.mean(weighted * inputs, axis=-1, keepdims=True)
    grad_in = row_scale * weighted - inputs * (row_scale * row_scale * row_scale) * inner_mean
    grad_gain = jnp.sum(grad_out * inputs * row_scale, axis=0)
    return (grad_in, grad_gain)


def rope_tables(positions, rope_width):
    frequency = ROPE_BASE ** (-2.0 * jnp.arange(rope_width // 2, dtype=jnp.float32) / rope_width)
    angles = positions.astype(jnp.float32)[:, None] * frequency[None, :]
    return (jnp.cos(angles), jnp.sin(angles))


def rotate(values, cosine, sine_vals):
    half_dim = values.shape[-1] // 2
    low_half = values[..., :half_dim]
    high_half = values[..., half_dim:]
    return jnp.concatenate(
        [low_half * cosine - high_half * sine_vals, high_half * cosine + low_half * sine_vals],
        axis=-1,
    )


def swish_derivative(values):
    sigmoid = jax.nn.sigmoid(values)
    return sigmoid * (1.0 + values * (1.0 - sigmoid))


def on_device(
    stream_in,
    stream_grad,
    prefix_len,
    routes,
    route_weight,
    attn_gain,
    query_proj,
    latent_proj,
    rope_key_proj,
    latent_gain,
    kv_up_proj,
    out_proj,
    ffn_gain,
    router_proj,
    shared_gate,
    shared_up,
    shared_down,
    expert_gate,
    expert_up,
    expert_down,
):
    n_shard = lax.axis_size("shard")
    n_rep = lax.axis_size("rep")
    rep_index = lax.axis_index("rep")
    shard_index = lax.axis_index("shard")
    tok_rows = stream_in.shape[0]
    seq_len = n_shard * tok_rows
    experts = router_proj.shape[1]
    capacity = max(2, tok_rows * TOP_K * 7 // (6 * experts))
    head_width = H * (DN + DV)
    kv_rows = tok_rows * head_width // 128
    rope_rows = tok_rows * DR // 128
    piece_rows = kv_rows + rope_rows
    score_scale = (DN + DR) ** (-0.5)
    weights = (
        attn_gain,
        query_proj,
        latent_proj,
        rope_key_proj,
        latent_gain,
        kv_up_proj,
        out_proj,
        ffn_gain,
        router_proj,
    )
    shared_mats = (shared_gate, shared_up, shared_down)
    (
        gain_attn,
        mat_query,
        mat_latent,
        mat_rope,
        gain_latent,
        mat_kv,
        mat_out,
        gain_ffn,
        mat_router,
    ) = (
        lax.all_gather(weights[0], "shard", axis=0, tiled=True),
        lax.all_gather(weights[1], "shard", axis=0, tiled=True),
        lax.all_gather(weights[2], "shard", axis=0, tiled=True),
        lax.all_gather(weights[3], "shard", axis=0, tiled=True),
        lax.all_gather(weights[4], "shard", axis=0, tiled=True),
        lax.all_gather(weights[5], "shard", axis=0, tiled=True),
        lax.all_gather(weights[6], "shard", axis=0, tiled=True),
        lax.all_gather(weights[7], "shard", axis=0, tiled=True),
        lax.all_gather(weights[8], "shard", axis=0, tiled=True),
    )
    mat_sgate, mat_sup, mat_sdown = (
        lax.all_gather(shared_mats[0], ("rep", "shard"), axis=0, tiled=True),
        lax.all_gather(shared_mats[1], ("rep", "shard"), axis=0, tiled=True),
        lax.all_gather(shared_mats[2], ("rep", "shard"), axis=0, tiled=True),
    )
    gain_attn = gain_attn.astype(jnp.float32)
    gain_latent = gain_latent.astype(jnp.float32)
    gain_ffn = gain_ffn.astype(jnp.float32)
    stream = stream_in.astype(jnp.float32)
    scale_one = rms_scale(stream)
    normed = (stream * scale_one * gain_attn).astype(jnp.bfloat16)
    positions = shard_index * tok_rows + jnp.arange(tok_rows)
    cosine, sine_vals = rope_tables(positions, DR)
    query_raw = wide_product(normed, mat_query).reshape(tok_rows, H, DN + DR)
    query_nope = query_raw[:, :, :DN].astype(jnp.bfloat16)
    query_rot = rotate(query_raw[:, :, DN:], cosine[:, None], sine_vals[:, None]).astype(
        jnp.bfloat16
    )
    latent = wide_product(normed, mat_latent)
    scale_lat = rms_scale(latent)
    latent_normed = (latent * scale_lat * gain_latent).astype(jnp.bfloat16)
    keyval_own = wide_product(latent_normed, mat_kv).astype(jnp.bfloat16)
    key_rot_own = rotate(wide_product(normed, mat_rope), cosine, sine_vals).astype(jnp.bfloat16)
    packed = jnp.concatenate(
        [keyval_own.reshape(kv_rows, 128), key_rot_own.reshape(rope_rows, 128)], axis=0
    )
    seq_keys = lax.all_gather(packed, "shard", axis=0, tiled=True).reshape(n_shard, piece_rows, 128)
    keyval = seq_keys[:, :kv_rows].reshape(seq_len, H, DN + DV)
    key_rot = seq_keys[:, kv_rows:].reshape(seq_len, DR)
    key_nope = keyval[:, :, :DN]
    values = keyval[:, :, DN:]
    prefix = lax.dynamic_index_in_dim(prefix_len, rep_index, keepdims=False)
    key_pos = jnp.arange(seq_len)
    allowed = (key_pos[None, :] <= positions[:, None]) | (key_pos[None, :] < prefix)

    def score_block():
        raw = jnp.einsum("thd,khd->htk", query_nope, key_nope, preferred_element_type=jnp.float32)
        raw = raw + jnp.einsum(
            "thd,kd->htk", query_rot, key_rot, preferred_element_type=jnp.float32
        )
        return jnp.where(allowed[None], raw * score_scale, MASKED)

    scores = score_block()
    top_score = jnp.max(scores, axis=-1, keepdims=True)
    expo = jnp.exp(scores - top_score)
    total_exp = jnp.sum(expo, axis=-1, keepdims=True)
    log_total = top_score + jnp.log(total_exp)
    probs_low = (expo / total_exp).astype(jnp.bfloat16)
    attended = jnp.einsum("htk,khd->thd", probs_low, values, preferred_element_type=jnp.float32)
    attended = attended.reshape(tok_rows, H * DV).astype(jnp.bfloat16)
    attn_out = wide_product(attended, mat_out)
    mid = stream + attn_out
    scale_two = rms_scale(mid)
    normed_two = (mid * scale_two * gain_ffn).astype(jnp.bfloat16)
    router_prob = jax.nn.softmax(wide_product(normed_two, mat_router), axis=-1)
    one_hot = (routes[:, :, None] == jnp.arange(experts)[None, None, :]).astype(jnp.float32)
    picked = jnp.sum(one_hot * router_prob[:, None, :], axis=-1)
    picked_sum = jnp.sum(picked, axis=-1, keepdims=True)
    gates = route_weight * picked / picked_sum
    sgate_val = wide_product(normed_two, mat_sgate)
    sup_val = wide_product(normed_two, mat_sup)
    shared_hidden = (jax.nn.silu(sgate_val) * sup_val).astype(jnp.bfloat16)
    shared_out = wide_product(shared_hidden, mat_sdown)
    flat_routes = routes.reshape(-1)
    route_hot = (flat_routes[:, None] == jnp.arange(experts)[None, :]).astype(jnp.int32)
    route_rank = jnp.sum((jnp.cumsum(route_hot, axis=0) - route_hot) * route_hot, axis=1)
    slot_index = flat_routes * capacity + route_rank
    send_rows = (
        jnp.zeros((experts * capacity, D), jnp.bfloat16)
        .at[slot_index]
        .set(jnp.repeat(normed_two, TOP_K, axis=0))
    )
    doubled = jnp.broadcast_to(
        send_rows.reshape(experts, 1, capacity, D), (experts, n_shard, capacity, D)
    ).reshape(-1, D)
    incoming_rows = lax.all_to_all(
        doubled, ("rep", "shard"), split_axis=0, concat_axis=0, tiled=True
    )
    gate_local = expert_gate[0]
    local_up_weight = expert_up[0]
    down_local = expert_down[0]
    expert_gate_value = wide_product(incoming_rows, gate_local)
    expert_up_value = wide_product(incoming_rows, local_up_weight)
    expert_inner_state = (jax.nn.silu(expert_gate_value) * expert_up_value).astype(jnp.bfloat16)
    expert_part = wide_product(expert_inner_state, down_local).astype(jnp.bfloat16)
    returned = lax.all_to_all(
        expert_part, ("rep", "shard"), split_axis=0, concat_axis=0, tiled=True
    )
    expert_sum = jnp.sum(
        returned.reshape(experts, n_shard, capacity, D).astype(jnp.float32), axis=1
    ).reshape(experts * capacity, D)
    picked_rows = expert_sum[slot_index].reshape(tok_rows, TOP_K, D)
    ffn_out = shared_out + jnp.sum(gates[:, :, None] * picked_rows, axis=1)
    residual = mid + ffn_out
    squares = jnp.stack(
        [
            jnp.sum(stream * stream),
            jnp.sum(attn_out * attn_out),
            jnp.sum(mid * mid),
            jnp.sum(ffn_out * ffn_out),
            jnp.sum(residual * residual),
        ]
    )
    totals = lax.psum(squares, ("rep", "shard"))
    stats = jnp.sqrt(totals / (tok_rows * n_rep * n_shard * D))
    (
        gain_attn,
        mat_query,
        mat_latent,
        mat_rope,
        gain_latent,
        mat_kv,
        mat_out,
        gain_ffn,
        mat_router,
    ) = (
        lax.all_gather(weights[0], "shard", axis=0, tiled=True),
        lax.all_gather(weights[1], "shard", axis=0, tiled=True),
        lax.all_gather(weights[2], "shard", axis=0, tiled=True),
        lax.all_gather(weights[3], "shard", axis=0, tiled=True),
        lax.all_gather(weights[4], "shard", axis=0, tiled=True),
        lax.all_gather(weights[5], "shard", axis=0, tiled=True),
        lax.all_gather(weights[6], "shard", axis=0, tiled=True),
        lax.all_gather(weights[7], "shard", axis=0, tiled=True),
        lax.all_gather(weights[8], "shard", axis=0, tiled=True),
    )
    mat_sgate, mat_sup, mat_sdown = (
        lax.all_gather(shared_mats[0], ("rep", "shard"), axis=0, tiled=True),
        lax.all_gather(shared_mats[1], ("rep", "shard"), axis=0, tiled=True),
        lax.all_gather(shared_mats[2], ("rep", "shard"), axis=0, tiled=True),
    )
    gain_attn = gain_attn.astype(jnp.float32)
    gain_latent = gain_latent.astype(jnp.float32)
    gain_ffn = gain_ffn.astype(jnp.float32)
    grad_top = stream_grad.astype(jnp.float32)
    gate_grad = jnp.sum(grad_top[:, None, :] * picked_rows, axis=-1)
    expert_grad = (gates[:, :, None] * grad_top[:, None, :]).astype(jnp.bfloat16).reshape(-1, D)
    send_grad = jnp.zeros((experts * capacity, D), jnp.bfloat16).at[slot_index].set(expert_grad)
    doubled_grad = jnp.broadcast_to(
        send_grad.reshape(experts, 1, capacity, D), (experts, n_shard, capacity, D)
    ).reshape(-1, D)
    received_grad = lax.all_to_all(
        doubled_grad, ("rep", "shard"), split_axis=0, concat_axis=0, tiled=True
    )
    grad_edown = jnp.einsum(
        "rf,rd->fd", expert_inner_state, received_grad, preferred_element_type=jnp.float32
    )
    inner_state_gradient = jnp.einsum(
        "rd,fd->rf", received_grad, down_local, preferred_element_type=jnp.float32
    )
    gate_value_gradient = (
        inner_state_gradient * expert_up_value * swish_derivative(expert_gate_value)
    ).astype(jnp.bfloat16)
    up_value_gradient = (inner_state_gradient * jax.nn.silu(expert_gate_value)).astype(jnp.bfloat16)
    grad_egate = jnp.einsum(
        "ux,ub->xb", incoming_rows, gate_value_gradient, preferred_element_type=jnp.float32
    )
    expert_up_gradient = jnp.einsum(
        "ux,ub->xb", incoming_rows, up_value_gradient, preferred_element_type=jnp.float32
    )
    part_in_grad = jnp.einsum(
        "rf,df->rd", gate_value_gradient, gate_local, preferred_element_type=jnp.float32
    )
    part_in_grad = (
        part_in_grad
        + jnp.einsum(
            "rf,df->rd", up_value_gradient, local_up_weight, preferred_element_type=jnp.float32
        )
    ).astype(jnp.bfloat16)
    returned_grad = lax.all_to_all(
        part_in_grad, ("rep", "shard"), split_axis=0, concat_axis=0, tiled=True
    )
    slot_grad = jnp.sum(
        returned_grad.reshape(experts, n_shard, capacity, D).astype(jnp.float32), axis=1
    ).reshape(experts * capacity, D)
    routed_grad = jnp.sum(slot_grad[slot_index].reshape(tok_rows, TOP_K, D), axis=1)
    shared_hidden_grad = jnp.einsum(
        "td,fd->tf", stream_grad, mat_sdown, preferred_element_type=jnp.float32
    )
    dshared_gate = (shared_hidden_grad * sup_val * swish_derivative(sgate_val)).astype(jnp.bfloat16)
    dshared_up = (shared_hidden_grad * jax.nn.silu(sgate_val)).astype(jnp.bfloat16)
    weighted_grad = route_weight * gate_grad
    picked_grad = weighted_grad / picked_sum - jnp.sum(
        weighted_grad * picked, axis=-1, keepdims=True
    ) / (picked_sum * picked_sum)
    prob_grad = jnp.sum(one_hot * picked_grad[:, :, None], axis=1)
    logit_grad = (
        router_prob * (prob_grad - jnp.sum(router_prob * prob_grad, axis=-1, keepdims=True))
    ).astype(jnp.bfloat16)
    normed_two_grad = jnp.einsum(
        "tf,df->td", dshared_gate, mat_sgate, preferred_element_type=jnp.float32
    )
    normed_two_grad = normed_two_grad + jnp.einsum(
        "tf,df->td", dshared_up, mat_sup, preferred_element_type=jnp.float32
    )
    normed_two_grad = normed_two_grad + jnp.einsum(
        "te,de->td", logit_grad, mat_router, preferred_element_type=jnp.float32
    )
    normed_two_grad = normed_two_grad + routed_grad
    norm_part, grad_gain_ffn = norm_back(normed_two_grad, mid, scale_two, gain_ffn)
    mid_grad = grad_top + norm_part
    attn_out_grad = mid_grad.astype(jnp.bfloat16)
    attended_grad = jnp.einsum(
        "td,vd->tv", attn_out_grad, mat_out, preferred_element_type=jnp.float32
    )
    attended_grad = attended_grad.astype(jnp.bfloat16).reshape(tok_rows, H, DV)
    probs_full = jnp.where(allowed[None], jnp.exp(score_block() - log_total), 0.0)
    value_grad = jnp.einsum(
        "htk,thd->khd",
        probs_full.astype(jnp.bfloat16),
        attended_grad,
        preferred_element_type=jnp.float32,
    )
    prob_att_grad = jnp.einsum(
        "thd,khd->htk", attended_grad, values, preferred_element_type=jnp.float32
    )
    scores_grad = probs_full * (
        prob_att_grad - jnp.sum(probs_full * prob_att_grad, axis=-1, keepdims=True)
    )
    scores_grad = scores_grad.astype(jnp.bfloat16)
    query_nope_grad = score_scale * jnp.einsum(
        "htk,khd->thd", scores_grad, key_nope, preferred_element_type=jnp.float32
    )
    query_rot_grad = score_scale * jnp.einsum(
        "htk,kd->thd", scores_grad, key_rot, preferred_element_type=jnp.float32
    )
    key_nope_grad = score_scale * jnp.einsum(
        "htk,thd->khd", scores_grad, query_nope, preferred_element_type=jnp.float32
    )
    key_rot_grad = score_scale * jnp.einsum(
        "htk,thd->kd", scores_grad, query_rot, preferred_element_type=jnp.float32
    )
    keyval_grad_all = jnp.concatenate([key_nope_grad, value_grad], axis=-1).reshape(
        n_shard, kv_rows, 128
    )
    key_grad_pieces = jnp.concatenate(
        [keyval_grad_all, key_rot_grad.reshape(n_shard, rope_rows, 128)], axis=1
    )
    own_keys = lax.psum_scatter(
        key_grad_pieces.reshape(-1, 128).astype(jnp.bfloat16),
        "shard",
        scatter_dimension=0,
        tiled=True,
    ).astype(jnp.float32)
    keyval_grad = own_keys[:kv_rows].reshape(tok_rows, head_width).astype(jnp.bfloat16)
    key_pre_grad = rotate(own_keys[kv_rows:].reshape(tok_rows, DR), cosine, -sine_vals).astype(
        jnp.bfloat16
    )
    query_rot_back = rotate(query_rot_grad, cosine[:, None], -sine_vals[:, None])
    query_grad = (
        jnp.concatenate([query_nope_grad, query_rot_back], axis=-1)
        .reshape(tok_rows, H * (DN + DR))
        .astype(jnp.bfloat16)
    )
    latent_normed_grad = jnp.einsum(
        "tc,lc->tl", keyval_grad, mat_kv, preferred_element_type=jnp.float32
    )
    latent_pre, grad_gain_latent = norm_back(latent_normed_grad, latent, scale_lat, gain_latent)
    latent_grad = latent_pre.astype(jnp.bfloat16)
    normed_grad = jnp.einsum("tq,dq->td", query_grad, mat_query, preferred_element_type=jnp.float32)
    normed_grad = normed_grad + jnp.einsum(
        "tr,dr->td", key_pre_grad, mat_rope, preferred_element_type=jnp.float32
    )
    normed_grad = normed_grad + jnp.einsum(
        "tl,dl->td", latent_grad, mat_latent, preferred_element_type=jnp.float32
    )
    attn_part, grad_gain_attn = norm_back(normed_grad, stream, scale_one, gain_attn)
    grad_stream = (mid_grad + attn_part).astype(jnp.bfloat16)
    owned = (
        lax.psum_scatter(
            grad_gain_attn[None][0], ("rep", "shard"), scatter_dimension=0, tiled=True
        ),
        lax.psum_scatter(
            jnp.einsum("td,tq->dq", normed, query_grad, preferred_element_type=jnp.float32),
            ("rep", "shard"),
            scatter_dimension=0,
            tiled=True,
        ),
        lax.psum_scatter(
            jnp.einsum("td,tl->dl", normed, latent_grad, preferred_element_type=jnp.float32),
            ("rep", "shard"),
            scatter_dimension=0,
            tiled=True,
        ),
        lax.psum_scatter(
            jnp.einsum("td,tr->dr", normed, key_pre_grad, preferred_element_type=jnp.float32),
            ("rep", "shard"),
            scatter_dimension=0,
            tiled=True,
        ),
        lax.psum_scatter(
            grad_gain_latent[None][0], ("rep", "shard"), scatter_dimension=0, tiled=True
        ),
        lax.psum_scatter(
            jnp.einsum("tl,tc->lc", latent_normed, keyval_grad, preferred_element_type=jnp.float32),
            ("rep", "shard"),
            scatter_dimension=0,
            tiled=True,
        ),
        lax.psum_scatter(
            jnp.einsum("tv,td->vd", attended, attn_out_grad, preferred_element_type=jnp.float32),
            ("rep", "shard"),
            scatter_dimension=0,
            tiled=True,
        ),
        lax.psum_scatter(grad_gain_ffn[None][0], ("rep", "shard"), scatter_dimension=0, tiled=True),
        lax.psum_scatter(
            jnp.einsum("td,te->de", normed_two, logit_grad, preferred_element_type=jnp.float32),
            ("rep", "shard"),
            scatter_dimension=0,
            tiled=True,
        ),
        lax.psum_scatter(
            jnp.einsum("td,tf->df", normed_two, dshared_gate, preferred_element_type=jnp.float32),
            ("rep", "shard"),
            scatter_dimension=0,
            tiled=True,
        ),
        lax.psum_scatter(
            jnp.einsum("td,tf->df", normed_two, dshared_up, preferred_element_type=jnp.float32),
            ("rep", "shard"),
            scatter_dimension=0,
            tiled=True,
        ),
        lax.psum_scatter(
            jnp.einsum("tf,td->fd", shared_hidden, stream_grad, preferred_element_type=jnp.float32),
            ("rep", "shard"),
            scatter_dimension=0,
            tiled=True,
        ),
    )
    return (
        residual.astype(jnp.bfloat16),
        grad_stream,
        stats,
        owned[0],
        owned[1],
        owned[2],
        owned[3],
        owned[4],
        owned[5],
        owned[6],
        owned[7],
        owned[8],
        owned[9],
        owned[10],
        owned[11],
        grad_egate[None],
        expert_up_gradient[None],
        grad_edown[None],
    )


def solution(mesh):
    placed = (
        P(("rep", "shard"), None),
        P(("rep", "shard"), None),
        P(),
        P(("rep", "shard"), None),
        P(("rep", "shard"), None),
        P("shard"),
        P("shard", None),
        P("shard", None),
        P("shard", None),
        P("shard"),
        P("shard", None),
        P("shard", None),
        P("shard"),
        P("shard", None),
        P(("rep", "shard"), None),
        P(("rep", "shard"), None),
        P(("rep", "shard"), None),
        P("rep", None, "shard"),
        P("rep", None, "shard"),
        P("rep", "shard", None),
    )
    return jax.shard_map(
        on_device,
        mesh=mesh,
        in_specs=placed,
        out_specs=(
            P(("rep", "shard"), None),
            P(("rep", "shard"), None),
            P(),
            P(("rep", "shard")),
            P(("rep", "shard"), None),
            P(("rep", "shard"), None),
            P(("rep", "shard"), None),
            P(("rep", "shard")),
            P(("rep", "shard"), None),
            P(("rep", "shard"), None),
            P(("rep", "shard")),
            P(("rep", "shard"), None),
            P(("rep", "shard"), None),
            P(("rep", "shard"), None),
            P(("rep", "shard"), None),
            P("rep", None, "shard"),
            P("rep", None, "shard"),
            P("rep", "shard", None),
        ),
        check_vma=False,
    )
```

profile of v0, /device:TPU:0, one launch (start us, length us, event | category | flops | bytes accessed | tf_op | source)
XLA Modules:
  0.0 4069.3 jit_solution(15590476726390060768)
XLA Ops:
  28.6 18.3 all-gather.10.cloned.1.call-done
  50.2 55.0 %all-gather.12.cloned.1.call-done = bf16[512,4096]{1,0:T(8,128)(2,1)} async-done(((bf16[256,4096]{1,0:T(8,128)(2,1)}), bf16[512,4096]{1,0:T(8,128)(2,1)}) %all-gather.12.cloned.1.call-update) | async-done | bytes 4194320 | tf_op jit(solution)/shard_map/all_gather | solution.py:119
  129.6 17.9 all-gather.14.cloned.1.call-done
  163.3 138.2 %all-gather.16.cloned.1.call-done = bf16[2048,3072]{1,0:T(8,128)(2,1)} async-done(((bf16[1024,3072]{1,0:T(8,128)(2,1)}), bf16[2048,3072]{1,0:T(8,128)(2,1)}) %all-gather.16.cloned.1.call-update) | async-done | bytes 12582928 | tf_op jit(solution)/shard_map/all_gather | solution.py:115
  314.1 92.8 %all-gather.18.cloned.1.call-done = bf16[2048,2048]{1,0:T(8,128)(2,1)} async-done(((bf16[1024,2048]{1,0:T(8,128)(2,1)}), bf16[2048,2048]{1,0:T(8,128)(2,1)}) %all-gather.18.cloned.1.call-update) | async-done | bytes 8388624 | tf_op jit(solution)/shard_map/all_gather | solution.py:120
  422.7 10.4 scatter_custom_fusion
  458.4 41.1 %all_gather.63 = bf16[2048,16]{0,1:T(8,128)(2,1)S(1)} all-gather(bf16[1024,16]{0,1:T(8,128)(2,1)S(1)} %copy-done.60), channel_id=1, replica_groups=mesh['rep'=16,'shard'=2] {'shard'}, dimensions={0}, use_global_device_ids=true | all-gather | bytes 98304 | tf_op jit(solution)/shard_map/all_gather | solution.py:122
  500.7 14.6 scatter_custom_fusion.1
  515.3 183.4 %all-to-all-done = bf16[32,56,2048]{2,1,0:T(8,128)(2,1)} async-done(((bf16[32,56,2048]{2,1,0:T(8,128)(2,1)}), bf16[32,56,2048]{2,1,0:T(8,128)(2,1)}, u32[]{:S(2)}, u32[]{:S(2)}) %all-to-all-start) | async-done | bytes 7340064 | tf_op jit(solution)/shard_map/all_to_all | solution.py:199
  708.5 10.8 fusion.7
  729.4 140.5 %all-to-all-done.2 = bf16[32,56,2048]{2,1,0:T(8,128)(2,1)} async-done(((bf16[32,56,2048]{2,1,0:T(8,128)(2,1)}), bf16[32,56,2048]{2,1,0:T(8,128)(2,1)}, u32[]{:S(2)}, u32[]{:S(2)}) %all-to-all-start.2) | async-done | bytes 7340064 | tf_op jit(solution)/shard_map/all_to_all | solution.py:265
  869.9 13.1 multiply_convert_fusion.1
  898.4 10.9 fusion.9
  909.4 11.5 add_convert_fusion
  920.9 192.0 %all-to-all-done.1 = bf16[32,56,2048]{2,1,0:T(8,128)(2,1)} async-done(((bf16[32,56,2048]{2,1,0:T(8,128)(2,1)}), bf16[32,56,2048]{2,1,0:T(8,128)(2,1)}, u32[]{:S(2)}, u32[]{:S(2)}) %all-to-all-start.1) | async-done | bytes 7340064 | tf_op jit(solution)/shard_map/all_to_all | solution.py:209
  1164.2 10.3 gather_fusion
  1189.9 88.5 %all-to-all-done.3 = bf16[32,56,2048]{2,1,0:T(8,128)(2,1)} async-done(((bf16[32,56,2048]{2,1,0:T(8,128)(2,1)}), bf16[32,56,2048]{2,1,0:T(8,128)(2,1)}, u32[]{:S(2)}, u32[]{:S(2)}) %all-to-all-start.3) | async-done | bytes 7340064 | tf_op jit(solution)/shard_map/all_to_all | solution.py:293
  1286.9 10.3 gather_fusion.1
  1342.5 32.5 reduce-scatter.13.cloned.1.call-done
  1438.0 10.5 fusion.86
  1458.6 10.4 convolution_bitcast_fusion
  1469.0 10.2 convolution_bitcast_fusion.1
  1479.2 33.0 reduce-scatter.31.cloned.1.call-done
  1528.9 37.4 all-reduce.3
  1571.9 74.7 %reduce-scatter.19.cloned.1.call-done = f32[64,64]{1,0:T(8,128)} async-done(((f32[2048,64]{1,0:T(8,128)}), f32[64,64]{1,0:T(8,128)}) %reduce-scatter.19.cloned.1.call-update) | async-done | bytes 16400 | tf_op jit(solution)/shard_map/reduce_scatter | solution.py:408
  1646.6 140.8 %reduce-scatter.17.cloned.1.call-done = f32[64,512]{1,0:T(8,128)} async-done(((f32[2048,512]{1,0:T(8,128)}), f32[64,512]{1,0:T(8,128)}) %reduce-scatter.17.cloned.1.call-update) | async-done | bytes 131088 | tf_op jit(solution)/shard_map/reduce_scatter | solution.py:402
  1787.4 182.5 %reduce-scatter.21.cloned.1.call-done = f32[16,4096]{1,0:T(8,128)} async-done(((f32[512,4096]{1,0:T(8,128)}), f32[16,4096]{1,0:T(8,128)}) %reduce-scatter.21.cloned.1.call-update) | async-done | bytes 262160 | tf_op jit(solution)/shard_map/reduce_scatter | solution.py:417
  1969.9 491.7 %reduce-scatter.25.cloned.1.call-done = f32[64,2816]{1,0:T(8,128)} async-done(((f32[2048,2816]{1,0:T(8,128)}), f32[64,2816]{1,0:T(8,128)}) %reduce-scatter.25.cloned.1.call-update) | async-done | bytes 720912 | tf_op jit(solution)/shard_map/reduce_scatter | solution.py:436
  2461.6 492.6 %reduce-scatter.27.cloned.1.call-done = f32[64,2816]{1,0:T(8,128)} async-done(((f32[2048,2816]{1,0:T(8,128)}), f32[64,2816]{1,0:T(8,128)}) %reduce-scatter.27.cloned.1.call-update) | async-done | bytes 720912 | tf_op jit(solution)/shard_map/reduce_scatter | solution.py:442
  2954.2 492.6 %reduce-scatter.29.cloned.1.call-done = f32[88,2048]{1,0:T(8,128)} async-done(((f32[2816,2048]{1,0:T(8,128)}), f32[88,2048]{1,0:T(8,128)}) %reduce-scatter.29.cloned.1.call-update) | async-done | bytes 720912 | tf_op jit(solution)/shard_map/reduce_scatter | solution.py:448
  3446.8 361.9 %reduce-scatter.23.cloned.1.call-done = f32[64,2048]{1,0:T(8,128)} async-done(((f32[2048,2048]{1,0:T(8,128)}), f32[64,2048]{1,0:T(8,128)}) %reduce-scatter.23.cloned.1.call-update) | async-done | bytes 524304 | tf_op jit(solution)/shard_map/reduce_scatter | solution.py:423
  3808.7 253.6 %reduce-scatter.15.cloned.1.call-done = f32[64,3072]{1,0:T(8,128)} async-done(((f32[2048,3072]{1,0:T(8,128)}), f32[64,3072]{1,0:T(8,128)}) %reduce-scatter.15.cloned.1.call-update) | async-done | bytes 786448 | tf_op jit(solution)/shard_map/reduce_scatter | solution.py:396
  (368 shorter events, 369.6 us)
Async XLA Ops:
  7.2 862.8 %copy-start = (bf16[1,704,2048]{2,1,0:T(8,128)(2,1)S(1)}, bf16[1,704,2048]{2,1,0:T(8,128)(2,1)}, u32[]{:S(2)}) copy-start(bf16[1,704,2048]{2,1,0:T(8,128)(2,1)} %param.39) | copy-start | bytes 8650756
  7.2 39.6 all-gather.10.cloned.1.call-start
  8.0 97.2 %all-gather.12.cloned.1.call-start = ((), (), s32[]{:S(2)}) async-start(), calls=%async_computation.15 | async-start | bytes 6291456 | tf_op jit(solution)/shard_map/all_gather | solution.py:119
  8.7 138.8 %all-gather.14.cloned.1.call-start = ((), (), s32[]{:S(2)}) async-start(), calls=%async_computation.16 | async-start | bytes 3194880 | tf_op jit(solution)/shard_map/all_gather | solution.py:150
  13.9 95.3 %copy-start.51 = (f32[2,1,256]{2,1,0:T(1,128)}, f32[2,1,256]{2,1,0:T(1,128)S(1)}, u32[]{:S(2)}) copy-start(f32[2,1,256]{2,1,0:T(1,128)S(1)} %convert_element_type.185) | copy-start | bytes 6148
  18.3 283.2 %copy-start.45 = (f32[2048]{0:T(1024)}, f32[2048]{0:T(1024)S(1)}, u32[]{:S(2)}) copy-start(f32[2048]{0:T(1024)S(1)} %convert_element_type.143) | copy-start | bytes 24580
  27.8 81.4 %copy-start.61 = (f32[128]{0:T(128)}, f32[128]{0:T(128)S(1)}, u32[]{:S(2)}) copy-start(f32[128]{0:T(128)S(1)} %get-tuple-element.64) | copy-start | bytes 1540
  28.3 281.3 %copy-start.47 = (f32[128,32]{0,1:T(8,128)}, f32[128,32]{0,1:T(8,128)S(1)}, u32[]{:S(2)}) copy-start(f32[128,32]{0,1:T(8,128)S(1)} %get-tuple-element.59) | copy-start | bytes 49156
  113.8 187.6 %all-gather.16.cloned.1.call-start = ((), (), s32[]{:S(2)}) async-start(), calls=%async_computation.17 | async-start | bytes 18874368 | tf_op jit(solution)/shard_map/all_gather | solution.py:115
  114.4 292.4 %all-gather.18.cloned.1.call-start = ((), (), s32[]{:S(2)}) async-start(), calls=%async_computation.18 | async-start | bytes 12582912 | tf_op jit(solution)/shard_map/all_gather | solution.py:120
  115.0 1003.1 %all-gather.22.cloned.1.call-start = ((), (), s32[]{:S(2)}) async-start(), calls=%async_computation.20 | async-start | bytes 11894784 | tf_op jit(solution)/shard_map/all_gather | solution.py:126
  122.0 291.1 %copy-start.49 = (f32[2048]{0:T(1024)}, f32[2048]{0:T(1024)S(1)}, u32[]{:S(2)}) copy-start(f32[2048]{0:T(1024)S(1)} %convert_element_type.154) | copy-start | bytes 24580
  129.6 180.7 %copy-start.39 = (pred[128,256]{1,0:T(8,128)(4,1)}, pred[128,256]{1,0:T(8,128)(4,1)S(1)}, u32[]{:S(2)}) copy-start(pred[128,256]{1,0:T(8,128)(4,1)S(1)} %fusion.50) | copy-start | bytes 98308
  163.3 147.0 %copy-start.41 = (bf16[256,64]{1,0:T(8,128)(2,1)}, bf16[256,64]{1,0:T(8,128)(2,1)S(1)}, u32[]{:S(2)}) copy-start(bf16[256,64]{1,0:T(8,128)(2,1)S(1)} %reshape.388) | copy-start | bytes 98308
  439.2 259.5 %all-to-all-start = ((bf16[32,56,2048]{2,1,0:T(8,128)(2,1)}), bf16[32,56,2048]{2,1,0:T(8,128)(2,1)}, u32[]{:S(2)}, u32[]{:S(2)}) async-start(bf16[32,56,2048]{2,1,0:T(8,128)(2,1)} %bitcast.173), calls=%async_computation | async-start | bytes 14680064 | tf_op jit(solution)/shard_map/all_to_all | solution.py:199
  443.9 681.3 %all-gather.20.cloned.1.call-start = ((), (), s32[]{:S(2)}) async-start(), calls=%async_computation.19 | async-start | bytes 11894784 | tf_op jit(solution)/shard_map/all_gather | solution.py:125
  704.8 165.1 %all-to-all-start.2 = ((bf16[32,56,2048]{2,1,0:T(8,128)(2,1)}), bf16[32,56,2048]{2,1,0:T(8,128)(2,1)}, u32[]{:S(2)}, u32[]{:S(2)}) async-start(bf16[32,56,2048]{2,1,0:T(8,128)(2,1)} %bitcast.174), calls=%async_computation.2 | async-start | bytes 14680064 | tf_op jit(solution)/shard_map/all_to_all | solution.py:265
  891.1 221.8 %all-to-all-start.1 = ((bf16[32,56,2048]{2,1,0:T(8,128)(2,1)}), bf16[32,56,2048]{2,1,0:T(8,128)(2,1)}, u32[]{:S(2)}, u32[]{:S(2)}) async-start(bf16[32,56,2048]{2,1,0:T(8,128)(2,1)} %bitcast.182), calls=%async_computation.1 | async-start | bytes 14680064 | tf_op jit(solution)/shard_map/all_to_all | solution.py:209
  897.6 234.7 %all-gather.24.cloned.1.call-start = ((), (), s32[]{:S(2)}) async-start(), calls=%async_computation.21 | async-start | bytes 11894784 | tf_op jit(solution)/shard_map/all_gather | solution.py:127
  1112.9 165.5 %all-to-all-start.3 = ((bf16[32,56,2048]{2,1,0:T(8,128)(2,1)}), bf16[32,56,2048]{2,1,0:T(8,128)(2,1)}, u32[]{:S(2)}, u32[]{:S(2)}) async-start(bf16[32,56,2048]{2,1,0:T(8,128)(2,1)} %bitcast.181), calls=%async_computation.3 | async-start | bytes 14680064 | tf_op jit(solution)/shard_map/all_to_all | solution.py:293
  1116.9 258.1 %reduce-scatter.13.cloned.1.call-start = ((), (), s32[]{:S(2)}) async-start(), calls=%async_computation.22 | async-start | bytes 3194880 | tf_op jit(solution)/shard_map/reduce_scatter | solution.py:362
  1141.7 170.5 %copy-start.19 = (bf16[128,2816]{1,0:T(8,128)(2,1)}, bf16[128,2816]{1,0:T(8,128)(2,1)S(1)}, u32[]{:S(2)}) copy-start(bf16[128,2816]{1,0:T(8,128)(2,1)S(1)} %get-tuple-element.43) | copy-start | bytes 2162692
  1340.9 171.3 %reduce-scatter.31.cloned.1.call-start = ((), (), s32[]{:S(2)}) async-start(), calls=%async_computation.31 | async-start | bytes 1081344
  1342.4 304.2 %reduce-scatter.19.cloned.1.call-start = ((), (), s32[]{:S(2)}) async-start(), calls=%async_computation.25 | async-start | bytes 1081344 | tf_op jit(solution)/shard_map/reduce_scatter | solution.py:408
  1382.5 404.9 %reduce-scatter.17.cloned.1.call-start = ((), (), s32[]{:S(2)}) async-start(), calls=%async_computation.24 | async-start | bytes 4325376 | tf_op jit(solution)/shard_map/reduce_scatter | solution.py:402
  1389.8 580.1 %reduce-scatter.21.cloned.1.call-start = ((), (), s32[]{:S(2)}) async-start(), calls=%async_computation.26 | async-start | bytes 8650752 | tf_op jit(solution)/shard_map/reduce_scatter | solution.py:417
  1394.5 1067.1 %reduce-scatter.25.cloned.1.call-start = ((), (), s32[]{:S(2)}) async-start(), calls=%async_computation.28 | async-start | bytes 23789568 | tf_op jit(solution)/shard_map/reduce_scatter | solution.py:436
  1405.1 1549.2 %reduce-scatter.27.cloned.1.call-start = ((), (), s32[]{:S(2)}) async-start(), calls=%async_computation.29 | async-start | bytes 23789568 | tf_op jit(solution)/shard_map/reduce_scatter | solution.py:442
  1415.5 2031.3 %reduce-scatter.29.cloned.1.call-start = ((), (), s32[]{:S(2)}) async-start(), calls=%async_computation.30 | async-start | bytes 23789568 | tf_op jit(solution)/shard_map/reduce_scatter | solution.py:448
  1426.1 2382.6 %reduce-scatter.23.cloned.1.call-start = ((), (), s32[]{:S(2)}) async-start(), calls=%async_computation.27 | async-start | bytes 17301504 | tf_op jit(solution)/shard_map/reduce_scatter | solution.py:423
  1435.7 2626.6 %reduce-scatter.15.cloned.1.call-start = ((), (), s32[]{:S(2)}) async-start(), calls=%async_computation.23 | async-start | bytes 25952256 | tf_op jit(solution)/shard_map/reduce_scatter | solution.py:396
  1522.8 2539.5 %copy-start.1 = (bf16[1,704,2048]{2,1,0:T(8,128)(2,1)S(1)}, bf16[1,704,2048]{2,1,0:T(8,128)(2,1)}, u32[]{:S(2)}) copy-start(bf16[1,704,2048]{2,1,0:T(8,128)(2,1)} %param.39) | copy-start | bytes 8650756
  (81 other events, 743.8 us)
Sparse Core Ops, SparseCore 0:
  9.6 37.2 all-gather.9
  48.4 56.7 all-gather.11
  114.0 33.5 all-gather.13
  148.9 152.4 all-gather.15
  302.8 103.9 all-gather.17
  409.6 163.7 all-gather.21
  576.2 123.0 all-gather.19
  901.3 181.3 all-gather.23
  1341.1 33.8 reduce-scatter.12
  1377.1 135.0 reduce-scatter.30
  1515.1 131.4 reduce-scatter.18
  1649.3 138.0 reduce-scatter.16
  1790.3 179.5 reduce-scatter.20
  1972.6 488.9 reduce-scatter.24
  2464.3 489.8 reduce-scatter.26
  2956.9 489.8 reduce-scatter.28
  3449.5 359.1 reduce-scatter.22
  3815.5 246.6 reduce-scatter.14
where the time goes:
time: 4070 us
  waiting for transfers between devices  3490 us (86%)
  matrix products  246 us (6%)
  local copies, waits for them, and re-layouts  133 us (3%)
  blocking collectives  101 us (2%)
  other arithmetic  66.3 us (2%)
    reduce_scatter x1, waiting for transfers between devices, on_device(): lax.psum_scatter(jnp.einsum('tf,td->fd', shared_hidden, stream_grad, pref...  493 us
    reduce_scatter x1, waiting for transfers between devices, on_device(): lax.psum_scatter(jnp.einsum('td,tf->df', normed_two, dshared_up, preferre...  493 us
    reduce_scatter x1, waiting for transfers between devices, on_device(): lax.psum_scatter(jnp.einsum('td,tf->df', normed_two, dshared_gate, prefer...  492 us
    reduce_scatter x1, waiting for transfers between devices, on_device(): lax.psum_scatter(jnp.einsum('tv,td->vd', attended, attn_out_grad, preferr...  362 us
    reduce_scatter x1, waiting for transfers between devices, on_device(): lax.psum_scatter(jnp.einsum('td,tq->dq', normed, query_grad, preferred_el...  254 us
    all_to_all x1, waiting for transfers between devices, on_device(): lax.all_to_all(expert_part, ('rep', 'shard'), split_axis=0, concat_axis=0...  192 us
    all_to_all x1, waiting for transfers between devices, on_device(): lax.all_to_all(doubled, ('rep', 'shard'), split_axis=0, concat_axis=0, ti...  183 us
    reduce_scatter x1, waiting for transfers between devices, on_device(): lax.psum_scatter(jnp.einsum('tl,tc->lc', latent_normed, keyval_grad, pref...  182 us
  transfers between devices with their start and end apart: 22, of which 19 were waited for; matrix products, arithmetic and copies ran while one was open for 9% of the time, Pallas kernels for 0%

commit v1 on v0

--- a/solution.py
+++ b/solution.py
@@ -1,6 +1,9 @@
+import functools
 import jax
 import jax.numpy as jnp
 from jax import lax
+from jax.experimental import pallas as pl
+from jax.experimental.pallas import tpu as pltpu
 from jax.sharding import PartitionSpec as P
 
 D = 2048
@@ -18,6 +21,18 @@
 
 def wide_product(left, right):
     return jnp.dot(left, right, preferred_element_type=jnp.float32)
+
+
+def contract(left, right, over, batch=((), ())):
+    return lax.dot_general(left, right, (over, batch), preferred_element_type=jnp.float32)
+
+
+def dot_nt(left, right):
+    return contract(left, right, ((1,), (1,)))
+
+
+def dot_tn(left, right):
+    return contract(left, right, ((0,), (0,)))
 
 
 def rms_scale(values):
@@ -53,7 +68,871 @@
     return sigmoid * (1.0 + values * (1.0 - sigmoid))
 
 
+MESH = pl.DeviceIdType.MESH
+SEM = pltpu.SemaphoreType.DMA
+HBM = pl.BlockSpec(memory_space=pl.ANY)
+
+def when(ok, f):
+    if ok is None: f()
+    else: pl.when(ok)(f)
+
+def place():
+    rep, x = lax.axis_index("rep"), lax.axis_index("shard")
+    return rep // 4, lax.rem(rep // 2, 2), lax.rem(rep, 2), x
+
+def device(z, y, c, x):
+    return ((z * 2 + y) * 2 + c, x)
+
+def slot(z, y, c, x):
+    return ((z * 2 + y) * 2 + c) * 2 + x
+
+def neighbours(nz):
+    z, y, c, x = place()
+    return dict(
+        zr=(device(z + 1, y, c, x), z + 1 < nz),
+        zl=(device(z - 1, y, c, x), z >= 1),
+        y=(device(z, 1 - y, c, x), None),
+        x=(device(z, y, c, 1 - x), None),
+        c=(device(z, y, 1 - c, x), None),
+    )
+
+def greet(nbr):
+    bar = pltpu.get_barrier_semaphore()
+    count = 0
+    for dev, ok in nbr.values():
+        when(ok, lambda dev=dev: pl.semaphore_signal(bar, inc=1, device_id=dev, device_id_type=MESH))
+        count = count + (1 if ok is None else jnp.where(ok, 1, 0))
+    pl.semaphore_wait(bar, count)
+
+def gather_kernel(nz, x_ref, t_ref, o_ref, ot_ref, own_sem, z_send, y_send, x_send, c_send, recv, crecv):
+    z, y, c, x = place()
+    nbr = neighbours(nz)
+    greet(nbr)
+    half = x_ref.shape[0] // 2
+    own = slot(z, y, c, x)
+    sems = dict(zr=z_send.at[0], zl=z_send.at[1], y=y_send, x=x_send, c=c_send)
+
+    def move(kind, h, b, mine=False):
+        if h == 2:
+            src, dst = t_ref if mine else ot_ref.at[b], ot_ref.at[b]
+        else:
+            rows = pl.ds(h * half, half)
+            src, dst = x_ref.at[rows] if mine else o_ref.at[b, rows], o_ref.at[b, rows]
+        return pltpu.make_async_remote_copy(
+            src_ref=src, dst_ref=dst, send_sem=sems[kind].at[h, b],
+            recv_sem=(crecv if kind == "c" else recv).at[h, b], device_id=nbr[kind][0], device_id_type=MESH)
+
+    def schedule(go):
+        def send(kind, h, b, mine=False):
+            def f():
+                for hh in (2, 0) if h == 0 else (1,):
+                    d = move(kind, hh, b, mine)
+                    d.start() if go else d.wait_send()
+
+            when(nbr[kind][1], f)
+
+        def arrive(h, b):
+            if go:
+                for hh in (2, 0) if h == 0 else (1,):
+                    move("x", hh, b).wait_recv()
+
+        second, third = ("y", "x"), ("x", "y")
+        for h in (0, 1):
+            send("zr", h, own, True)
+            send("zl", h, own, True)
+            send(second[h], h, own, True)
+        for h in (0, 1):
+            send(third[h], h, own, True)
+            send("c", h, own, True)
+        rounds = [[(z, None)]]
+        for s in range(nz - 1):
+            rounds.append([(z - 1 - s, z - 1 - s >= 0), (z + 1 + s, z + 1 + s < nz)])
+
+        def drain1(rnd):
+            for i, (zb, ok) in enumerate(rnd):
+                for h in (0, 1):
+                    def f(zb=zb, h=h, i=i):
+                        b = slot(zb, y, c, x)
+                        arrive(h, b)
+                        send("zr" if i == 0 else "zl", h, b)
+                        send(second[h], h, b)
+                        send(third[h], h, b)
+                        send("c", h, b)
+                    when(ok, f)
+
+        def drain2(rnd):
+            for zb, ok in rnd:
+                for h in (0, 1):
+                    def f(zb=zb, h=h):
+                        b = slot(zb, 1 - y, c, x) if h == 0 else slot(zb, y, c, 1 - x)
+                        arrive(h, b)
+                        send(third[h], h, b)
+                        send("c", h, b)
+                    when(ok, f)
+
+        def drain3(rnd):
+            for zb, ok in rnd:
+                for h in (0, 1):
+                    def f(zb=zb, h=h):
+                        b = slot(zb, y, c, 1 - x) if h == 0 else slot(zb, 1 - y, c, x)
+                        arrive(h, b)
+                        send("c", h, b)
+                        b = slot(zb, 1 - y, c, 1 - x)
+                        arrive(h, b)
+                        send("c", h, b)
+                    when(ok, f)
+
+        for s in range(nz - 1):
+            drain1(rounds[s + 1])
+            drain2(rounds[s])
+            if s >= 1:
+                drain3(rounds[s - 1])
+        drain2(rounds[nz - 1])
+        drain3(rounds[nz - 2])
+        drain3(rounds[nz - 1])
+
+    local = [
+        pltpu.make_async_copy(x_ref, o_ref.at[own], own_sem.at[0]),
+        pltpu.make_async_copy(t_ref, ot_ref.at[own], own_sem.at[1]),
+    ]
+    for d in local:
+        d.start()
+    schedule(True)
+    for zb in range(nz):
+        for yb in range(2):
+            for xb in range(2):
+                for h in (2, 0, 1):
+                    move("c", h, slot(zb, yb, 1 - c, xb)).wait_recv()
+    for d in local:
+        d.wait()
+    schedule(False)
+
+
+def all_gather(x, t, n, nz, cid):
+    return pl.pallas_call(
+        functools.partial(gather_kernel, nz),
+        out_shape=[jax.ShapeDtypeStruct((n,) + v.shape, v.dtype) for v in (x, t)],
+        in_specs=[pl.BlockSpec(memory_space=pl.ANY)] * 2,
+        out_specs=[pl.BlockSpec(memory_space=pl.ANY)] * 2,
+        scratch_shapes=[SEM((2,)), SEM((2, 3, n)), SEM((3, n)), SEM((3, n)), SEM((3, n)), SEM((3, n)), SEM((3, n))],
+        compiler_params=pltpu.CompilerParams(collective_id=cid, has_side_effects=True),
+    )(x, t)
+
+
+def far_first(nz, z):
+    def pick(i):
+        total = 0
+        for k in range(nz):
+            ranked = sorted(range(nz), key=lambda d: (-abs(d - k), -d if k < nz // 2 else d))
+            total = total + jnp.where(z == k, ranked[i], 0)
+        return total
+    return [pick(i) for i in range(nz)]
+
+def add_rows(total, other, lo, other_lo, count):
+    step = 16 if count % 16 == 0 else 8
+    def body(i, carry):
+        r = pl.ds(pl.multiple_of(lo + i * step, step), step)
+        s = pl.ds(pl.multiple_of(other_lo + i * step, step), step)
+        total[r] = (total[r].astype(jnp.float32) + other[s].astype(jnp.float32)).astype(total.dtype)
+        return carry
+    lax.fori_loop(0, count // step, body, 0)
+
+def scatter_kernel(nz, lo, x_ref, o_ref, mine, core, one, two, line, load_sem, core_send, core_recv, one_send, one_recv, two_send, two_recv, line_send, line_recv):
+    z, y, c, x = place()
+    nbr = neighbours(nz)
+    greet(nbr)
+    T = mine.shape[1]
+    half = T // 2
+    rows = lambda h: pl.ds(h * half, half)
+    place_of = lambda zb, yb, xb: (zb * 2 + yb) * 2 + xb
+    cols = pl.ds(lo, mine.shape[2])
+    order = far_first(nz, z)
+    combos = [(1 - y, 1 - x), (y, 1 - x), (1 - y, x), (y, x)]
+
+    def core_copy(zb, yb, xb):
+        k = place_of(zb, yb, xb)
+        return remote(x_ref.at[slot(zb, yb, 1 - c, xb), :, cols], core.at[k], core_send.at[k], core_recv.at[k], nbr["c"][0])
+
+    def load(zb, yb, xb):
+        k = place_of(zb, yb, xb)
+        return pltpu.make_async_copy(x_ref.at[slot(zb, yb, c, xb), :, cols], mine.at[k], load_sem.at[k])
+
+    def one_copy(h, zb, j):
+        k = place_of(zb, j, 1 - x) if h == 0 else place_of(zb, 1 - y, j)
+        i = zb * 2 + j
+        return remote(mine.at[k, rows(h)], one.at[h, i], one_send.at[h, i], one_recv.at[h, i], nbr["x" if h == 0 else "y"][0])
+
+    def two_copy(h, zb):
+        k = place_of(zb, 1 - y, x) if h == 0 else place_of(zb, y, 1 - x)
+        return remote(mine.at[k, rows(h)], two.at[h, zb], two_send.at[h, zb], two_recv.at[h, zb], nbr["y" if h == 0 else "x"][0])
+
+    def line_copy(h, zb, right):
+        k = place_of(zb, y, x)
+        d = 0 if right else 1
+        return remote(mine.at[k, rows(h)], line.at[d, h, zb], line_send.at[h, zb], line_recv.at[d, h, zb], nbr["zr" if right else "zl"][0])
+
+    for zb in order:
+        for yb, xb in combos:
+            core_copy(zb, yb, xb).start()
+            load(zb, yb, xb).start()
+
+    def stage0(zb):
+        for n, (yb, xb) in enumerate(combos):
+            k = place_of(zb, yb, xb)
+            core_copy(zb, yb, xb).wait_recv()
+            load(zb, yb, xb).wait()
+            add_rows(mine.at[k], core.at[k], 0, 0, T)
+            if n in (0, 1):
+                one_copy(0, zb, yb).start()
+            if n in (0, 2):
+                one_copy(1, zb, xb).start()
+
+    def stage1(zb):
+        for far in (True, False):
+            for h in (0, 1):
+                j = (1 - y if far else y) if h == 0 else (1 - x if far else x)
+                one_copy(h, zb, j).wait_recv()
+                k = place_of(zb, j, x) if h == 0 else place_of(zb, y, j)
+                add_rows(mine.at[k], one.at[h, zb * 2 + j], h * half, 0, half)
+                if far:
+                    two_copy(h, zb).start()
+
+    def stage2(zb):
+        k = place_of(zb, y, x)
+        for h in (0, 1):
+            two_copy(h, zb).wait_recv()
+            add_rows(mine.at[k], two.at[h, zb], h * half, 0, half)
+            def go(right, h=h):
+                line_copy(h, zb, right).wait_recv()
+                add_rows(mine.at[k], line.at[0 if right else 1, h, zb], h * half, 0, half)
+            when(jnp.logical_and(zb > z, z >= 1), lambda: go(True))
+            when(jnp.logical_and(zb < z, z + 1 < nz), lambda: go(False))
+            when(zb > z, lambda: line_copy(h, zb, True).start())
+            when(zb < z, lambda: line_copy(h, zb, False).start())
+
+    for i in range(nz + 2):
+        if i < nz: stage0(order[i])
+        if 1 <= i < nz + 1: stage1(order[i - 1])
+        if 2 <= i: stage2(order[i - 2])
+    k = place_of(z, y, x)
+    for h in (0, 1):
+        lo = h * half
+        o_ref[rows(h)] = mine[k, rows(h)].astype(jnp.float32)
+        for d, ok in ((0, z >= 1), (1, z + 1 < nz)):
+            def fin(d=d, h=h):
+                line_copy(h, z, d == 0).wait_recv()
+                o_ref[rows(h)] += line[d, h, z].astype(jnp.float32)
+            when(ok, fin)
+    for zb in order:
+        for yb, xb in combos:
+            core_copy(zb, yb, xb).wait_send()
+        for h in (0, 1):
+            for j in (0, 1):
+                one_copy(h, zb, j).wait_send()
+            two_copy(h, zb).wait_send()
+            when(zb > z, lambda: line_copy(h, zb, True).wait_send())
+            when(zb < z, lambda: line_copy(h, zb, False).wait_send())
+
+def reduce_scatter(x, nz, cid):
+    N, T, D = x.shape
+    sem = pltpu.SemaphoreType.DMA
+    bf = x.dtype
+    parts = max(1, N // 32)
+    W = D // parts
+    outs = [
+        pl.pallas_call(
+            functools.partial(scatter_kernel, nz, i * W),
+            out_shape=jax.ShapeDtypeStruct((T, W), jnp.float32),
+            in_specs=[pl.BlockSpec(memory_space=pl.ANY)],
+            out_specs=pl.BlockSpec(memory_space=pltpu.VMEM),
+            scratch_shapes=[
+                pltpu.VMEM((N // 2, T, W), bf), pltpu.VMEM((N // 2, T, W), bf),
+                pltpu.VMEM((2, 2 * nz, T // 2, W), bf), pltpu.VMEM((2, nz, T // 2, W), bf),
+                pltpu.VMEM((2, 2, nz, T // 2, W), bf),
+                sem((N // 2,)), sem((N // 2,)), sem((N // 2,)), sem((2, 2 * nz)), sem((2, 2 * nz)),
+                sem((2, nz)), sem((2, nz)), sem((2, nz)), sem((2, 2, nz))],
+            compiler_params=pltpu.CompilerParams(
+                collective_id=cid + i, has_side_effects=True, vmem_limit_bytes=48 << 20
+            ),
+        )(x)
+        for i in range(parts)
+    ]
+    return outs[0] if parts == 1 else jnp.concatenate(outs, axis=1)
+
+
+def remote(src, dst, send_sem, recv_sem, dev):
+    return pltpu.make_async_remote_copy(
+        src_ref=src, dst_ref=dst, send_sem=send_sem, recv_sem=recv_sem, device_id=dev, device_id_type=MESH
+    )
+
+
+def quad_neighbours():
+    z, y, c, x = place()
+    return dict(x=(device(z, y, c, 1 - x), None), c=(device(z, y, 1 - c, x), None))
+
+
+def open_kernel(stream, wq, kv, lat, tiny, stream_all, wq_o, kv_o, lat_o, tiny_o, b0, b1, b2, b3, b4, load, store, send, recv):
+    z, y, c, x = place()
+    nbr = quad_neighbours()
+    greet(nbr)
+    own, side = c * 2 + x, c * 2 + 1 - x
+    rows = lat.shape[0] // 2
+    mine = pl.ds(pl.multiple_of(c * rows, rows), rows)
+    xdev, cdev = nbr["x"][0], nbr["c"][0]
+
+    def heads(ref, out, xx):
+        n = out.shape[2]
+        return ref.at[:, pl.ds(pl.multiple_of((xx * 2 + c) * n, 128), n)]
+
+    xs = [
+        remote(stream, stream_all.at[own], send.at[0], recv.at[0], xdev),
+        remote(tiny, tiny_o.at[x], send.at[1], recv.at[1], xdev),
+        remote(lat.at[mine], lat_o.at[x, mine], send.at[2], recv.at[2], xdev),
+        remote(heads(kv, kv_o, 1 - x), kv_o.at[x], send.at[3], recv.at[3], xdev),
+        remote(heads(wq, wq_o, 1 - x), wq_o.at[x], send.at[4], recv.at[4], xdev),
+    ]
+    for d in xs:
+        d.start()
+    cs = [remote(stream, stream_all.at[own], send.at[5], recv.at[5], cdev)]
+    cs[0].start()
+    here = [
+        (stream, b0, stream_all.at[own]), (tiny, b4, tiny_o.at[x]), (lat, b3, lat_o.at[x]),
+        (heads(kv, kv_o, x), b2, kv_o.at[x]), (heads(wq, wq_o, x), b1, wq_o.at[x]),
+    ]
+    for i, (a, b, o) in enumerate(here):
+        pltpu.make_async_copy(a, b, load.at[i]).start()
+    for i, (a, b, o) in enumerate(here):
+        pltpu.make_async_copy(a, b, load.at[i]).wait()
+        pltpu.make_async_copy(b, o, store.at[i]).start()
+    xs[0].wait_recv()
+    cs.append(remote(stream_all.at[side], stream_all.at[side], send.at[6], recv.at[6], cdev))
+    cs[1].start()
+    xs[1].wait_recv()
+    xs[2].wait_recv()
+    cs.append(remote(lat_o.at[1 - x, mine], lat_o.at[1 - x, mine], send.at[7], recv.at[7], cdev))
+    cs[2].start()
+    xs[3].wait_recv()
+    xs[4].wait_recv()
+    for d in cs:
+        d.wait_recv()
+    for i, (a, b, o) in enumerate(here):
+        pltpu.make_async_copy(b, o, store.at[i]).wait()
+    for d in xs + cs:
+        d.wait_send()
+
+
+def open_quad(stream, wq, kv, lat, tiny, cid):
+    sd = jax.ShapeDtypeStruct
+    ins = (stream, wq, kv, lat, tiny)
+    shapes = [(4,) + stream.shape, (2, wq.shape[0], wq.shape[1] // 4), (2, kv.shape[0], kv.shape[1] // 4), (2,) + lat.shape, (2,) + tiny.shape]
+    return pl.pallas_call(
+        open_kernel,
+        out_shape=[sd(shape, v.dtype) for shape, v in zip(shapes, ins)],
+        in_specs=[HBM] * 5,
+        out_specs=[HBM] * 5,
+        scratch_shapes=[pltpu.VMEM(shape[1:], v.dtype) for shape, v in zip(shapes, ins)] + [SEM((5,)), SEM((5,)), SEM((8,)), SEM((8,))],
+        compiler_params=pltpu.CompilerParams(collective_id=cid, has_side_effects=True, vmem_limit_bytes=16 << 20),
+    )(*ins)
+
+
+def quad_gather_kernel(x_ref, o_ref, local, send, recv):
+    z, y, c, x = place()
+    nbr = quad_neighbours()
+    greet(nbr)
+    own, side = c * 2 + x, c * 2 + 1 - x
+    half = x_ref.shape[0] // 2
+    copies = []
+    for h in (0, 1):
+        r = pl.ds(h * half, half)
+        a = remote(x_ref.at[r], o_ref.at[own, r], send.at[0, h], recv.at[0, h], nbr["x"][0])
+        b = remote(x_ref.at[r], o_ref.at[own, r], send.at[1, h], recv.at[1, h], nbr["c"][0])
+        d = remote(o_ref.at[side, r], o_ref.at[side, r], send.at[2, h], recv.at[2, h], nbr["c"][0])
+        a.start()
+        b.start()
+        copies.append((a, b, d))
+    here = pltpu.make_async_copy(x_ref, o_ref.at[own], local)
+    here.start()
+    for a, b, d in copies:
+        a.wait_recv()
+        d.start()
+    for a, b, d in copies:
+        b.wait_recv()
+        d.wait_recv()
+        a.wait_send()
+        b.wait_send()
+        d.wait_send()
+    here.wait()
+
+
+def quad_gather(v, cid):
+    return pl.pallas_call(
+        quad_gather_kernel,
+        out_shape=jax.ShapeDtypeStruct((4,) + v.shape, v.dtype),
+        in_specs=[HBM],
+        out_specs=HBM,
+        scratch_shapes=[SEM, SEM((3, 2)), SEM((3, 2))],
+        compiler_params=pltpu.CompilerParams(collective_id=cid, has_side_effects=True),
+    )(v)
+
+
+def quad_scatter_kernel(v_ref, o_ref, mine, core, far, load, send, recv):
+    z, y, c, x = place()
+    nbr = quad_neighbours()
+    greet(nbr)
+    half = o_ref.shape[0] // 2
+    steps = []
+    for h in (0, 1):
+        r = pl.ds(h * half, half)
+        for j, xb in ((0, 1 - x), (1, x)):
+            a = remote(v_ref.at[(1 - c) * 2 + xb, r], core.at[j, r], send.at[j, h], recv.at[j, h], nbr["c"][0])
+            b = pltpu.make_async_copy(v_ref.at[c * 2 + xb, r], mine.at[j, r], load.at[j, h])
+            a.start()
+            b.start()
+            steps.append((a, b))
+    outs = []
+    for h in (0, 1):
+        r = pl.ds(h * half, half)
+        a, b = steps[2 * h]
+        a.wait_recv()
+        b.wait()
+        add_rows(mine.at[0], core.at[0], h * half, h * half, half)
+        f = remote(mine.at[0, r], far.at[r], send.at[2, h], recv.at[2, h], nbr["x"][0])
+        f.start()
+        outs.append(f)
+    for h in (0, 1):
+        a, b = steps[2 * h + 1]
+        a.wait_recv()
+        b.wait()
+        outs[h].wait_recv()
+        def body(i, carry, h=h):
+            r = pl.ds(pl.multiple_of(h * half + i * 16, 16), 16)
+            o_ref[r] = (mine[1, r].astype(jnp.float32) + core[1, r].astype(jnp.float32)) + far[r].astype(jnp.float32)
+            return carry
+        lax.fori_loop(0, half // 16, body, 0)
+    for a, b in steps:
+        a.wait_send()
+    for f in outs:
+        f.wait_send()
+
+
+def quad_scatter(v, cid):
+    _, rows, cols = v.shape
+    buf = pltpu.VMEM((2, rows, cols), v.dtype)
+    return pl.pallas_call(
+        quad_scatter_kernel,
+        out_shape=jax.ShapeDtypeStruct((rows, cols), jnp.float32),
+        in_specs=[HBM],
+        out_specs=pl.BlockSpec(memory_space=pltpu.VMEM),
+        scratch_shapes=[buf, buf, pltpu.VMEM((rows, cols), v.dtype), SEM((2, 2)), SEM((3, 2)), SEM((3, 2))],
+        compiler_params=pltpu.CompilerParams(
+            collective_id=cid, has_side_effects=True, vmem_limit_bytes=24 << 20
+        ),
+    )(v)
+
+
+def owners_kernel(nz, na, *refs):
+    ins, rest = refs[:na], refs[na:]
+    outs, rest = rest[:na], rest[na:]
+    mine, rest = rest[:na], rest[na:]
+    one, rest = rest[:na], rest[na:]
+    line, rest = rest[:na], rest[na:]
+    total, rest = rest[:na], rest[na:]
+    load, one_send, one_recv, line_send, line_recv, own_sem, q_send, q_recv = rest
+    z, y, c, x = place()
+    nbr = neighbours(nz)
+    nbr["d"] = (device(z, y, 1 - c, 1 - x), None)
+    greet(nbr)
+    order = far_first(nz, z)
+    xdev, cdev, ddev, ydev = (nbr[k][0] for k in ("x", "c", "d", "y"))
+
+    def loads(a, zb, yb):
+        k = zb * 2 + yb
+        return pltpu.make_async_copy(ins[a].at[k], mine[a].at[k], load.at[a, k])
+
+    def one_copy(a, zb):
+        return remote(mine[a].at[zb * 2 + 1 - y], one[a].at[zb], one_send.at[a, zb], one_recv.at[a, zb], ydev)
+
+    def line_copy(a, zb, right):
+        d = 0 if right else 1
+        return remote(
+            mine[a].at[zb * 2 + y], line[a].at[d, zb], line_send.at[a, zb], line_recv.at[d, a, zb],
+            nbr["zr" if right else "zl"][0],
+        )
+
+    for zb in order:
+        for a in range(na):
+            loads(a, zb, 1 - y).start()
+        for a in range(na):
+            loads(a, zb, y).start()
+    for zb in order:
+        for a in range(na):
+            loads(a, zb, 1 - y).wait()
+            one_copy(a, zb).start()
+    for zb in order:
+        for a in range(na):
+            rows = mine[a].shape[1]
+            k = zb * 2 + y
+            loads(a, zb, y).wait()
+            one_copy(a, zb).wait_recv()
+            add_rows(mine[a].at[k], one[a].at[zb], 0, 0, rows)
+
+            def go(right):
+                line_copy(a, zb, right).wait_recv()
+                add_rows(mine[a].at[k], line[a].at[0 if right else 1, zb], 0, 0, rows)
+
+            when(jnp.logical_and(zb > z, z >= 1), lambda: go(True))
+            when(jnp.logical_and(zb < z, z + 1 < nz), lambda: go(False))
+            when(zb > z, lambda: line_copy(a, zb, True).start())
+            when(zb < z, lambda: line_copy(a, zb, False).start())
+    k = z * 2 + y
+    member, group = c * 2 + x, x * 2 + c
+    sends = []
+    for a in range(na):
+        rows = mine[a].shape[1]
+
+        def fin(right):
+            line_copy(a, z, right).wait_recv()
+            add_rows(mine[a].at[k], line[a].at[0 if right else 1, z], 0, 0, rows)
+
+        when(z >= 1, lambda: fin(True))
+        when(z + 1 < nz, lambda: fin(False))
+        if a < na - 1 and outs[a].shape[0] != 4:
+            d = pltpu.make_async_copy(mine[a].at[k], outs[a], own_sem.at[a])
+            d.start()
+            sends.append((d, None))
+            continue
+        part = outs[a].shape[1] if a < na - 1 else rows
+        whole = part == rows
+        dst = total[a] if a == na - 1 else outs[a]
+
+        def piece(m):
+            return mine[a].at[k] if whole else mine[a].at[k, pl.ds(m * part, part)]
+
+        d = pltpu.make_async_copy(piece(member), dst.at[group], own_sem.at[a])
+        d.start()
+        sends.append((d, None))
+        for i, (dev, cc, xx) in enumerate(((xdev, c, 1 - x), (cdev, 1 - c, x), (ddev, 1 - c, 1 - x))):
+            d = remote(piece(cc * 2 + xx), dst.at[group], q_send.at[a, i], q_recv.at[a, i], dev)
+            d.start()
+            sends.append((d, True))
+    for d, far in sends:
+        d.wait()
+    outs[na - 1][...] = total[na - 1][0] + total[na - 1][1] + total[na - 1][2] + total[na - 1][3]
+    for zb in order:
+        for a in range(na):
+            one_copy(a, zb).wait_send()
+            when(zb > z, lambda: line_copy(a, zb, True).wait_send())
+            when(zb < z, lambda: line_copy(a, zb, False).wait_send())
+
+
+def to_owners(arrays, spread, nz, cid):
+    na = len(arrays)
+    shapes, specs = [], []
+    for a, v in enumerate(arrays):
+        _, rows, cols = v.shape
+        if a == na - 1:
+            shapes.append(jax.ShapeDtypeStruct((rows, cols), v.dtype))
+            specs.append(pl.BlockSpec(memory_space=pltpu.VMEM))
+            continue
+        if spread[a]:
+            shapes.append(jax.ShapeDtypeStruct((4, rows // 4 if rows % 64 == 0 else rows, cols), v.dtype))
+        else:
+            shapes.append(jax.ShapeDtypeStruct((rows, cols), v.dtype))
+        specs.append(HBM)
+    last = arrays[-1].shape
+    return pl.pallas_call(
+        functools.partial(owners_kernel, nz, na),
+        out_shape=shapes,
+        in_specs=[HBM] * na,
+        out_specs=specs,
+        scratch_shapes=[pltpu.VMEM(v.shape, v.dtype) for v in arrays]
+        + [pltpu.VMEM((nz,) + v.shape[1:], v.dtype) for v in arrays]
+        + [pltpu.VMEM((2, nz) + v.shape[1:], v.dtype) for v in arrays]
+        + [pltpu.VMEM((4,) + (last[1:] if a == na - 1 else (8, 128)), jnp.float32) for a in range(na)]
+        + [SEM((na, 2 * nz)), SEM((na, nz)), SEM((na, nz)), SEM((na, nz)), SEM((2, na, nz)), SEM((na,)), SEM((na, 3)), SEM((na, 3))],
+        compiler_params=pltpu.CompilerParams(
+            collective_id=cid, has_side_effects=True, vmem_limit_bytes=40 << 20
+        ),
+    )(*arrays)
+
+
+def experts_kernel(nt_ref, sg_ref, slot_ref, gate_ref, wg_ref, wu_ref, wd_ref, ws_ref, wsd_ref,
+                   out_ref, ng_ref, dwg_hbm, dwu_hbm, dwd_hbm, dws_ref, dsd_ref,
+                   dwg, dwu, dwd, sem, *, slots):
+    f32, b16 = jnp.float32, jnp.bfloat16
+    i = pl.program_id(0)
+    @pl.when(i == 0)
+    def _():
+        for r in (dwg, dwu, dwd, dws_ref, dsd_ref):
+            r[...] = jnp.zeros_like(r)
+    tokens = nt_ref.shape[0] * nt_ref.shape[1]
+    width = nt_ref.shape[2]
+    nt = nt_ref[...].reshape(tokens, width)
+    sg = sg_ref[...].reshape(tokens, width)
+    hit = lax.broadcasted_iota(jnp.int32, (slots, tokens), 0) == slot_ref[0]
+    pick = hit.astype(f32).astype(b16)
+    x = wide_product(pick, nt).astype(b16)
+    g0 = wide_product(pick, sg)
+    gate = jnp.sum(jnp.where(hit, gate_ref[0], 0.0), axis=1, keepdims=True)
+    g = (gate * g0).astype(b16)
+    gv = dot_nt(x, wg_ref[...])
+    uv = dot_nt(x, wu_ref[...])
+    sig = jax.nn.sigmoid(gv)
+    act = gv * sig
+    hid = (act * uv).astype(b16)
+    part = wide_product(hid, wd_ref[...])
+    gg = jnp.sum(g0 * part, axis=1, keepdims=True)
+    gg_high = gg.astype(b16).astype(f32)
+    column = lax.axis_index("rep") * 4 + lax.axis_index("shard") * 2
+    lane = lax.broadcasted_iota(jnp.int32, (slots, 128), 1)
+    gg = jnp.where(lane == column, gg_high, jnp.where(lane == column + 1, gg - gg_high, 0.0)).astype(b16)
+    e_out = (gate * part).astype(b16)
+    dwd[...] += dot_tn(hid, g)
+    hg = dot_nt(g, wd_ref[...])
+    dg = (hg * uv * (sig * (1.0 + gv * (1.0 - sig)))).astype(b16)
+    du = (hg * act).astype(b16)
+    dwg[...] += dot_tn(dg, x)
+    dwu[...] += dot_tn(du, x)
+    ing = (wide_product(dg, wg_ref[...]) + wide_product(du, wu_ref[...])).astype(b16)
+    fs = wsd_ref.shape[0]
+    s = dot_nt(nt, ws_ref[...])
+    sgv, suv = s[:, :fs], s[:, fs:]
+    ssig = jax.nn.sigmoid(sgv)
+    sact = sgv * ssig
+    sh = (sact * suv).astype(b16)
+    shg = dot_nt(sg, wsd_ref[...])
+    dsg = (shg * suv * (ssig * (1.0 + sgv * (1.0 - ssig))))
+    dsu = (shg * sact)
+    ds = jnp.concatenate([dsg, dsu], axis=1).astype(b16)
+    dsd_ref[...] += dot_tn(sh, sg)
+    dws_ref[...] += dot_tn(ds, nt)
+    out = wide_product(sh, wsd_ref[...]) + dot_tn(pick, e_out)
+    out_ref[...] = out.astype(b16).reshape(out_ref.shape)
+    ng = wide_product(ds, ws_ref[...]) + dot_tn(pick, ing)
+    ng_ref[:, :, :width] = ng.astype(b16).reshape(nt_ref.shape)
+    ng_ref[:, :, width:] = dot_tn(pick, gg).astype(b16).reshape(ng_ref.shape[:2] + (128,))
+    @pl.when(i == pl.num_programs(0) - 1)
+    def _():
+        cs = [pltpu.make_async_copy(a, b, sem.at[j]) for j, (a, b) in enumerate(((dwg, dwg_hbm), (dwu, dwu_hbm), (dwd, dwd_hbm)))]
+        for c in cs: c.start()
+        for c in cs: c.wait()
+
+def experts_both(nt, sg, slot, gate, wg, wu, wd, ws, wsd, capacity, blocks=4):
+    n, tok, width = nt.shape
+    steps = n // blocks
+    f = wg.shape[0]; fs = wsd.shape[0]
+    f32 = jnp.float32
+    one = lambda a: pl.BlockSpec(a.shape, lambda i: (0,) * a.ndim, pipeline_mode=pl.Buffered(1))
+    blk = pl.BlockSpec((blocks, tok, width), lambda i: (i, 0, 0))
+    row = pl.BlockSpec((1, 1, blocks * tok), lambda i: (i, 0, 0))
+    sd = jax.ShapeDtypeStruct
+    anyspec = HBM
+    acc = pltpu.VMEM((f, width), f32)
+    return pl.pallas_call(
+        functools.partial(experts_kernel, slots=blocks * capacity),
+        grid=(steps,),
+        in_specs=[blk, blk, row, row] + [one(w) for w in (wg, wu, wd, ws, wsd)],
+        out_specs=[blk, pl.BlockSpec((blocks, tok, width + 128), lambda i: (i, 0, 0)), anyspec, anyspec, anyspec,
+                   pl.BlockSpec((2 * fs, width), lambda i: (0, 0)), pl.BlockSpec((fs, width), lambda i: (0, 0))],
+        out_shape=[sd(nt.shape, nt.dtype), sd((n, tok, width + 128), nt.dtype),
+                   sd((f, width), f32), sd((f, width), f32), sd((f, width), f32),
+                   sd((2 * fs, width), f32), sd((fs, width), f32)],
+        scratch_shapes=[acc, acc, acc, SEM((3,))],
+        compiler_params=pltpu.CompilerParams(vmem_limit_bytes=64 << 20, dimension_semantics=("arbitrary",)),
+    )(nt, sg, slot.reshape(steps, 1, blocks * tok), gate.reshape(steps, 1, blocks * tok), wg, wu, wd, ws, wsd)
+
+
 def on_device(
+    stream_in, stream_grad, prefix_len, routes, route_weight, attn_gain, query_proj, latent_proj, rope_key_proj,
+    latent_gain, kv_up_proj, out_proj, ffn_gain, router_proj, shared_gate, shared_up, shared_down, expert_gate,
+    expert_up, expert_down,
+):
+    f32, b16 = jnp.float32, jnp.bfloat16
+    both = ("rep", "shard")
+    n_shard, n_rep = lax.axis_size("shard"), lax.axis_size("rep")
+    n_dev = n_rep * n_shard
+    nz = n_rep // 4
+    quads = n_rep // 2
+    rep, x = lax.axis_index("rep"), lax.axis_index("shard")
+    c = lax.rem(rep, 2)
+    member, group = c * 2 + x, x * 2 + c
+    tok, width = stream_in.shape
+    experts = router_proj.shape[1]
+    capacity = max(2, tok * TOP_K * 7 // (6 * experts))
+    seq = n_shard * tok
+    scale = (DN + DR) ** (-0.5)
+    heads = H // 4
+    qcols, kcols = heads * (DN + DR), heads * (DN + DV)
+    kvr = latent_proj.shape[1]
+    lanes = kvr + DR
+
+    dh = width // n_shard
+    gl = jnp.pad(latent_gain, (0, dh - kvr // n_shard))
+    tiny = jnp.concatenate([rope_key_proj.T, router_proj.T, attn_gain[None], ffn_gain[None], gl[None]], axis=0)
+    tiny = jnp.pad(tiny, ((0, -tiny.shape[0] % 16), (0, 0)))
+    stream_all, mat_q, mat_kv, mat_lat, tiny = open_quad(stream_in, query_proj, kv_up_proj, latent_proj, tiny, 1)
+    mat_q = mat_q.reshape(width, qcols)
+    mat_kv = mat_kv.reshape(kvr, kcols)
+    mat_lat = mat_lat.reshape(width, kvr)
+    joined = jnp.concatenate([tiny[0], tiny[1]], axis=1)
+    rope_t, router_t = joined[:DR], joined[DR : DR + experts]
+    gain_attn = joined[DR + experts].astype(f32)
+    gain_ffn = joined[DR + experts + 1].astype(f32)
+    gain_latent = tiny[:, DR + experts + 2, : kvr // n_shard].reshape(kvr).astype(f32)
+    mat_out = lax.dynamic_slice_in_dim(out_proj, c * heads * DV, heads * DV, 0)
+
+    grad_all = lax.all_gather(stream_grad, both, axis=0)
+    one_hot = (routes[:, :, None] == jnp.arange(experts)[None, None, :]).astype(f32)
+    mask = jnp.sum(one_hot, axis=1)
+    weight = jnp.sum(one_hot * route_weight[:, :, None], axis=1)
+    fs = shared_down.shape[0]
+    lanes_s = -(-fs // 128) * 128
+    own_w = width // n_dev
+    split = jnp.stack([shared_gate, shared_up], axis=1).reshape(own_w, 2, n_dev, fs)
+    split = jnp.pad(split, ((0, 0), (0, 0), (0, 0), (0, lanes_s - fs))).transpose(2, 0, 1, 3).reshape(n_dev, own_w, 2 * lanes_s)
+    w_s = lax.all_to_all(split, both, split_axis=0, concat_axis=0, tiled=True).reshape(width, 2 * lanes_s).T
+    w_sd = jnp.pad(shared_down, ((0, lanes_s - fs), (0, 0)))
+
+    stream4 = stream_all.reshape(4 * tok, width).astype(f32)
+    normed = (stream4 * rms_scale(stream4) * gain_attn).astype(b16)
+    positions = jnp.arange(seq)
+    cosine, sine = rope_tables(positions, DR)
+    q_raw = wide_product(normed, mat_q).reshape(2, seq, heads, DN + DR)
+    q_nope = q_raw[..., :DN].astype(b16)
+    q_rot = rotate(q_raw[..., DN:], cosine[:, None], sine[:, None]).astype(b16)
+    latent = wide_product(normed, mat_lat)
+    scale_lat = rms_scale(latent)
+    latent_normed = (latent * scale_lat * gain_latent).astype(b16)
+    k_rot = rotate(dot_nt(normed, rope_t).reshape(2, seq, DR), cosine, sine).astype(b16)
+    keyval = wide_product(latent_normed, mat_kv).astype(b16).reshape(2, seq, heads, DN + DV)
+    k_nope, values = keyval[..., :DN], keyval[..., DN:]
+    prefix = lax.dynamic_slice_in_dim(prefix_len, rep - c, 2)
+    allowed = (positions[None, None, :] <= positions[None, :, None]) | (positions[None, None, :] < prefix[:, None, None])
+    allowed = allowed[:, None]
+    raw = contract(q_nope, k_nope, ((3,), (3,)), ((0, 2), (0, 2)))
+    raw = raw + jnp.swapaxes(contract(q_rot, k_rot, ((3,), (2,)), ((0,), (0,))), 1, 2)
+    scores = jnp.where(allowed, raw * scale, MASKED)
+    expo = jnp.exp(scores - jnp.max(scores, axis=-1, keepdims=True))
+    probs = expo / jnp.sum(expo, axis=-1, keepdims=True)
+    probs_low = probs.astype(b16)
+    attended = jnp.swapaxes(contract(probs_low, values, ((3,), (1,)), ((0, 1), (0, 2))), 1, 2)
+    attended = attended.astype(b16).reshape(4 * tok, heads * DV)
+    part = wide_product(attended, mat_out).astype(b16).reshape(4, tok, width)
+    attn_out = quad_scatter(part, 3)
+    stream = stream_in.astype(f32)
+    mid = stream + attn_out
+    scale_two = rms_scale(mid)
+    normed_two = (mid * scale_two * gain_ffn).astype(b16)
+
+    router_prob = jax.nn.softmax(dot_nt(normed_two, router_t), axis=-1)
+    picked = mask * router_prob
+    picked_sum = jnp.sum(picked, axis=-1, keepdims=True)
+    gates = weight * picked / picked_sum
+    nt_all, tails = all_gather(normed_two, jnp.concatenate([gates.T, mask.T], axis=0), n_dev, nz, 4)
+    gates_e = lax.dynamic_index_in_dim(tails, rep, 1, False)
+    mask_e = lax.dynamic_index_in_dim(tails, experts + rep, 1, False)
+
+    blocks = 4
+    before = (jnp.arange(tok)[:, None] < jnp.arange(tok)[None, :]).astype(b16)
+    rank = wide_product(mask_e.astype(b16), before).astype(jnp.int32)
+    first = (jnp.arange(n_dev, dtype=jnp.int32) % blocks * capacity)[:, None]
+    place_of = jnp.where(mask_e > 0, first + rank, -1)
+    out, n_grad, grad_eg, grad_eu, grad_ed, grad_s, grad_sd = experts_both(
+        nt_all, grad_all, place_of, gates_e, jnp.swapaxes(expert_gate, 1, 2)[0], jnp.swapaxes(expert_up, 1, 2)[0],
+        expert_down[0], w_s, w_sd, capacity, blocks)
+    n_grad = reduce_scatter(n_grad, nz, 16)
+    ffn_out = reduce_scatter(out, nz, 24)
+    back = lax.all_to_all(grad_s.T.astype(b16).reshape(n_dev, own_w, 2 * lanes_s), both, split_axis=0, concat_axis=0, tiled=True)
+    back = back.reshape(n_dev, own_w, 2, lanes_s)[..., :fs].transpose(2, 1, 0, 3).reshape(2, own_w, n_dev * fs).astype(f32)
+    gate_grad = jnp.sum(n_grad[:, width : width + 4 * experts].reshape(tok, experts, 4), axis=-1)
+    n_grad = n_grad[:, :width]
+    residual = mid + ffn_out
+
+    weighted = weight * gate_grad
+    picked_grad = weighted / picked_sum - jnp.sum(weighted * picked, axis=-1, keepdims=True) / (picked_sum * picked_sum)
+    prob_grad = mask * picked_grad
+    logit_grad = (router_prob * (prob_grad - jnp.sum(router_prob * prob_grad, axis=-1, keepdims=True))).astype(b16)
+    n_grad = n_grad + wide_product(logit_grad, router_t)
+    norm_part, ffn_gain_grad = norm_back(n_grad, mid, scale_two, gain_ffn)
+    mid_grad = stream_grad.astype(f32) + norm_part
+    aog = mid_grad.astype(b16)
+    tail = jnp.pad(logit_grad, ((0, 0), (0, 128 - experts)))
+    aog_all = quad_gather(jnp.concatenate([aog, tail], axis=1), 7).reshape(4 * tok, width + 128)
+    logit_all = aog_all[:, width : width + experts]
+    aog_all = aog_all[:, :width]
+
+    att_grad = dot_nt(aog_all, mat_out).astype(b16)
+    grad_out = dot_tn(attended, aog_all)
+    att_grad = att_grad.reshape(2, seq, heads, DV)
+    value_grad = jnp.swapaxes(contract(probs_low, att_grad, ((2,), (1,)), ((0, 1), (0, 2))), 1, 2)
+    prob_grad_a = contract(att_grad, values, ((3,), (3,)), ((0, 2), (0, 2)))
+    s_grad = probs * (prob_grad_a - jnp.sum(probs * prob_grad_a, axis=-1, keepdims=True))
+    s_grad = s_grad.astype(b16)
+    qn_grad = scale * jnp.swapaxes(contract(s_grad, k_nope, ((3,), (1,)), ((0, 1), (0, 2))), 1, 2)
+    qr_grad = scale * jnp.swapaxes(contract(s_grad, k_rot, ((3,), (1,)), ((0,), (0,))), 1, 2)
+    kn_grad = scale * jnp.swapaxes(contract(s_grad, q_nope, ((2,), (1,)), ((0, 1), (0, 2))), 1, 2)
+    kr_grad = scale * contract(s_grad, q_rot, ((1, 2), (2, 1)), ((0,), (0,)))
+    keyval_grad = jnp.concatenate([kn_grad, value_grad], axis=-1).astype(b16).reshape(4 * tok, kcols)
+    qr_grad = rotate(qr_grad, cosine[:, None], -sine[:, None])
+    query_grad = jnp.concatenate([qn_grad, qr_grad], axis=-1).astype(b16).reshape(4 * tok, qcols)
+    lat_part = dot_nt(keyval_grad, mat_kv)
+    lat_part = jnp.concatenate([lat_part, kr_grad.reshape(4 * tok, DR), jnp.zeros((4 * tok, -lanes % 128), f32)], axis=1)
+    lat_sum = jnp.sum(quad_gather(lat_part.astype(b16), 8).astype(f32), axis=0)
+    lat_sum, kr_sum = lat_sum[:, :kvr], lat_sum[:, kvr:lanes].reshape(2, seq, DR)
+    key_pre = rotate(kr_sum, cosine, -sine).reshape(4 * tok, DR).astype(b16)
+    weighted_l = lat_sum * gain_latent
+    inner = jnp.mean(weighted_l * latent, axis=-1, keepdims=True)
+    latent_pre = scale_lat * weighted_l - latent * (scale_lat * scale_lat * scale_lat) * inner
+    lat_gain_rows = lat_sum * latent * scale_lat
+    lat_gain_grad = jnp.sum(lax.dynamic_slice_in_dim(lat_gain_rows, member * tok, tok, 0), axis=0)
+    lat_grad = jnp.concatenate([latent_pre.astype(b16), key_pre], axis=1)
+    part = dot_nt(query_grad, mat_q)
+    normed_grad = quad_scatter(part.astype(b16).reshape(4, tok, width), 9)
+    lat_own = lax.dynamic_slice_in_dim(lat_grad, member * tok, tok, 0)
+    normed_grad = normed_grad + dot_nt(lat_own[:, :kvr], mat_lat) + wide_product(lat_own[:, kvr:], rope_t)
+    attn_part, attn_gain_grad = norm_back(normed_grad, stream, rms_scale(stream), gain_attn)
+    grad_stream = (mid_grad + attn_part).astype(b16)
+
+    gq = dot_tn(normed, query_grad).astype(b16)
+    gkv = dot_tn(latent_normed, keyval_grad).astype(b16)
+    cols = lambda v: lax.dynamic_index_in_dim(v.reshape(4 * tok, quads, 4, own_w), member, 2, False).reshape(4 * tok, -1)
+    nt_quad = lax.dynamic_slice_in_dim(nt_all, (rep // 2) * 4, 4, 0).reshape(4 * tok, width)
+    glat = dot_tn(cols(normed), lat_grad)
+    grouter = dot_tn(cols(nt_quad), logit_all)
+    glat = jnp.concatenate([glat, grouter, jnp.zeros((glat.shape[0], -(lanes + experts) % 128), f32)], axis=1).astype(b16)
+    squares = jnp.stack([jnp.sum(v * v) for v in (stream, attn_out, mid, ffn_out, residual)])
+    side = jnp.concatenate(
+        [attn_gain_grad.reshape(quads, -1), ffn_gain_grad.reshape(quads, -1), lat_gain_grad.reshape(quads, -1),
+         jnp.broadcast_to(squares[None], (quads, 5))], axis=1)
+    side = jnp.pad(side, ((0, 0), (0, 1024 - side.shape[1]))).reshape(quads, 8, 128)
+    o_q, o_kv, o_out, o_lat, o_side = to_owners(
+        [gq.reshape(quads, -1, qcols), gkv.reshape(quads, -1, kcols), grad_out.astype(b16).reshape(quads, -1, width),
+         glat.reshape(quads, own_w, -1), side], (True, True, False, False, True), nz, 10)
+    o_side = o_side.reshape(-1)
+    per = width // quads
+    perl = kvr // quads
+    ga = lax.dynamic_slice_in_dim(o_side, member * own_w, own_w)
+    gf = lax.dynamic_slice_in_dim(o_side, per + member * own_w, own_w)
+    gla = lax.dynamic_slice_in_dim(o_side, 2 * per + member * (perl // 4), perl // 4)
+    totals = o_side[2 * per + perl : 2 * per + perl + 5]
+    stats = jnp.sqrt(totals / (tok * n_dev * width))
+    fits = lambda v, rows: v if v.shape[1] == rows else lax.dynamic_slice_in_dim(v, member * rows, rows, 1)
+    o_q = jnp.moveaxis(fits(o_q, own_w).astype(f32), 0, 1).reshape(own_w, -1)
+    o_kv = jnp.moveaxis(fits(o_kv, kvr // n_dev).astype(f32), 0, 1).reshape(kvr // n_dev, -1)
+    pairs = []
+    for q in range(quads):
+        for cc in range(2):
+            for xx in range(2):
+                pairs.append((q * 4 + cc * 2 + xx, (xx * 2 + cc) * quads + q))
+    o_out = lax.ppermute(o_out, both, pairs).astype(f32)
+    o_lat = o_lat.astype(f32)
+    return (
+        residual.astype(b16), grad_stream, stats, ga, o_q, o_lat[:, :kvr], o_lat[:, kvr:lanes], gla, o_kv, o_out, gf,
+        o_lat[:, lanes : lanes + experts], back[0], back[1], grad_sd[:fs], jnp.swapaxes(grad_eg[None], 1, 2), jnp.swapaxes(grad_eu[None], 1, 2), grad_ed[None],
+    )
+
+
+def on_device_weights(
     stream_in,
     stream_grad,
     prefix_len,
@@ -157,10 +1036,8 @@
     allowed = (key_pos[None, :] <= positions[:, None]) | (key_pos[None, :] < prefix)
 
     def score_block():
-        raw = jnp.einsum("thd,khd->htk", query_nope, key_nope, preferred_element_type=jnp.float32)
-        raw = raw + jnp.einsum(
-            "thd,kd->htk", query_rot, key_rot, preferred_element_type=jnp.float32
-        )
+        raw = contract(query_nope, key_nope, ((2,), (2,)), ((1,), (1,)))
+        raw = raw + jnp.transpose(contract(query_rot, key_rot, ((2,), (1,)), ((), ())), (1, 0, 2))
         return jnp.where(allowed[None], raw * score_scale, MASKED)
 
     scores = score_block()
@@ -169,7 +1046,7 @@
     total_exp = jnp.sum(expo, axis=-1, keepdims=True)
     log_total = top_score + jnp.log(total_exp)
     probs_low = (expo / total_exp).astype(jnp.bfloat16)
-    attended = jnp.einsum("htk,khd->thd", probs_low, values, preferred_element_type=jnp.float32)
+    attended = jnp.transpose(contract(probs_low, values, ((2,), (0,)), ((0,), (1,))), (1, 0, 2))
     attended = attended.reshape(tok_rows, H * DV).astype(jnp.bfloat16)
     attn_out = wide_product(attended, mat_out)
     mid = stream + attn_out
@@ -265,30 +1142,18 @@
     received_grad = lax.all_to_all(
         doubled_grad, ("rep", "shard"), split_axis=0, concat_axis=0, tiled=True
     )
-    grad_edown = jnp.einsum(
-        "rf,rd->fd", expert_inner_state, received_grad, preferred_element_type=jnp.float32
-    )
-    inner_state_gradient = jnp.einsum(
-        "rd,fd->rf", received_grad, down_local, preferred_element_type=jnp.float32
-    )
+    grad_edown = contract(expert_inner_state, received_grad, ((0,), (0,)), ((), ()))
+    inner_state_gradient = contract(received_grad, down_local, ((1,), (1,)), ((), ()))
     gate_value_gradient = (
         inner_state_gradient * expert_up_value * swish_derivative(expert_gate_value)
     ).astype(jnp.bfloat16)
     up_value_gradient = (inner_state_gradient * jax.nn.silu(expert_gate_value)).astype(jnp.bfloat16)
-    grad_egate = jnp.einsum(
-        "ux,ub->xb", incoming_rows, gate_value_gradient, preferred_element_type=jnp.float32
-    )
-    expert_up_gradient = jnp.einsum(
-        "ux,ub->xb", incoming_rows, up_value_gradient, preferred_element_type=jnp.float32
-    )
-    part_in_grad = jnp.einsum(
-        "rf,df->rd", gate_value_gradient, gate_local, preferred_element_type=jnp.float32
-    )
+    grad_egate = contract(incoming_rows, gate_value_gradient, ((0,), (0,)), ((), ()))
+    expert_up_gradient = contract(incoming_rows, up_value_gradient, ((0,), (0,)), ((), ()))
+    part_in_grad = contract(gate_value_gradient, gate_local, ((1,), (1,)), ((), ()))
     part_in_grad = (
         part_in_grad
-        + jnp.einsum(
-            "rf,df->rd", up_value_gradient, local_up_weight, preferred_element_type=jnp.float32
-        )
+        + contract(up_value_gradient, local_up_weight, ((1,), (1,)), ((), ()))
     ).astype(jnp.bfloat16)
     returned_grad = lax.all_to_all(
         part_in_grad, ("rep", "shard"), split_axis=0, concat_axis=0, tiled=True
@@ -297,9 +1162,7 @@
         returned_grad.reshape(experts, n_shard, capacity, D).astype(jnp.float32), axis=1
     ).reshape(experts * capacity, D)
     routed_grad = jnp.sum(slot_grad[slot_index].reshape(tok_rows, TOP_K, D), axis=1)
-    shared_hidden_grad = jnp.einsum(
-        "td,fd->tf", stream_grad, mat_sdown, preferred_element_type=jnp.float32
-    )
+    shared_hidden_grad = contract(stream_grad, mat_sdown, ((1,), (1,)), ((), ()))
     dshared_gate = (shared_hidden_grad * sup_val * swish_derivative(sgate_val)).astype(jnp.bfloat16)
     dshared_up = (shared_hidden_grad * jax.nn.silu(sgate_val)).astype(jnp.bfloat16)
     weighted_grad = route_weight * gate_grad
@@ -310,49 +1173,26 @@
     logit_grad = (
         router_prob * (prob_grad - jnp.sum(router_prob * prob_grad, axis=-1, keepdims=True))
     ).astype(jnp.bfloat16)
-    normed_two_grad = jnp.einsum(
-        "tf,df->td", dshared_gate, mat_sgate, preferred_element_type=jnp.float32
-    )
-    normed_two_grad = normed_two_grad + jnp.einsum(
-        "tf,df->td", dshared_up, mat_sup, preferred_element_type=jnp.float32
-    )
-    normed_two_grad = normed_two_grad + jnp.einsum(
-        "te,de->td", logit_grad, mat_router, preferred_element_type=jnp.float32
-    )
+    normed_two_grad = contract(dshared_gate, mat_sgate, ((1,), (1,)), ((), ()))
+    normed_two_grad = normed_two_grad + contract(dshared_up, mat_sup, ((1,), (1,)), ((), ()))
+    normed_two_grad = normed_two_grad + contract(logit_grad, mat_router, ((1,), (1,)), ((), ()))
     normed_two_grad = normed_two_grad + routed_grad
     norm_part, grad_gain_ffn = norm_back(normed_two_grad, mid, scale_two, gain_ffn)
     mid_grad = grad_top + norm_part
     attn_out_grad = mid_grad.astype(jnp.bfloat16)
-    attended_grad = jnp.einsum(
-        "td,vd->tv", attn_out_grad, mat_out, preferred_element_type=jnp.float32
-    )
+    attended_grad = contract(attn_out_grad, mat_out, ((1,), (1,)), ((), ()))
     attended_grad = attended_grad.astype(jnp.bfloat16).reshape(tok_rows, H, DV)
     probs_full = jnp.where(allowed[None], jnp.exp(score_block() - log_total), 0.0)
-    value_grad = jnp.einsum(
-        "htk,thd->khd",
-        probs_full.astype(jnp.bfloat16),
-        attended_grad,
-        preferred_element_type=jnp.float32,
-    )
-    prob_att_grad = jnp.einsum(
-        "thd,khd->htk", attended_grad, values, preferred_element_type=jnp.float32
-    )
+    value_grad = jnp.transpose(contract(probs_full.astype(jnp.bfloat16), attended_grad, ((1,), (0,)), ((0,), (1,))), (1, 0, 2))
+    prob_att_grad = contract(attended_grad, values, ((2,), (2,)), ((1,), (1,)))
     scores_grad = probs_full * (
         prob_att_grad - jnp.sum(probs_full * prob_att_grad, axis=-1, keepdims=True)
     )
     scores_grad = scores_grad.astype(jnp.bfloat16)
-    query_nope_grad = score_scale * jnp.einsum(
-        "htk,khd->thd", scores_grad, key_nope, preferred_element_type=jnp.float32
-    )
-    query_rot_grad = score_scale * jnp.einsum(
-        "htk,kd->thd", scores_grad, key_rot, preferred_element_type=jnp.float32
-    )
-    key_nope_grad = score_scale * jnp.einsum(
-        "htk,thd->khd", scores_grad, query_nope, preferred_element_type=jnp.float32
-    )
-    key_rot_grad = score_scale * jnp.einsum(
-        "htk,thd->kd", scores_grad, query_rot, preferred_element_type=jnp.float32
-    )
+    query_nope_grad = score_scale * jnp.transpose(contract(scores_grad, key_nope, ((2,), (0,)), ((0,), (1,))), (1, 0, 2))
+    query_rot_grad = score_scale * jnp.transpose(contract(scores_grad, key_rot, ((2,), (0,)), ((), ())), (1, 0, 2))
+    key_nope_grad = score_scale * jnp.transpose(contract(scores_grad, query_nope, ((1,), (0,)), ((0,), (1,))), (1, 0, 2))
+    key_rot_grad = score_scale * contract(scores_grad, query_rot, ((0, 1,), (1, 0,)), ((), ()))
     keyval_grad_all = jnp.concatenate([key_nope_grad, value_grad], axis=-1).reshape(
         n_shard, kv_rows, 128
     )
@@ -375,18 +1215,12 @@
         .reshape(tok_rows, H * (DN + DR))
         .astype(jnp.bfloat16)
     )
-    latent_normed_grad = jnp.einsum(
-        "tc,lc->tl", keyval_grad, mat_kv, preferred_element_type=jnp.float32
-    )
+    latent_normed_grad = contract(keyval_grad, mat_kv, ((1,), (1,)), ((), ()))
     latent_pre, grad_gain_latent = norm_back(latent_normed_grad, latent, scale_lat, gain_latent)
     latent_grad = latent_pre.astype(jnp.bfloat16)
-    normed_grad = jnp.einsum("tq,dq->td", query_grad, mat_query, preferred_element_type=jnp.float32)
-    normed_grad = normed_grad + jnp.einsum(
-        "tr,dr->td", key_pre_grad, mat_rope, preferred_element_type=jnp.float32
-    )
-    normed_grad = normed_grad + jnp.einsum(
-        "tl,dl->td", latent_grad, mat_latent, preferred_element_type=jnp.float32
-    )
+    normed_grad = contract(query_grad, mat_query, ((1,), (1,)), ((), ()))
+    normed_grad = normed_grad + contract(key_pre_grad, mat_rope, ((1,), (1,)), ((), ()))
+    normed_grad = normed_grad + contract(latent_grad, mat_latent, ((1,), (1,)), ((), ()))
     attn_part, grad_gain_attn = norm_back(normed_grad, stream, scale_one, gain_attn)
     grad_stream = (mid_grad + attn_part).astype(jnp.bfloat16)
     owned = (
@@ -394,19 +1228,19 @@
             grad_gain_attn[None][0], ("rep", "shard"), scatter_dimension=0, tiled=True
         ),
         lax.psum_scatter(
-            jnp.einsum("td,tq->dq", normed, query_grad, preferred_element_type=jnp.float32),
+            contract(normed, query_grad, ((0,), (0,)), ((), ())),
             ("rep", "shard"),
             scatter_dimension=0,
             tiled=True,
         ),
         lax.psum_scatter(
-            jnp.einsum("td,tl->dl", normed, latent_grad, preferred_element_type=jnp.float32),
+            contract(normed, latent_grad, ((0,), (0,)), ((), ())),
             ("rep", "shard"),
             scatter_dimension=0,
             tiled=True,
         ),
         lax.psum_scatter(
-            jnp.einsum("td,tr->dr", normed, key_pre_grad, preferred_element_type=jnp.float32),
+            contract(normed, key_pre_grad, ((0,), (0,)), ((), ())),
             ("rep", "shard"),
             scatter_dimension=0,
             tiled=True,
@@ -415,38 +1249,38 @@
             grad_gain_latent[None][0], ("rep", "shard"), scatter_dimension=0, tiled=True
         ),
         lax.psum_scatter(
-            jnp.einsum("tl,tc->lc", latent_normed, keyval_grad, preferred_element_type=jnp.float32),
+            contract(latent_normed, keyval_grad, ((0,), (0,)), ((), ())),
             ("rep", "shard"),
             scatter_dimension=0,
             tiled=True,
         ),
         lax.psum_scatter(
-            jnp.einsum("tv,td->vd", attended, attn_out_grad, preferred_element_type=jnp.float32),
+            contract(attended, attn_out_grad, ((0,), (0,)), ((), ())),
             ("rep", "shard"),
             scatter_dimension=0,
             tiled=True,
         ),
         lax.psum_scatter(grad_gain_ffn[None][0], ("rep", "shard"), scatter_dimension=0, tiled=True),
         lax.psum_scatter(
-            jnp.einsum("td,te->de", normed_two, logit_grad, preferred_element_type=jnp.float32),
+            contract(normed_two, logit_grad, ((0,), (0,)), ((), ())),
             ("rep", "shard"),
             scatter_dimension=0,
             tiled=True,
         ),
         lax.psum_scatter(
-            jnp.einsum("td,tf->df", normed_two, dshared_gate, preferred_element_type=jnp.float32),
+            contract(normed_two, dshared_gate, ((0,), (0,)), ((), ())),
             ("rep", "shard"),
             scatter_dimension=0,
             tiled=True,
         ),
         lax.psum_scatter(
-            jnp.einsum("td,tf->df", normed_two, dshared_up, preferred_element_type=jnp.float32),
+            contract(normed_two, dshared_up, ((0,), (0,)), ((), ())),
             ("rep", "shard"),
             scatter_dimension=0,
             tiled=True,
         ),
         lax.psum_scatter(
-            jnp.einsum("tf,td->fd", shared_hidden, stream_grad, preferred_element_type=jnp.float32),
+            contract(shared_hidden, stream_grad, ((0,), (0,)), ((), ())),
             ("rep", "shard"),
             scatter_dimension=0,
             tiled=True,
@@ -472,6 +1306,11 @@
         expert_up_gradient[None],
         grad_edown[None],
     )
+
+
+def by_size(*args):
+    tokens = lax.axis_size("rep") * lax.axis_size("shard") * args[0].shape[0]
+    return (on_device if tokens * args[0].shape[1] <= 1 << 23 else on_device_weights)(*args)
 
 
 def solution(mesh):
@@ -498,7 +1337,7 @@
         P("rep", "shard", None),
     )
     return jax.shard_map(
-        on_device,
+        by_size,
         mesh=mesh,
         in_specs=placed,
         out_specs=(

time: 4070 us -> 870 us (0.21)
  waiting for transfers between devices: 3490 us -> 0.69 us
  Pallas kernels: 0 us -> 667 us
  matrix products: 246 us -> 42.7 us
  blocking collectives: 101 us -> 0 us
  local copies, waits for them, and re-layouts: 133 us -> 87.9 us
    reduce_scatter x9 -> x0, waiting for transfers between devices: 2520 us -> none  [the longest x1 493 us: on_device(): lax.psum_scatter(jnp.einsum('tf,td->fd', shared_hidden, stream_grad, pref...]
    pallas_call x0 -> x10, Pallas kernels: none -> 667 us  [the longest x2 168 us: reduce_scatter(): pl.pallas_call(functools.partial(scatter_kernel, nz, i * W), out_shape=ja...]
    all_to_all x4 -> x2, waiting for transfers between devices: 604 us -> 0.01 us  [the longest x1 0.01 us: on_device(): lax.all_to_all(grad_s.T.astype(b16).reshape(n_dev, own_w, 2 * lanes_s), b...]
    all_gather x8 -> x1, waiting for transfers between devices: 322 us -> 0.01 us  [on_device(): grad_all = lax.all_gather(stream_grad, both, axis=0)]
    dot_general x32 -> x20, matrix products: 174 us -> 29.8 us  [contract(): lax.dot_general(left, right, (over, batch), preferred_element_type=jnp.fl...]
    all_gather x5 -> x0, blocking collectives: 64 us -> none  [the longest x1 41.1 us: on_device(): lax.all_gather(weights[8], 'shard', axis=0, tiled=True)]
    dot_general x12 -> x7, matrix products: 70.6 us -> 12.8 us  [wide_product(): return jnp.dot(left, right, preferred_element_type=jnp.float32)]
  transfers between devices with their start and end apart: 22 -> 4, of which waited for: 19 -> 0; matrix products, arithmetic and copies ran while one was open for 9% -> 11% of each run, Pallas kernels for 0% -> 38%
where the time goes in v1:
time: 870 us; the launch traced here: 862 us
  Pallas kernels  667 us (77%)
  local copies, waits for them, and re-layouts  87.9 us (10%)
  matrix products  42.7 us (5%)
  other arithmetic  35.3 us (4%)
  between operations  16 us (2%)
  starting transfers between devices  11.7 us (1%)
    pallas_call x2, Pallas kernels, reduce_scatter(): pl.pallas_call(functools.partial(scatter_kernel, nz, i * W), out_shape=ja...  168 us
    pallas_call x1, Pallas kernels, open_quad(): pl.pallas_call(open_kernel, out_shape=[sd(shape, v.dtype) for shape, v in...  120 us
    pallas_call x1, Pallas kernels, experts_both(): pl.pallas_call(functools.partial(experts_kernel, slots=blocks * capacity)...  114 us
    pallas_call x1, Pallas kernels, to_owners(): pl.pallas_call(functools.partial(owners_kernel, nz, na), out_shape=shapes...  95.3 us
    pallas_call x1, Pallas kernels, all_gather(): pl.pallas_call(functools.partial(gather_kernel, nz), out_shape=[jax.Shape...  83.3 us
    pallas_call x2, Pallas kernels, quad_scatter(): pl.pallas_call(quad_scatter_kernel, out_shape=jax.ShapeDtypeStruct((rows,...  45 us
    pallas_call x2, Pallas kernels, quad_gather(): pl.pallas_call(quad_gather_kernel, out_shape=jax.ShapeDtypeStruct((4,) +...  41.2 us
    dot_general x20, matrix products, contract(): lax.dot_general(left, right, (over, batch), preferred_element_type=jnp.fl...  29.8 us
  transfers between devices with their start and end apart: 4, of which 0 were waited for; matrix products, arithmetic and copies ran while one was open for 11% of the time, Pallas kernels for 38%

profile of v1, /device:TPU:0, one launch (start us, length us, event | category | flops | bytes accessed | tf_op | source)
XLA Modules:
  0.0 861.6 jit_solution(5475697556784891200)
XLA Ops:
  7.9 2.2 stack.27
  13.7 3.3 fusion.39
  18.5 7.7 all-to-all-start
  26.4 2.8 copy-done.2
  32.1 120.4 %shard_map.331 = (bf16[4,128,2048]{2,1,0:T(8,128)(2,1)S(1)}, bf16[2,1024,768]{2,1,0:T(8,128)(2,1)S(1)}, bf16[2,256,1024]{2,1,0:T(8,128)(2,1)S(1)}, bf16[2,1024,5...) custom-call(bf16[128,2048]{1,0:T(8,128)(2,1)S(1)} %copy-done, bf16[1024,3072]{1,0:T(8,128)(2,1)S(1)} %copy-done.2, ...), custom_call_target="tpu_custom_call" | custom-call | tf_op jit(solution)/shard_map/pallas_call | solution.py:428
  152.5 2.9 convert_element_type.247
  157.6 4.8 copy.237
  169.7 2.6 reshape.583
  173.3 2.7 fusion.2
  185.6 4.0 fusion.21
  189.6 2.2 copy.242
  191.9 3.0 convolution_convert_fusion.3
  194.9 29.5 %shard_map.332 = f32[128,2048]{1,0:T(8,128)S(1)} custom-call(bf16[4,128,2048]{2,1,0:T(8,128)(2,1)S(1)} %bitcast.211), custom_call_target="tpu_custom_call" | custom-call | tf_op jit(solution)/shard_map/pallas_call | solution.py:521
  226.9 2.9 copy.274
  231.9 83.3 %shard_map.333 = (bf16[32,128,2048]{2,1,0:T(8,128)(2,1)}, f32[32,32,128]{2,1,0:T(8,128)}) custom-call(bf16[128,2048]{1,0:T(8,128)(2,1)} %copy-done.25, f32[32,128]{1,0:T(8,128)} %pad_maximum_fusion.6.t_ref), custom_call_target="tpu_custom_call" | custom-call | tf_op jit(solution)/shard_map/pallas_call | solution.py:212
  316.7 5.5 reshape.615
  324.0 2.5 copy.275
  326.5 4.1 reshape_reshape.3
  336.7 2.3 copy.252
  339.0 113.8 %shard_map.334 = (bf16[32,128,2048]{2,1,0:T(8,128)(2,1)}, bf16[32,128,2176]{2,1,0:T(8,128)(2,1)}, f32[704,2048]{1,0:T(8,128)}, f32[704,2048]{1,0:T(8,128)}, f32[...) custom-call(bf16[32,128,2048]{2,1,0:T(8,128)(2,1)} %get-tuple-element.42.nt_ref, ...), custom_call_target="tpu_custom_call" | custom-call | tf_op jit(solution)/shard_map/pallas_call | solution.py:731
  452.9 86.8 %shard_map.336 = f32[128,2176]{1,0:T(8,128)S(1)} custom-call(bf16[32,128,2176]{2,1,0:T(8,128)(2,1)} %get-tuple-element.45.x_ref), custom_call_target="tpu_custom_call" | custom-call | tf_op jit(solution)/shard_map/pallas_call | solution.py:343
  540.3 81.5 %shard_map.335 = f32[128,2048]{1,0:T(8,128)S(1)} custom-call(bf16[32,128,2048]{2,1,0:T(8,128)(2,1)} %get-tuple-element.44.x_ref), custom_call_target="tpu_custom_call" | custom-call | tf_op jit(solution)/shard_map/pallas_call | solution.py:343
  626.3 19.2 %shard_map.337 = bf16[4,128,2176]{2,1,0:T(8,128)(2,1)} custom-call(bf16[128,2176]{1,0:T(8,128)(2,1)} %fusion.42.x_ref), custom_call_target="tpu_custom_call" | custom-call | tf_op jit(solution)/shard_map/pallas_call | solution.py:468
  645.5 3.5 fusion.14
  649.7 3.8 convolution_bitcast_fusion
  663.6 22.0 %shard_map.339 = bf16[4,512,640]{2,1,0:T(8,128)(2,1)} custom-call(bf16[512,640]{1,0:T(8,128)(2,1)} %maximum_maximum_fusion.x_ref), custom_call_target="tpu_custom_call" | custom-call | tf_op jit(solution)/shard_map/pallas_call | solution.py:468
  685.6 2.3 convert_reduce_fusion
  691.7 2.6 convolution_convert_fusion.1
  705.5 15.5 %shard_map.338 = f32[128,2048]{1,0:T(8,128)S(1)} custom-call(bf16[4,128,2048]{2,1,0:T(8,128)(2,1)S(1)} %bitcast.210), custom_call_target="tpu_custom_call" | custom-call | tf_op jit(solution)/shard_map/pallas_call | solution.py:521
  731.8 3.2 all-to-all-start.1
  735.0 3.3 stack.35
  742.6 95.3 %shard_map.340 = (bf16[4,64,768]{2,1,0:T(8,128)(2,1)S(1)}, bf16[4,16,1024]{2,1,0:T(8,128)(2,1)S(1)}, bf16[64,2048]{1,0:T(8,128)(2,1)S(1)}, bf16[64,640]{1,0:T(8,128)(2,1)S(1)}, f32[8,128]{1,0:T(8,128)S(1)}) custom-call(bf16[8,256,768]{2,1,0:T(8,128)(2,1)S(1)} %bitcast.209, bf16[8,64,1024]{2,1,0:T(8,128)(2,1)S(1)} %bitcast.206, ...), custom_call_target="tpu_custom_call" | custom-call | tf_op jit(solution)/shard_map/pallas_call | solution.py:643
  (377 shorter events, 103.9 us)
Async XLA Ops:
  7.2 331.8 %all-gather.3.cloned.1.call-start = ((), (), s32[]{:S(2)}) async-start(), calls=%async_computation.2 | async-start | bytes 17301504 | tf_op jit(solution)/shard_map/all_gather | solution.py:784
  17.0 9.3 %copy-start.75 = (bf16[1024,64]{0,1:T(8,128)(2,1)S(1)}, bf16[1024,64]{0,1:T(8,128)(2,1)}, u32[]{:S(2)}) copy-start(bf16[1024,64]{0,1:T(8,128)(2,1)} %param.28) | copy-start | bytes 393220
  17.0 9.4 %copy-start = (bf16[128,2048]{1,0:T(8,128)(2,1)S(1)}, bf16[128,2048]{1,0:T(8,128)(2,1)}, u32[]{:S(2)}) copy-start(bf16[128,2048]{1,0:T(8,128)(2,1)} %stream.1) | copy-start | bytes 1572868
  18.5 318.2 %all-to-all-start = ((bf16[32,64,256]{2,1,0:T(8,128)(2,1)}), bf16[32,64,256]{2,1,0:T(8,128)(2,1)}, u32[]{:S(2)}, u32[]{:S(2)}) async-start(bf16[32,64,256]{2,1,0:T(8,128)(2,1)} %reshape.588), calls=%async_computation | async-start | bytes 2097152 | tf_op jit(solution)/shard_map/all_to_all | solution.py:793
  162.4 63.6 %copy-start.20 = (bf16[96,1024]{1,0:T(8,128)(2,1)}, bf16[96,1024]{1,0:T(8,128)(2,1)S(1)}, u32[]{:S(2)}) copy-start(bf16[96,1024]{1,0:T(8,128)(2,1)S(1)} %get-tuple-element.199) | copy-start | bytes 589828
  162.4 63.6 %copy-start.22 = (bf16[96,1024]{1,0:T(8,128)(2,1)}, bf16[96,1024]{1,0:T(8,128)(2,1)S(1)}, u32[]{:S(2)}) copy-start(bf16[96,1024]{1,0:T(8,128)(2,1)S(1)} %get-tuple-element.200) | copy-start | bytes 589828
  163.6 9.7 %copy-start.71 = (f32[1,2048]{1,0:T(1,128)}, f32[1,2048]{1,0:T(1,128)S(1)}, u32[]{:S(2)}) copy-start(f32[1,2048]{1,0:T(1,128)S(1)} %get-tuple-element.178) | copy-start | bytes 24580
  167.3 148.8 %copy-start.80 = (f32[512]{0:T(512)}, f32[512]{0:T(512)S(1)}, u32[]{:S(2)}) copy-start(f32[512]{0:T(512)S(1)} %get-tuple-element.212) | copy-start | bytes 6148
  226.9 88.3 %copy-start.62 = (bf16[88,2048]{1,0:T(8,128)(2,1)S(1)}, bf16[88,2048]{1,0:T(8,128)(2,1)}, u32[]{:S(2)}) copy-start(bf16[88,2048]{1,0:T(8,128)(2,1)} %param.36) | copy-start | bytes 1081348
  229.9 92.3 %copy-start.35 = (f32[128,16]{1,0:T(8,128)}, f32[128,16]{1,0:T(8,128)S(1)}, u32[]{:S(2)}) copy-start(f32[128,16]{1,0:T(8,128)S(1)} %copy.245) | copy-start | bytes 24580
  230.0 92.2 %copy-start.43 = (f32[128,16]{1,0:T(8,128)}, f32[128,16]{1,0:T(8,128)S(1)}, u32[]{:S(2)}) copy-start(f32[128,16]{1,0:T(8,128)S(1)} %copy.244) | copy-start | bytes 24580
  230.2 92.1 %copy-start.45 = (f32[128,16]{1,0:T(8,128)}, f32[128,16]{1,0:T(8,128)S(1)}, u32[]{:S(2)}) copy-start(f32[128,16]{1,0:T(8,128)S(1)} %copy.243) | copy-start | bytes 24580
  231.3 91.0 %copy-start.94 = (f32[128]{0:T(128)}, f32[128]{0:T(128)S(1)}, u32[]{:S(2)}) copy-start(f32[128]{0:T(128)S(1)} %get-tuple-element.183) | copy-start | bytes 1540
  452.8 87.1 %copy-start.46 = (f32[128,16]{1,0:T(8,128)S(1)}, f32[128,16]{1,0:T(8,128)}, u32[]{:S(2)}) copy-start(f32[128,16]{1,0:T(8,128)} %copy-done.45) | copy-start | bytes 24580
  452.8 87.1 %copy-start.68 = (f32[128,16]{1,0:T(8,128)S(1)}, f32[128,16]{1,0:T(8,128)}, u32[]{:S(2)}) copy-start(f32[128,16]{1,0:T(8,128)} %get-tuple-element.184) | copy-start | bytes 24580
  452.8 87.2 %copy-start.95 = (f32[128]{0:T(128)S(1)}, f32[128]{0:T(128)}, u32[]{:S(2)}) copy-start(f32[128]{0:T(128)} %copy-done.94) | copy-start | bytes 1540
  452.8 87.2 %copy-start.36 = (f32[128,16]{1,0:T(8,128)S(1)}, f32[128,16]{1,0:T(8,128)}, u32[]{:S(2)}) copy-start(f32[128,16]{1,0:T(8,128)} %copy-done.35) | copy-start | bytes 24580
  452.9 87.2 %copy-start.44 = (f32[128,16]{1,0:T(8,128)S(1)}, f32[128,16]{1,0:T(8,128)}, u32[]{:S(2)}) copy-start(f32[128,16]{1,0:T(8,128)} %copy-done.43) | copy-start | bytes 24580
  452.9 87.2 %copy-start.86 = (f32[128]{0:T(128)S(1)}, f32[128]{0:T(128)}, u32[]{:S(2)}) copy-start(f32[128]{0:T(128)} %copy-done.85) | copy-start | bytes 1540
  452.9 87.2 %copy-start.88 = (f32[128]{0:T(128)S(1)}, f32[128]{0:T(128)}, u32[]{:S(2)}) copy-start(f32[128]{0:T(128)} %copy-done.87) | copy-start | bytes 1540
  540.3 81.7 %copy-start.17 = (f32[128,2048]{1,0:T(8,128)S(1)}, f32[128,2048]{1,0:T(8,128)}, u32[]{:S(2)}) copy-start(f32[128,2048]{1,0:T(8,128)} %copy-done.16) | copy-start | bytes 3145732
  540.3 81.7 %copy-start.52 = (bf16[16,2048]{1,0:T(8,128)(2,1)S(1)}, bf16[16,2048]{1,0:T(8,128)(2,1)}, u32[]{:S(2)}) copy-start(bf16[16,2048]{1,0:T(8,128)(2,1)} %copy-done.51) | copy-start | bytes 196612
  540.3 81.7 %copy-start.74 = (f32[1,2048]{1,0:T(1,128)S(1)}, f32[1,2048]{1,0:T(1,128)}, u32[]{:S(2)}) copy-start(f32[1,2048]{1,0:T(1,128)} %copy-done.73) | copy-start | bytes 24580
  540.3 81.7 %copy-start.90 = (f32[128]{0:T(128)S(1)}, f32[128]{0:T(128)}, u32[]{:S(2)}) copy-start(f32[128]{0:T(128)} %copy-done.89) | copy-start | bytes 1540
  700.2 21.1 %copy-start.69 = (bf16[2,8,8,256]{3,2,0,1:T(8,128)(2,1)}, bf16[2,8,8,256]{3,2,0,1:T(8,128)(2,1)S(1)}, u32[]{:S(2)}) copy-start(bf16[2,8,8,256]{3,2,0,1:T(8,128)(2,1)S(1)} %copy.308) | copy-start | bytes 196612
  705.5 15.6 %copy-start.91 = (f32[512]{0:T(512)S(1)}, f32[512]{0:T(512)}, u32[]{:S(2)}) copy-start(f32[512]{0:T(512)} %get-tuple-element.211) | copy-start | bytes 6148
  731.8 115.8 %all-to-all-start.1 = ((bf16[32,64,256]{2,1,0:T(8,128)(2,1)}), bf16[32,64,256]{2,1,0:T(8,128)(2,1)S(1)}, u32[]{:S(2)}, u32[]{:S(2)}) async-start(bf16[32,64,256]{2,1,0:T(8,128)(2,1)} %bitcast.225), calls=%async_computation.1 | async-start | bytes 2097152 | tf_op jit(solution)/shard_map/all_to_all | solution.py:845
  742.6 96.2 %copy-start.108 = (f32[128]{0:T(128)S(1)}, f32[128]{0:T(128)}, u32[]{:S(2)}) copy-start(f32[128]{0:T(128)} %get-tuple-element.167) | copy-start | bytes 1540
  742.6 96.3 %copy-start.31 = (f32[128,2048]{1,0:T(8,128)S(1)}, f32[128,2048]{1,0:T(8,128)}, u32[]{:S(2)}) copy-start(f32[128,2048]{1,0:T(8,128)} %get-tuple-element.229) | copy-start | bytes 3145732
  742.6 96.3 %copy-start.97 = (f32[128]{0:T(128)S(1)}, f32[128]{0:T(128)}, u32[]{:S(2)}) copy-start(f32[128]{0:T(128)} %get-tuple-element.217) | copy-start | bytes 1540
  742.6 96.3 %copy-start.101 = (f32[128]{0:T(128)S(1)}, f32[128]{0:T(128)}, u32[]{:S(2)}) copy-start(f32[128]{0:T(128)} %get-tuple-element.216) | copy-start | bytes 1540
  838.0 8.9 %collective-permute-start = (bf16[64,2048]{1,0:T(8,128)(2,1)S(1)}, bf16[64,2048]{1,0:T(8,128)(2,1)S(1)}, u32[]{:S(2)}, u32[]{:S(2)}) collective-permute-start(bf16[64,2048]{1,0:T(8,128)(2,1)S(1)} %get-tuple-element.50), channel_id=1, source_target_pairs={{0,0},{1,16},{2,8},{3,24},{4,1},{5,17},{6,9},{7,25},{8,2},{9,18},{... | collective-permute-start | bytes 786440 | tf_op jit(solution)/shard_map/ppermute | solution.py:927
  (83 other events, 245.2 us)
Sparse Core Ops, SparseCore 0:
  11.0 169.1 all-gather.2

commit v2 on v1

--- a/solution.py
+++ b/solution.py
@@ -215,6 +215,7 @@
         in_specs=[pl.BlockSpec(memory_space=pl.ANY)] * 2,
         out_specs=[pl.BlockSpec(memory_space=pl.ANY)] * 2,
         scratch_shapes=[SEM((2,)), SEM((2, 3, n)), SEM((3, n)), SEM((3, n)), SEM((3, n)), SEM((3, n)), SEM((3, n))],
+        cost_estimate=lasting(85),
         compiler_params=pltpu.CompilerParams(collective_id=cid, has_side_effects=True),
     )(x, t)
 
@@ -229,13 +230,16 @@
     return [pick(i) for i in range(nz)]
 
 def add_rows(total, other, lo, other_lo, count):
-    step = 16 if count % 16 == 0 else 8
+    step = next(k for k in (32, 16, 8) if count % k == 0)
+
     def body(i, carry):
         r = pl.ds(pl.multiple_of(lo + i * step, step), step)
         s = pl.ds(pl.multiple_of(other_lo + i * step, step), step)
-        total[r] = (total[r].astype(jnp.float32) + other[s].astype(jnp.float32)).astype(total.dtype)
+        total[r] = total[r] + other[s]
         return carry
+
     lax.fori_loop(0, count // step, body, 0)
+
 
 def scatter_kernel(nz, lo, x_ref, o_ref, mine, core, one, two, line, load_sem, core_send, core_recv, one_send, one_recv, two_send, two_recv, line_send, line_recv):
     z, y, c, x = place()
@@ -351,7 +355,8 @@
                 pltpu.VMEM((2, 2, nz, T // 2, W), bf),
                 sem((N // 2,)), sem((N // 2,)), sem((N // 2,)), sem((2, 2 * nz)), sem((2, 2 * nz)),
                 sem((2, nz)), sem((2, nz)), sem((2, nz)), sem((2, 2, nz))],
-            compiler_params=pltpu.CompilerParams(
+            cost_estimate=lasting(85),
+        compiler_params=pltpu.CompilerParams(
                 collective_id=cid + i, has_side_effects=True, vmem_limit_bytes=48 << 20
             ),
         )(x)
@@ -360,6 +365,10 @@
     return outs[0] if parts == 1 else jnp.concatenate(outs, axis=1)
 
 
+def lasting(us):
+    return pl.CostEstimate(flops=0, bytes_accessed=int(us * 3.5e6), transcendentals=0)
+
+
 def remote(src, dst, send_sem, recv_sem, dev):
     return pltpu.make_async_remote_copy(
         src_ref=src, dst_ref=dst, send_sem=send_sem, recv_sem=recv_sem, device_id=dev, device_id_type=MESH
@@ -371,29 +380,53 @@
     return dict(x=(device(z, y, c, 1 - x), None), c=(device(z, y, 1 - c, x), None))
 
 
-def open_kernel(stream, wq, kv, lat, tiny, stream_all, wq_o, kv_o, lat_o, tiny_o, b0, b1, b2, b3, b4, load, store, send, recv):
+def open_kernel(nz, stream, wq, kv, lat, tiny, stream_all, wq_o, kv_o, lat_o, tiny_o, b0, b1, b2, b3, b4,
+                load, store, send, recv, x_send, x_recv, zr_send, zl_send, y_send, p_recv):
     z, y, c, x = place()
-    nbr = quad_neighbours()
+    nbr = neighbours(nz)
     greet(nbr)
-    own, side = c * 2 + x, c * 2 + 1 - x
+    quads = 2 * nz
+    own, side, other = c * 2 + x, c * 2 + 1 - x, 1 - x
     rows = lat.shape[0] // 2
-    mine = pl.ds(pl.multiple_of(c * rows, rows), rows)
     xdev, cdev = nbr["x"][0], nbr["c"][0]
 
     def heads(ref, out, xx):
         n = out.shape[2]
         return ref.at[:, pl.ds(pl.multiple_of((xx * 2 + c) * n, 128), n)]
 
+    def rows_of(a, j):
+        n = (wq.shape[0] // quads, kv.shape[0] // quads, rows // quads)[a]
+        return pl.ds(pl.multiple_of((c * rows if a == 2 else 0) + j * n, n), n)
+
+    def piece(a, j):
+        return (wq_o, kv_o, lat_o)[a].at[other, rows_of(a, j)]
+
+    mine = z * 2 + y
+
+    def first(a):
+        r = rows_of(a, mine)
+        if a == 2:
+            src, dst = lat.at[r], lat_o.at[x, r]
+        else:
+            ref, out = ((wq, wq_o), (kv, kv_o))[a]
+            n = out.shape[2]
+            src, dst = ref.at[r, pl.ds(pl.multiple_of((other * 2 + c) * n, 128), n)], out.at[x, r]
+        return remote(src, dst, x_send.at[a], x_recv.at[a], xdev)
+
+    def along(a, j, kind):
+        sems = dict(zr=zr_send, zl=zl_send, y=y_send)[kind]
+        return remote(piece(a, j), piece(a, j), sems.at[a, j], p_recv.at[a, j], nbr[kind][0])
+
+    kinds = (2, 1, 0)
+    for a in kinds:
+        first(a).start()
     xs = [
         remote(stream, stream_all.at[own], send.at[0], recv.at[0], xdev),
         remote(tiny, tiny_o.at[x], send.at[1], recv.at[1], xdev),
-        remote(lat.at[mine], lat_o.at[x, mine], send.at[2], recv.at[2], xdev),
-        remote(heads(kv, kv_o, 1 - x), kv_o.at[x], send.at[3], recv.at[3], xdev),
-        remote(heads(wq, wq_o, 1 - x), wq_o.at[x], send.at[4], recv.at[4], xdev),
     ]
     for d in xs:
         d.start()
-    cs = [remote(stream, stream_all.at[own], send.at[5], recv.at[5], cdev)]
+    cs = [remote(stream, stream_all.at[own], send.at[2], recv.at[2], cdev)]
     cs[0].start()
     here = [
         (stream, b0, stream_all.at[own]), (tiny, b4, tiny_o.at[x]), (lat, b3, lat_o.at[x]),
@@ -404,35 +437,119 @@
     for i, (a, b, o) in enumerate(here):
         pltpu.make_async_copy(a, b, load.at[i]).wait()
         pltpu.make_async_copy(b, o, store.at[i]).start()
+
+    def spread(go):
+        def send(a, j, kind):
+            d = along(a, j, kind)
+            ok = nbr[kind][1]
+            when(ok, (lambda: d.start()) if go else (lambda: d.wait_send()))
+
+        for a in kinds:
+            if go:
+                first(a).wait_recv()
+            for kind in ("zr", "zl", "y"):
+                send(a, mine, kind)
+        for s in range(nz - 1):
+            for kind, zb, ok in (("zr", z - 1 - s, z - 1 - s >= 0), ("zl", z + 1 + s, z + 1 + s < nz)):
+
+                def f(kind=kind, zb=zb):
+                    j = zb * 2 + y
+                    for a in kinds:
+                        if go:
+                            along(a, j, "y").wait_recv()
+                        send(a, j, kind)
+                        send(a, j, "y")
+
+                pl.when(ok)(f)
+
+    spread(True)
     xs[0].wait_recv()
-    cs.append(remote(stream_all.at[side], stream_all.at[side], send.at[6], recv.at[6], cdev))
+    cs.append(remote(stream_all.at[side], stream_all.at[side], send.at[3], recv.at[3], cdev))
     cs[1].start()
     xs[1].wait_recv()
-    xs[2].wait_recv()
-    cs.append(remote(lat_o.at[1 - x, mine], lat_o.at[1 - x, mine], send.at[7], recv.at[7], cdev))
+    for zb in range(nz):
+        for a in kinds:
+            along(a, zb * 2 + 1 - y, "y").wait_recv()
+    half = pl.ds(pl.multiple_of(c * rows, rows), rows)
+    cs.append(remote(lat_o.at[other, half], lat_o.at[other, half], send.at[4], recv.at[4], cdev))
     cs[2].start()
-    xs[3].wait_recv()
-    xs[4].wait_recv()
     for d in cs:
         d.wait_recv()
     for i, (a, b, o) in enumerate(here):
         pltpu.make_async_copy(b, o, store.at[i]).wait()
     for d in xs + cs:
         d.wait_send()
-
-
-def open_quad(stream, wq, kv, lat, tiny, cid):
+    for a in kinds:
+        first(a).wait_send()
+    spread(False)
+
+
+def open_quad(stream, wq, kv, lat, tiny, nz, cid):
     sd = jax.ShapeDtypeStruct
     ins = (stream, wq, kv, lat, tiny)
     shapes = [(4,) + stream.shape, (2, wq.shape[0], wq.shape[1] // 4), (2, kv.shape[0], kv.shape[1] // 4), (2,) + lat.shape, (2,) + tiny.shape]
+    pieces = SEM((3, 2 * nz))
     return pl.pallas_call(
-        open_kernel,
+        functools.partial(open_kernel, nz),
         out_shape=[sd(shape, v.dtype) for shape, v in zip(shapes, ins)],
         in_specs=[HBM] * 5,
         out_specs=[HBM] * 5,
-        scratch_shapes=[pltpu.VMEM(shape[1:], v.dtype) for shape, v in zip(shapes, ins)] + [SEM((5,)), SEM((5,)), SEM((8,)), SEM((8,))],
+        scratch_shapes=[pltpu.VMEM(shape[1:], v.dtype) for shape, v in zip(shapes, ins)]
+        + [SEM((5,)), SEM((5,)), SEM((5,)), SEM((5,)), SEM((3,)), SEM((3,)), pieces, pieces, pieces, pieces],
+        cost_estimate=lasting(50),
         compiler_params=pltpu.CompilerParams(collective_id=cid, has_side_effects=True, vmem_limit_bytes=16 << 20),
     )(*ins)
+
+
+def split_kernel(units, gate, up, out):
+    lanes = out.shape[2] // 2
+    for j in range(out.shape[0]):
+        lo = min(units * j // 128 * 128, gate.shape[1] - 2 * lanes)
+        row = lax.broadcasted_iota(jnp.int32, (2 * lanes, lanes), 0)
+        lane = lax.broadcasted_iota(jnp.int32, (2 * lanes, lanes), 1)
+        pick = ((row == lane + (units * j - lo)) & (lane < units)).astype(jnp.float32).astype(gate.dtype)
+        for k, ref in enumerate((gate, up)):
+            out[j, :, k * lanes : (k + 1) * lanes] = wide_product(ref[:, lo : lo + 2 * lanes], pick).astype(out.dtype)
+
+
+def split_units(gate, up, n_dev, units):
+    vmem = pl.BlockSpec(memory_space=pltpu.VMEM)
+    return pl.pallas_call(
+        functools.partial(split_kernel, units),
+        out_shape=jax.ShapeDtypeStruct((n_dev, gate.shape[0], 256), gate.dtype),
+        in_specs=[vmem, vmem],
+        out_specs=vmem,
+        cost_estimate=lasting(4),
+        compiler_params=pltpu.CompilerParams(vmem_limit_bytes=16 << 20),
+    )(gate, up)
+
+
+def join_kernel(units, blocks, gate, up):
+    lanes = blocks.shape[2] // 2
+    row = lax.broadcasted_iota(jnp.int32, (lanes, lanes), 0)
+    lane = lax.broadcasted_iota(jnp.int32, (lanes, lanes), 1)
+    for t in range(gate.shape[1] // lanes):
+        totals = [None, None]
+        for j in range(lanes * t // units, (lanes * t + lanes - 1) // units + 1):
+            pick = ((row + (units * j - lanes * t) == lane) & (row < units)).astype(jnp.float32).astype(blocks.dtype)
+            for k in (0, 1):
+                v = wide_product(blocks[j, :, k * lanes : (k + 1) * lanes], pick)
+                totals[k] = v if totals[k] is None else totals[k] + v
+        for k, ref in enumerate((gate, up)):
+            ref[:, t * lanes : (t + 1) * lanes] = totals[k]
+
+
+def join_units(blocks, total, units):
+    vmem = pl.BlockSpec(memory_space=pltpu.VMEM)
+    out = jax.ShapeDtypeStruct((blocks.shape[1], total), jnp.float32)
+    return pl.pallas_call(
+        functools.partial(join_kernel, units),
+        out_shape=[out, out],
+        in_specs=[vmem],
+        out_specs=[vmem, vmem],
+        cost_estimate=lasting(4),
+        compiler_params=pltpu.CompilerParams(vmem_limit_bytes=16 << 20),
+    )(blocks)
 
 
 def quad_gather_kernel(x_ref, o_ref, local, send, recv):
@@ -471,6 +588,7 @@
         in_specs=[HBM],
         out_specs=HBM,
         scratch_shapes=[SEM, SEM((3, 2)), SEM((3, 2))],
+        cost_estimate=lasting(18),
         compiler_params=pltpu.CompilerParams(collective_id=cid, has_side_effects=True),
     )(v)
 
@@ -524,141 +642,279 @@
         in_specs=[HBM],
         out_specs=pl.BlockSpec(memory_space=pltpu.VMEM),
         scratch_shapes=[buf, buf, pltpu.VMEM((rows, cols), v.dtype), SEM((2, 2)), SEM((3, 2)), SEM((3, 2))],
+        cost_estimate=lasting(16),
         compiler_params=pltpu.CompilerParams(
             collective_id=cid, has_side_effects=True, vmem_limit_bytes=24 << 20
         ),
     )(v)
 
 
-def owners_kernel(nz, na, *refs):
-    ins, rest = refs[:na], refs[na:]
-    outs, rest = rest[:na], rest[na:]
-    mine, rest = rest[:na], rest[na:]
-    one, rest = rest[:na], rest[na:]
-    line, rest = rest[:na], rest[na:]
-    total, rest = rest[:na], rest[na:]
-    load, one_send, one_recv, line_send, line_recv, own_sem, q_send, q_recv = rest
+def finish_kernel(nz, na, own, far, stream, attn, mid, *refs):
+    ins, refs = refs[:na], refs[na:]
+    (res_o, q_o, kv_o, out_o, lat_o, router_o, side_o, stat_o), refs = refs[:8], refs[8:]
+    (t_mine, t_core, t_one, t_two, t_line, ffn), refs = refs[:6], refs[6:]
+    mine, refs = refs[:na], refs[na:]
+    one, refs = refs[:na], refs[na:]
+    line, refs = refs[:na], refs[na:]
+    (q_all, kv_all, out_all, side_all, stat, stat_in), refs = refs[:6], refs[6:]
+    (t_load, core_send, core_recv, tx_send, tx_recv, ty_send, ty_recv, tz_send, tz_recv,
+     load, y_send, y_recv, z_send, z_recv, own_sem, q_send, q_recv, out_send, out_recv, st_send, st_recv) = refs
     z, y, c, x = place()
     nbr = neighbours(nz)
     nbr["d"] = (device(z, y, 1 - c, 1 - x), None)
+    quads = 2 * nz
+    linear = slot(z, y, c, x)
+    target = (x * 2 + c) * quads + z * 2 + y
+    group, q = linear // quads, lax.rem(linear, quads)
+    source = device(q // 2, lax.rem(q, 2), lax.rem(group, 2), group // 2)
+    away = target != linear
+    nbr["to"] = ((target // 2, lax.rem(target, 2)), away)
+    nbr["from"] = (source, away)
+    bits = [b for b in range(8) if 1 << b < nz]
+    for b in bits:
+        low = lax.rem(z // (1 << b), 2)
+        nbr["z%d" % b] = (device(z + (1 - 2 * low) * (1 << b), y, c, x), None)
     greet(nbr)
     order = far_first(nz, z)
     xdev, cdev, ddev, ydev = (nbr[k][0] for k in ("x", "c", "d", "y"))
-
-    def loads(a, zb, yb):
-        k = zb * 2 + yb
-        return pltpu.make_async_copy(ins[a].at[k], mine[a].at[k], load.at[a, k])
-
-    def one_copy(a, zb):
-        return remote(mine[a].at[zb * 2 + 1 - y], one[a].at[zb], one_send.at[a, zb], one_recv.at[a, zb], ydev)
-
-    def line_copy(a, zb, right):
+    zdev = lambda right: nbr["zr" if right else "zl"][0]
+    add = lambda total, other: add_rows(total, other, 0, 0, total.shape[0])
+    place_of = lambda zb, yb, xb: (zb * 2 + yb) * 2 + xb
+    combos = [(1 - y, 1 - x), (y, 1 - x), (1 - y, x), (y, x)]
+
+    def t_core_copy(k):
+        return remote(far.at[k], t_core.at[k], core_send.at[k], core_recv.at[k], cdev)
+
+    def t_load_copy(k):
+        return pltpu.make_async_copy(own.at[k], t_mine.at[k], t_load.at[k])
+
+    def tx_copy(zb, yb):
+        i = zb * 2 + yb
+        return remote(t_mine.at[place_of(zb, yb, 1 - x)], t_one.at[i], tx_send.at[i], tx_recv.at[i], xdev)
+
+    def ty_copy(zb):
+        return remote(t_mine.at[place_of(zb, 1 - y, x)], t_two.at[zb], ty_send.at[zb], ty_recv.at[zb], ydev)
+
+    def tz_copy(zb, right):
         d = 0 if right else 1
-        return remote(
-            mine[a].at[zb * 2 + y], line[a].at[d, zb], line_send.at[a, zb], line_recv.at[d, a, zb],
-            nbr["zr" if right else "zl"][0],
-        )
+        return remote(t_mine.at[place_of(zb, y, x)], t_line.at[d, zb], tz_send.at[zb], tz_recv.at[d, zb], zdev(right))
+
+    def t_stage0(zb):
+        for i, (yb, xb) in enumerate(combos):
+            k = place_of(zb, yb, xb)
+            t_core_copy(k).wait_recv()
+            t_load_copy(k).wait()
+            add(t_mine.at[k], t_core.at[k])
+            if i < 2:
+                tx_copy(zb, yb).start()
+
+    def t_stage1(zb):
+        for yb in (1 - y, y):
+            tx_copy(zb, yb).wait_recv()
+            add(t_mine.at[place_of(zb, yb, x)], t_one.at[zb * 2 + yb])
+            if yb is not y:
+                ty_copy(zb).start()
+
+    def on_line(zb, arrive, leave):
+        when(jnp.logical_and(zb > z, z >= 1), lambda: arrive(True))
+        when(jnp.logical_and(zb < z, z + 1 < nz), lambda: arrive(False))
+        when(zb > z, lambda: leave(True))
+        when(zb < z, lambda: leave(False))
+
+    def t_stage2(zb):
+        total = t_mine.at[place_of(zb, y, x)]
+        ty_copy(zb).wait_recv()
+        add(total, t_two.at[zb])
+
+        def arrive(right):
+            tz_copy(zb, right).wait_recv()
+            add(total, t_line.at[0 if right else 1, zb])
+
+        on_line(zb, arrive, lambda right: tz_copy(zb, right).start())
+
+    def w_load(a, k):
+        src = ins[a].at[k, c * 2 + x] if len(ins[a].shape) == 4 else ins[a].at[k]
+        return pltpu.make_async_copy(src, mine[a].at[k], load.at[a, k])
+
+    def wy_copy(a, zb):
+        return remote(mine[a].at[zb * 2 + 1 - y], one[a].at[zb], y_send.at[a, zb], y_recv.at[a, zb], ydev)
+
+    def wz_copy(a, zb, right):
+        d = 0 if right else 1
+        return remote(mine[a].at[zb * 2 + y], line[a].at[d, zb], z_send.at[a, zb], z_recv.at[d, a, zb], zdev(right))
+
+    def w_stage0(zb):
+        for a in range(na):
+            w_load(a, zb * 2 + 1 - y).wait()
+            wy_copy(a, zb).start()
+
+    def w_stage1(zb):
+        for a in range(na):
+            total = mine[a].at[zb * 2 + y]
+            w_load(a, zb * 2 + y).wait()
+            wy_copy(a, zb).wait_recv()
+            add(total, one[a].at[zb])
+
+            def arrive(right):
+                wz_copy(a, zb, right).wait_recv()
+                add(total, line[a].at[0 if right else 1, zb])
+
+            on_line(zb, arrive, lambda right: wz_copy(a, zb, right).start())
 
     for zb in order:
-        for a in range(na):
-            loads(a, zb, 1 - y).start()
-        for a in range(na):
-            loads(a, zb, y).start()
-    for zb in order:
-        for a in range(na):
-            loads(a, zb, 1 - y).wait()
-            one_copy(a, zb).start()
-    for zb in order:
-        for a in range(na):
-            rows = mine[a].shape[1]
-            k = zb * 2 + y
-            loads(a, zb, y).wait()
-            one_copy(a, zb).wait_recv()
-            add_rows(mine[a].at[k], one[a].at[zb], 0, 0, rows)
-
-            def go(right):
-                line_copy(a, zb, right).wait_recv()
-                add_rows(mine[a].at[k], line[a].at[0 if right else 1, zb], 0, 0, rows)
-
-            when(jnp.logical_and(zb > z, z >= 1), lambda: go(True))
-            when(jnp.logical_and(zb < z, z + 1 < nz), lambda: go(False))
-            when(zb > z, lambda: line_copy(a, zb, True).start())
-            when(zb < z, lambda: line_copy(a, zb, False).start())
+        for yb, xb in combos:
+            k = place_of(zb, yb, xb)
+            t_core_copy(k).start()
+            t_load_copy(k).start()
+        for yb in (1 - y, y):
+            for a in range(na):
+                w_load(a, zb * 2 + yb).start()
+    for i in range(nz):
+        if i < 2:
+            w_stage0(order[i])
+        t_stage0(order[i])
+    for i in range(nz):
+        t_stage1(order[i])
+        if i + 2 < nz:
+            w_stage0(order[i + 2])
+        w_stage1(order[i])
+        t_stage2(order[i])
+
+    here = t_mine.at[place_of(z, y, x)]
+    for right, ok in ((True, z >= 1), (False, z + 1 < nz)):
+
+        def last(right=right):
+            tz_copy(z, right).wait_recv()
+
+        when(ok, last)
+    rows = 16
+
+    def body(i, sums):
+        r = pl.ds(pl.multiple_of(i * rows, rows), rows)
+        left = jnp.where(z >= 1, t_line[0, z, r].astype(jnp.float32), 0.0)
+        right = jnp.where(z + 1 < nz, t_line[1, z, r].astype(jnp.float32), 0.0)
+        v = here[r].astype(jnp.float32) + left + right
+        total = mid[r] + v
+        res_o[r] = total.astype(res_o.dtype)
+        fold = lambda u: jnp.sum((u * u).reshape(rows, -1, 128), axis=(0, 1))[None]
+        terms = (stream[r].astype(jnp.float32), attn[r], mid[r], v, total)
+        return tuple(s + fold(u) for s, u in zip(sums, terms))
+
+    sums = lax.fori_loop(0, mid.shape[0] // rows, body, (jnp.zeros((1, 128), jnp.float32),) * 5)
+    stat[...] = jnp.concatenate(sums + (jnp.zeros((3, 128), jnp.float32),), axis=0)
+    rounds = ["c", "x", "y"] + ["z%d" % b for b in bits]
+
+    def stat_copy(i):
+        return remote(stat, stat_in.at[i], st_send.at[i], st_recv.at[i], nbr[rounds[i]][0])
+
+    def stat_next(i):
+        if 0 < i <= len(rounds):
+            stat_copy(i - 1).wait()
+            stat[...] = stat[...] + stat_in[i - 1]
+        if i < len(rounds):
+            stat_copy(i).start()
+
+    stat_next(0)
+
     k = z * 2 + y
     member, group = c * 2 + x, x * 2 + c
-    sends = []
-    for a in range(na):
-        rows = mine[a].shape[1]
+    waits = []
+    spread = {0: q_all, 1: kv_all, na - 1: side_all}
+    for n_done, a in enumerate((2, 0, 1, 3, 4, na - 1)):
+        total = mine[a].at[k]
 
         def fin(right):
-            line_copy(a, z, right).wait_recv()
-            add_rows(mine[a].at[k], line[a].at[0 if right else 1, z], 0, 0, rows)
+            wz_copy(a, z, right).wait_recv()
+            add(total, line[a].at[0 if right else 1, z])
 
         when(z >= 1, lambda: fin(True))
         when(z + 1 < nz, lambda: fin(False))
-        if a < na - 1 and outs[a].shape[0] != 4:
-            d = pltpu.make_async_copy(mine[a].at[k], outs[a], own_sem.at[a])
+        if a in spread:
+            dst = spread[a]
+            part = dst.shape[1]
+            piece = lambda m: total if a == na - 1 else total.at[pl.ds(pl.multiple_of(m * part, part), part)]
+            d = pltpu.make_async_copy(piece(member), dst.at[group], own_sem.at[a])
             d.start()
-            sends.append((d, None))
-            continue
-        part = outs[a].shape[1] if a < na - 1 else rows
-        whole = part == rows
-        dst = total[a] if a == na - 1 else outs[a]
-
-        def piece(m):
-            return mine[a].at[k] if whole else mine[a].at[k, pl.ds(m * part, part)]
-
-        d = pltpu.make_async_copy(piece(member), dst.at[group], own_sem.at[a])
-        d.start()
-        sends.append((d, None))
-        for i, (dev, cc, xx) in enumerate(((xdev, c, 1 - x), (cdev, 1 - c, x), (ddev, 1 - c, 1 - x))):
-            d = remote(piece(cc * 2 + xx), dst.at[group], q_send.at[a, i], q_recv.at[a, i], dev)
-            d.start()
-            sends.append((d, True))
-    for d, far in sends:
+            waits.append(d)
+            for i, (dev, cc, xx) in enumerate(((xdev, c, 1 - x), (cdev, 1 - c, x), (ddev, 1 - c, 1 - x))):
+                d = remote(piece(cc * 2 + xx), dst.at[group], q_send.at[a, i], q_recv.at[a, i], dev)
+                d.start()
+                waits.append(d)
+        elif a == 2:
+            to = remote(total, out_all, out_send, out_recv, nbr["to"][0])
+            stay = pltpu.make_async_copy(total, out_all, own_sem.at[a])
+            when(away, lambda: to.start())
+            when(jnp.logical_not(away), lambda: stay.start())
+
+        stat_next(n_done + 1)
+    for i in range(na + 1, len(rounds) + 1):
+        stat_next(i)
+    stat_o[...] = stat[...]
+    router_o[...] = mine[4][k].astype(jnp.float32)
+    lat_o[...] = mine[3][k].astype(jnp.float32)
+    when(away, lambda: to.wait())
+    when(jnp.logical_not(away), lambda: stay.wait())
+    out_o[...] = out_all[...].astype(jnp.float32)
+    for d in waits:
         d.wait()
-    outs[na - 1][...] = total[na - 1][0] + total[na - 1][1] + total[na - 1][2] + total[na - 1][3]
+    for g in range(4):
+        for dst, src in ((q_o, q_all), (kv_o, kv_all)):
+            n = src.shape[2]
+            dst[:, g * n : (g + 1) * n] = src[g].astype(jnp.float32)
+    side_o[...] = side_all[0] + side_all[1] + side_all[2] + side_all[3]
+
     for zb in order:
+        for yb, xb in combos:
+            t_core_copy(place_of(zb, yb, xb)).wait_send()
+        for yb in (1 - y, y):
+            tx_copy(zb, yb).wait_send()
+        ty_copy(zb).wait_send()
+        on_line(zb, lambda right: None, lambda right: tz_copy(zb, right).wait_send())
         for a in range(na):
-            one_copy(a, zb).wait_send()
-            when(zb > z, lambda: line_copy(a, zb, True).wait_send())
-            when(zb < z, lambda: line_copy(a, zb, False).wait_send())
-
-
-def to_owners(arrays, spread, nz, cid):
+            wy_copy(a, zb).wait_send()
+            on_line(zb, lambda right: None, lambda right: wz_copy(a, zb, right).wait_send())
+
+
+def finish(own, far, stream, attn, mid, arrays, nz, cid):
     na = len(arrays)
-    shapes, specs = [], []
-    for a, v in enumerate(arrays):
-        _, rows, cols = v.shape
-        if a == na - 1:
-            shapes.append(jax.ShapeDtypeStruct((rows, cols), v.dtype))
-            specs.append(pl.BlockSpec(memory_space=pltpu.VMEM))
-            continue
-        if spread[a]:
-            shapes.append(jax.ShapeDtypeStruct((4, rows // 4 if rows % 64 == 0 else rows, cols), v.dtype))
-        else:
-            shapes.append(jax.ShapeDtypeStruct((rows, cols), v.dtype))
-        specs.append(HBM)
-    last = arrays[-1].shape
+    tok, width = mid.shape
+    n, quads = 4 * nz, 2 * nz
+    f32, b16, sd = jnp.float32, own.dtype, jax.ShapeDtypeStruct
+    q, kv, out, lat, router, side = arrays
+    vmem = pl.BlockSpec(memory_space=pltpu.VMEM)
+    shapes = [
+        sd((tok, width), b16), sd((q.shape[1] // 4, 4 * q.shape[2]), f32), sd((kv.shape[1] // 4, 4 * kv.shape[2]), f32),
+        sd(out.shape[1:], f32), sd(lat.shape[2:], f32), sd(router.shape[2:], f32), sd(side.shape[1:], f32), sd((8, 128), f32),
+    ]
+    buf = lambda *shape: pltpu.VMEM(shape, b16)
     return pl.pallas_call(
-        functools.partial(owners_kernel, nz, na),
+        functools.partial(finish_kernel, nz, na),
         out_shape=shapes,
-        in_specs=[HBM] * na,
-        out_specs=specs,
-        scratch_shapes=[pltpu.VMEM(v.shape, v.dtype) for v in arrays]
-        + [pltpu.VMEM((nz,) + v.shape[1:], v.dtype) for v in arrays]
-        + [pltpu.VMEM((2, nz) + v.shape[1:], v.dtype) for v in arrays]
-        + [pltpu.VMEM((4,) + (last[1:] if a == na - 1 else (8, 128)), jnp.float32) for a in range(na)]
-        + [SEM((na, 2 * nz)), SEM((na, nz)), SEM((na, nz)), SEM((na, nz)), SEM((2, na, nz)), SEM((na,)), SEM((na, 3)), SEM((na, 3))],
-        compiler_params=pltpu.CompilerParams(
-            collective_id=cid, has_side_effects=True, vmem_limit_bytes=40 << 20
-        ),
-    )(*arrays)
-
-
-def experts_kernel(nt_ref, sg_ref, slot_ref, gate_ref, wg_ref, wu_ref, wd_ref, ws_ref, wsd_ref,
-                   out_ref, ng_ref, dwg_hbm, dwu_hbm, dwd_hbm, dws_ref, dsd_ref,
-                   dwg, dwu, dwd, sem, *, slots):
+        in_specs=[HBM, HBM, vmem, vmem, vmem] + [HBM] * na,
+        out_specs=[vmem] * 8,
+        scratch_shapes=[buf(n, tok, width), buf(n, tok, width), buf(quads, tok, width), buf(nz, tok, width),
+                        buf(2, nz, tok, width), pltpu.VMEM((8, 128), f32)]
+        + [pltpu.VMEM((quads,) + v.shape[-2:], v.dtype) for v in arrays]
+        + [pltpu.VMEM((nz,) + v.shape[-2:], v.dtype) for v in arrays]
+        + [pltpu.VMEM((2, nz) + v.shape[-2:], v.dtype) for v in arrays]
+        + [buf(4, q.shape[1] // 4, q.shape[2]), buf(4, kv.shape[1] // 4, kv.shape[2]), buf(*out.shape[1:]),
+           pltpu.VMEM((4,) + side.shape[1:], f32), pltpu.VMEM((8, 128), f32), pltpu.VMEM((8, 8, 128), f32)]
+        + [SEM((n,)), SEM((n,)), SEM((n,)), SEM((quads,)), SEM((quads,)), SEM((nz,)), SEM((nz,)), SEM((nz,)), SEM((2, nz)),
+           SEM((na, quads)), SEM((na, nz)), SEM((na, nz)), SEM((na, nz)), SEM((2, na, nz)), SEM((na,)), SEM((na, 3)),
+           SEM((na, 3)), SEM, SEM, SEM((8,)), SEM((8,))],
+        cost_estimate=lasting(130),
+        compiler_params=pltpu.CompilerParams(collective_id=cid, has_side_effects=True, vmem_limit_bytes=58 << 20),
+    )(own, far, stream, attn, mid, *arrays)
+
+
+def silu_parts(values):
+    sigmoid = jax.nn.sigmoid(values)
+    return values * sigmoid, sigmoid * (1.0 + values * (1.0 - sigmoid))
+
+
+def experts_kernel(nt_ref, sg_ref, tail_ref, wg_ref, wu_ref, wd_ref, ws_ref, wsd_ref,
+                   own_ref, far_ref, ng_ref, dwg_hbm, dwu_hbm, dwd_hbm, dws_out, dsd_ref,
+                   dwg, dwu, dwd, dws_ref, sem, *, slots):
     f32, b16 = jnp.float32, jnp.bfloat16
     i = pl.program_id(0)
     @pl.when(i == 0)
@@ -669,16 +925,25 @@
     width = nt_ref.shape[2]
     nt = nt_ref[...].reshape(tokens, width)
     sg = sg_ref[...].reshape(tokens, width)
-    hit = lax.broadcasted_iota(jnp.int32, (slots, tokens), 0) == slot_ref[0]
+    blocks, tok = nt_ref.shape[:2]
+    lines = tail_ref.shape[1] // 2
+    me = lax.axis_index("rep")
+    gate_row = tail_ref[:, pl.ds(me, 1), :].reshape(blocks, tok)
+    named = tail_ref[:, pl.ds(lines + me, 1), :].reshape(blocks, tok)
+    before = lax.broadcasted_iota(jnp.int32, (tok, tok), 0) < lax.broadcasted_iota(jnp.int32, (tok, tok), 1)
+    rank = wide_product(named.astype(b16), before.astype(f32).astype(b16)).astype(jnp.int32)
+    rank = rank + lax.broadcasted_iota(jnp.int32, (blocks, tok), 0) * (slots // blocks)
+    place_of = jnp.where(named > 0, rank, -1)
+    in_row = lambda v: jnp.concatenate([v[j : j + 1] for j in range(blocks)], axis=1)
+    hit = lax.broadcasted_iota(jnp.int32, (slots, tokens), 0) == in_row(place_of)
     pick = hit.astype(f32).astype(b16)
     x = wide_product(pick, nt).astype(b16)
     g0 = wide_product(pick, sg)
-    gate = jnp.sum(jnp.where(hit, gate_ref[0], 0.0), axis=1, keepdims=True)
+    gate = jnp.sum(jnp.where(hit, in_row(gate_row), 0.0), axis=1, keepdims=True)
     g = (gate * g0).astype(b16)
     gv = dot_nt(x, wg_ref[...])
     uv = dot_nt(x, wu_ref[...])
-    sig = jax.nn.sigmoid(gv)
-    act = gv * sig
+    act, slope = silu_parts(gv)
     hid = (act * uv).astype(b16)
     part = wide_product(hid, wd_ref[...])
     gg = jnp.sum(g0 * part, axis=1, keepdims=True)
@@ -689,57 +954,73 @@
     e_out = (gate * part).astype(b16)
     dwd[...] += dot_tn(hid, g)
     hg = dot_nt(g, wd_ref[...])
-    dg = (hg * uv * (sig * (1.0 + gv * (1.0 - sig)))).astype(b16)
+    dg = (hg * uv * slope).astype(b16)
     du = (hg * act).astype(b16)
     dwg[...] += dot_tn(dg, x)
     dwu[...] += dot_tn(du, x)
     ing = (wide_product(dg, wg_ref[...]) + wide_product(du, wu_ref[...])).astype(b16)
     fs = wsd_ref.shape[0]
-    s = dot_nt(nt, ws_ref[...])
+    s = wide_product(nt, ws_ref[...])
     sgv, suv = s[:, :fs], s[:, fs:]
-    ssig = jax.nn.sigmoid(sgv)
-    sact = sgv * ssig
+    sact, sslope = silu_parts(sgv)
     sh = (sact * suv).astype(b16)
     shg = dot_nt(sg, wsd_ref[...])
-    dsg = (shg * suv * (ssig * (1.0 + sgv * (1.0 - ssig))))
-    dsu = (shg * sact)
-    ds = jnp.concatenate([dsg, dsu], axis=1).astype(b16)
+    ds = jnp.concatenate([shg * suv * sslope, shg * sact], axis=1).astype(b16)
     dsd_ref[...] += dot_tn(sh, sg)
     dws_ref[...] += dot_tn(ds, nt)
     out = wide_product(sh, wsd_ref[...]) + dot_tn(pick, e_out)
-    out_ref[...] = out.astype(b16).reshape(out_ref.shape)
-    ng = wide_product(ds, ws_ref[...]) + dot_tn(pick, ing)
+    out = out.astype(b16).reshape(nt_ref.shape)
+    c = lax.rem(lax.axis_index("rep"), 2)
+    for j in (0, 1):
+
+        @pl.when(c == j)
+        def _(j=j):
+            own_ref[...] = out[2 * j : 2 * j + 2]
+            far_ref[...] = out[2 - 2 * j : 4 - 2 * j]
+
+    ng = dot_nt(ds, ws_ref[...]) + dot_tn(pick, ing)
     ng_ref[:, :, :width] = ng.astype(b16).reshape(nt_ref.shape)
     ng_ref[:, :, width:] = dot_tn(pick, gg).astype(b16).reshape(ng_ref.shape[:2] + (128,))
     @pl.when(i == pl.num_programs(0) - 1)
     def _():
         cs = [pltpu.make_async_copy(a, b, sem.at[j]) for j, (a, b) in enumerate(((dwg, dwg_hbm), (dwu, dwu_hbm), (dwd, dwd_hbm)))]
         for c in cs: c.start()
+        dws_out[...] = dws_ref[...].T.astype(b16)
         for c in cs: c.wait()
 
-def experts_both(nt, sg, slot, gate, wg, wu, wd, ws, wsd, capacity, blocks=4):
+def experts_both(nt, sg, tails, wg, wu, wd, ws, wsd, capacity, blocks=4):
     n, tok, width = nt.shape
     steps = n // blocks
     f = wg.shape[0]; fs = wsd.shape[0]
     f32 = jnp.float32
     one = lambda a: pl.BlockSpec(a.shape, lambda i: (0,) * a.ndim, pipeline_mode=pl.Buffered(1))
     blk = pl.BlockSpec((blocks, tok, width), lambda i: (i, 0, 0))
-    row = pl.BlockSpec((1, 1, blocks * tok), lambda i: (i, 0, 0))
+    half = pl.BlockSpec((blocks // 2, tok, width), lambda i: (i, 0, 0))
+    row = pl.BlockSpec((blocks,) + tails.shape[1:], lambda i: (i, 0, 0))
     sd = jax.ShapeDtypeStruct
     anyspec = HBM
     acc = pltpu.VMEM((f, width), f32)
     return pl.pallas_call(
         functools.partial(experts_kernel, slots=blocks * capacity),
         grid=(steps,),
-        in_specs=[blk, blk, row, row] + [one(w) for w in (wg, wu, wd, ws, wsd)],
-        out_specs=[blk, pl.BlockSpec((blocks, tok, width + 128), lambda i: (i, 0, 0)), anyspec, anyspec, anyspec,
-                   pl.BlockSpec((2 * fs, width), lambda i: (0, 0)), pl.BlockSpec((fs, width), lambda i: (0, 0))],
-        out_shape=[sd(nt.shape, nt.dtype), sd((n, tok, width + 128), nt.dtype),
+        in_specs=[blk, blk, row] + [one(w) for w in (wg, wu, wd, ws, wsd)],
+        out_specs=[half, half, pl.BlockSpec((blocks, tok, width + 128), lambda i: (i, 0, 0)), anyspec, anyspec, anyspec,
+                   pl.BlockSpec((width, 2 * fs), lambda i: (0, 0)), pl.BlockSpec((fs, width), lambda i: (0, 0))],
+        out_shape=[sd((n // 2, tok, width), nt.dtype)] * 2 + [sd((n, tok, width + 128), nt.dtype),
                    sd((f, width), f32), sd((f, width), f32), sd((f, width), f32),
-                   sd((2 * fs, width), f32), sd((fs, width), f32)],
-        scratch_shapes=[acc, acc, acc, SEM((3,))],
+                   sd((width, 2 * fs), nt.dtype), sd((fs, width), f32)],
+        scratch_shapes=[acc, acc, acc, pltpu.VMEM((2 * fs, width), f32), SEM((3,))],
         compiler_params=pltpu.CompilerParams(vmem_limit_bytes=64 << 20, dimension_semantics=("arbitrary",)),
-    )(nt, sg, slot.reshape(steps, 1, blocks * tok), gate.reshape(steps, 1, blocks * tok), wg, wu, wd, ws, wsd)
+        cost_estimate=lasting(110),
+    )(nt, sg, tails, wg, wu, wd, ws, wsd)
+
+
+def swap(v, nz, f):
+    pairs = [
+        (slot(*f(z, y, c, x)), slot(z, y, c, x))
+        for z in range(nz) for y in range(2) for c in range(2) for x in range(2)
+    ]
+    return lax.ppermute(v, ("rep", "shard"), pairs)
 
 
 def on_device(
@@ -770,7 +1051,7 @@
     gl = jnp.pad(latent_gain, (0, dh - kvr // n_shard))
     tiny = jnp.concatenate([rope_key_proj.T, router_proj.T, attn_gain[None], ffn_gain[None], gl[None]], axis=0)
     tiny = jnp.pad(tiny, ((0, -tiny.shape[0] % 16), (0, 0)))
-    stream_all, mat_q, mat_kv, mat_lat, tiny = open_quad(stream_in, query_proj, kv_up_proj, latent_proj, tiny, 1)
+    stream_all, mat_q, mat_kv, mat_lat, tiny = open_quad(stream_in, query_proj, kv_up_proj, latent_proj, tiny, nz, 1)
     mat_q = mat_q.reshape(width, qcols)
     mat_kv = mat_kv.reshape(kvr, kcols)
     mat_lat = mat_lat.reshape(width, kvr)
@@ -781,16 +1062,16 @@
     gain_latent = tiny[:, DR + experts + 2, : kvr // n_shard].reshape(kvr).astype(f32)
     mat_out = lax.dynamic_slice_in_dim(out_proj, c * heads * DV, heads * DV, 0)
 
-    grad_all = lax.all_gather(stream_grad, both, axis=0)
+    late_grad, stream_all = lax.optimization_barrier((stream_grad, stream_all))
+    grad_all = lax.all_gather(late_grad, both, axis=0)
     one_hot = (routes[:, :, None] == jnp.arange(experts)[None, None, :]).astype(f32)
     mask = jnp.sum(one_hot, axis=1)
     weight = jnp.sum(one_hot * route_weight[:, :, None], axis=1)
     fs = shared_down.shape[0]
     lanes_s = -(-fs // 128) * 128
     own_w = width // n_dev
-    split = jnp.stack([shared_gate, shared_up], axis=1).reshape(own_w, 2, n_dev, fs)
-    split = jnp.pad(split, ((0, 0), (0, 0), (0, 0), (0, lanes_s - fs))).transpose(2, 0, 1, 3).reshape(n_dev, own_w, 2 * lanes_s)
-    w_s = lax.all_to_all(split, both, split_axis=0, concat_axis=0, tiled=True).reshape(width, 2 * lanes_s).T
+    split = split_units(shared_gate, shared_up, n_dev, fs)
+    w_s = lax.all_to_all(split, both, split_axis=0, concat_axis=0, tiled=True).reshape(width, 2 * lanes_s)
     w_sd = jnp.pad(shared_down, ((0, lanes_s - fs), (0, 0)))
 
     stream4 = stream_all.reshape(4 * tok, width).astype(f32)
@@ -829,24 +1110,15 @@
     picked_sum = jnp.sum(picked, axis=-1, keepdims=True)
     gates = weight * picked / picked_sum
     nt_all, tails = all_gather(normed_two, jnp.concatenate([gates.T, mask.T], axis=0), n_dev, nz, 4)
-    gates_e = lax.dynamic_index_in_dim(tails, rep, 1, False)
-    mask_e = lax.dynamic_index_in_dim(tails, experts + rep, 1, False)
-
-    blocks = 4
-    before = (jnp.arange(tok)[:, None] < jnp.arange(tok)[None, :]).astype(b16)
-    rank = wide_product(mask_e.astype(b16), before).astype(jnp.int32)
-    first = (jnp.arange(n_dev, dtype=jnp.int32) % blocks * capacity)[:, None]
-    place_of = jnp.where(mask_e > 0, first + rank, -1)
-    out, n_grad, grad_eg, grad_eu, grad_ed, grad_s, grad_sd = experts_both(
-        nt_all, grad_all, place_of, gates_e, jnp.swapaxes(expert_gate, 1, 2)[0], jnp.swapaxes(expert_up, 1, 2)[0],
-        expert_down[0], w_s, w_sd, capacity, blocks)
+
+    mats = (jnp.swapaxes(expert_gate, 1, 2)[0], jnp.swapaxes(expert_up, 1, 2)[0], expert_down[0], w_s, w_sd)
+    out_own, out_far, n_grad, grad_eg, grad_eu, grad_ed, grad_s, grad_sd = experts_both(
+        nt_all, grad_all, tails, *mats, capacity, 4)
     n_grad = reduce_scatter(n_grad, nz, 16)
-    ffn_out = reduce_scatter(out, nz, 24)
-    back = lax.all_to_all(grad_s.T.astype(b16).reshape(n_dev, own_w, 2 * lanes_s), both, split_axis=0, concat_axis=0, tiled=True)
-    back = back.reshape(n_dev, own_w, 2, lanes_s)[..., :fs].transpose(2, 1, 0, 3).reshape(2, own_w, n_dev * fs).astype(f32)
+    back = lax.all_to_all(grad_s.reshape(n_dev, own_w, 2 * lanes_s), both, split_axis=0, concat_axis=0, tiled=True)
+    back = join_units(back, n_dev * fs, fs)
     gate_grad = jnp.sum(n_grad[:, width : width + 4 * experts].reshape(tok, experts, 4), axis=-1)
     n_grad = n_grad[:, :width]
-    residual = mid + ffn_out
 
     weighted = weight * gate_grad
     picked_grad = weighted / picked_sum - jnp.sum(weighted * picked, axis=-1, keepdims=True) / (picked_sum * picked_sum)
@@ -858,7 +1130,7 @@
     aog = mid_grad.astype(b16)
     tail = jnp.pad(logit_grad, ((0, 0), (0, 128 - experts)))
     aog_all = quad_gather(jnp.concatenate([aog, tail], axis=1), 7).reshape(4 * tok, width + 128)
-    logit_all = aog_all[:, width : width + experts]
+    logit_all = aog_all[:, width:]
     aog_all = aog_all[:, :width]
 
     att_grad = dot_nt(aog_all, mat_out).astype(b16)
@@ -876,8 +1148,10 @@
     qr_grad = rotate(qr_grad, cosine[:, None], -sine[:, None])
     query_grad = jnp.concatenate([qn_grad, qr_grad], axis=-1).astype(b16).reshape(4 * tok, qcols)
     lat_part = dot_nt(keyval_grad, mat_kv)
-    lat_part = jnp.concatenate([lat_part, kr_grad.reshape(4 * tok, DR), jnp.zeros((4 * tok, -lanes % 128), f32)], axis=1)
-    lat_sum = jnp.sum(quad_gather(lat_part.astype(b16), 8).astype(f32), axis=0)
+    lat_part = jnp.concatenate([lat_part, kr_grad.reshape(4 * tok, DR)], axis=1).astype(b16)
+    lat_part = lat_part.astype(f32) + swap(lat_part, nz, lambda z, y, c, x: (z, y, c, 1 - x)).astype(f32)
+    lat_part = lat_part.astype(b16)
+    lat_sum = lat_part.astype(f32) + swap(lat_part, nz, lambda z, y, c, x: (z, y, 1 - c, x)).astype(f32)
     lat_sum, kr_sum = lat_sum[:, :kvr], lat_sum[:, kvr:lanes].reshape(2, seq, DR)
     key_pre = rotate(kr_sum, cosine, -sine).reshape(4 * tok, DR).astype(b16)
     weighted_l = lat_sum * gain_latent
@@ -895,40 +1169,26 @@
 
     gq = dot_tn(normed, query_grad).astype(b16)
     gkv = dot_tn(latent_normed, keyval_grad).astype(b16)
-    cols = lambda v: lax.dynamic_index_in_dim(v.reshape(4 * tok, quads, 4, own_w), member, 2, False).reshape(4 * tok, -1)
     nt_quad = lax.dynamic_slice_in_dim(nt_all, (rep // 2) * 4, 4, 0).reshape(4 * tok, width)
-    glat = dot_tn(cols(normed), lat_grad)
-    grouter = dot_tn(cols(nt_quad), logit_all)
-    glat = jnp.concatenate([glat, grouter, jnp.zeros((glat.shape[0], -(lanes + experts) % 128), f32)], axis=1).astype(b16)
-    squares = jnp.stack([jnp.sum(v * v) for v in (stream, attn_out, mid, ffn_out, residual)])
-    side = jnp.concatenate(
-        [attn_gain_grad.reshape(quads, -1), ffn_gain_grad.reshape(quads, -1), lat_gain_grad.reshape(quads, -1),
-         jnp.broadcast_to(squares[None], (quads, 5))], axis=1)
+    lat_grad = jnp.pad(lat_grad, ((0, 0), (0, -lanes % 128)))
+    glat = dot_tn(normed, lat_grad).astype(b16).reshape(quads, 4, own_w, -1)
+    grouter = dot_tn(nt_quad, logit_all).astype(b16).reshape(quads, 4, own_w, -1)
+    side = jnp.concatenate([v.reshape(quads, -1) for v in (attn_gain_grad, ffn_gain_grad, lat_gain_grad)], axis=1)
     side = jnp.pad(side, ((0, 0), (0, 1024 - side.shape[1]))).reshape(quads, 8, 128)
-    o_q, o_kv, o_out, o_lat, o_side = to_owners(
-        [gq.reshape(quads, -1, qcols), gkv.reshape(quads, -1, kcols), grad_out.astype(b16).reshape(quads, -1, width),
-         glat.reshape(quads, own_w, -1), side], (True, True, False, False, True), nz, 10)
+    stream_out, o_q, o_kv, o_out, o_lat, o_router, o_side, o_stat = finish(
+        out_own, out_far, stream_in, attn_out, mid,
+        [gq.reshape(quads, -1, qcols), gkv.reshape(quads, -1, kcols), grad_out.astype(b16).reshape(quads, -1, width), glat, grouter, side],
+        nz, 10)
     o_side = o_side.reshape(-1)
     per = width // quads
     perl = kvr // quads
     ga = lax.dynamic_slice_in_dim(o_side, member * own_w, own_w)
     gf = lax.dynamic_slice_in_dim(o_side, per + member * own_w, own_w)
     gla = lax.dynamic_slice_in_dim(o_side, 2 * per + member * (perl // 4), perl // 4)
-    totals = o_side[2 * per + perl : 2 * per + perl + 5]
-    stats = jnp.sqrt(totals / (tok * n_dev * width))
-    fits = lambda v, rows: v if v.shape[1] == rows else lax.dynamic_slice_in_dim(v, member * rows, rows, 1)
-    o_q = jnp.moveaxis(fits(o_q, own_w).astype(f32), 0, 1).reshape(own_w, -1)
-    o_kv = jnp.moveaxis(fits(o_kv, kvr // n_dev).astype(f32), 0, 1).reshape(kvr // n_dev, -1)
-    pairs = []
-    for q in range(quads):
-        for cc in range(2):
-            for xx in range(2):
-                pairs.append((q * 4 + cc * 2 + xx, (xx * 2 + cc) * quads + q))
-    o_out = lax.ppermute(o_out, both, pairs).astype(f32)
-    o_lat = o_lat.astype(f32)
+    stats = jnp.sqrt(jnp.sum(o_stat[:5], axis=1) / (tok * n_dev * width))
     return (
-        residual.astype(b16), grad_stream, stats, ga, o_q, o_lat[:, :kvr], o_lat[:, kvr:lanes], gla, o_kv, o_out, gf,
-        o_lat[:, lanes : lanes + experts], back[0], back[1], grad_sd[:fs], jnp.swapaxes(grad_eg[None], 1, 2), jnp.swapaxes(grad_eu[None], 1, 2), grad_ed[None],
+        stream_out, grad_stream, stats, ga, o_q, o_lat[:, :kvr], o_lat[:, kvr:lanes], gla, o_kv, o_out, gf,
+        o_router[:, :experts], back[0], back[1], grad_sd[:fs], jnp.swapaxes(grad_eg[None], 1, 2), jnp.swapaxes(grad_eu[None], 1, 2), grad_ed[None],
     )
 
 

time: 870 us -> 760 us (0.87)
  Pallas kernels: 667 us -> 600 us
  local copies, waits for them, and re-layouts: 87.9 us -> 55.4 us
    pallas_call x2 -> x1, Pallas kernels: 168 us -> 87 us  [reduce_scatter(): pl.pallas_call(functools.partial(scatter_kernel, nz, i * W), out_shape=ja...]
    pallas_call x1, Pallas kernels: 83.3 us -> 112 us  [all_gather(): pl.pallas_call(functools.partial(gather_kernel, nz), out_shape=[jax.Shape...]
    pallas_call x2 -> x1, Pallas kernels: 41.2 us -> 19.5 us  [quad_gather(): pl.pallas_call(quad_gather_kernel, out_shape=jax.ShapeDtypeStruct((4,) +...]
    another operation x8 -> x0, local copies, waits for them, and re-layouts: 13.4 us -> none  [the longest x4 5.7 us: on_device(): jnp.stack([shared_gate, shared_up], axis=1).reshape(own_w, 2, n_dev, fs)]
    convert_element_type x5 -> x0, local copies, waits for them, and re-layouts: 11.2 us -> none  [the longest x2 8.38 us: on_device(): stream4 = stream_all.reshape(4 * tok, width).astype(f32)]
    pallas_call x1, Pallas kernels: 114 us -> 125 us  [experts_both(): pl.pallas_call(functools.partial(experts_kernel, slots=blocks * capacity)...]
    pallas_call x2 -> x4, Pallas kernels: 216 us -> 208 us  [the longest x1 163 us: finish(): pl.pallas_call(functools.partial(finish_kernel, nz, na), out_shape=shapes...]
    unnamed x228 -> x224, local copies, waits for them, and re-layouts: 21.6 us -> 27.1 us
  transfers between devices with their start and end apart: 4 -> 5, of which waited for: 0 -> 0; matrix products, arithmetic and copies ran while one was open for 11% -> 11% of each run, Pallas kernels for 38% -> 43%
where the time goes in v2:
time: 760 us; the launch traced here: 755 us
  Pallas kernels  600 us (79%)
  local copies, waits for them, and re-layouts  55.4 us (7%)
  matrix products  45.1 us (6%)
  other arithmetic  29.8 us (4%)
  between operations  15.7 us (2%)
  starting transfers between devices  9.08 us (1%)
    pallas_call x1, Pallas kernels, finish(): pl.pallas_call(functools.partial(finish_kernel, nz, na), out_shape=shapes...  163 us
    pallas_call x1, Pallas kernels, experts_both(): pl.pallas_call(functools.partial(experts_kernel, slots=blocks * capacity)...  125 us
    pallas_call x1, Pallas kernels, all_gather(): pl.pallas_call(functools.partial(gather_kernel, nz), out_shape=[jax.Shape...  112 us
    pallas_call x1, Pallas kernels, reduce_scatter(): pl.pallas_call(functools.partial(scatter_kernel, nz, i * W), out_shape=ja...  87 us
    pallas_call x2, Pallas kernels, quad_scatter(): pl.pallas_call(quad_scatter_kernel, out_shape=jax.ShapeDtypeStruct((rows,...  49.4 us
    pallas_call x1, Pallas kernels, open_quad(): pl.pallas_call(functools.partial(open_kernel, nz), out_shape=[sd(shape, v...  41.2 us
    dot_general x20, matrix products, contract(): lax.dot_general(left, right, (over, batch), preferred_element_type=jnp.fl...  35.1 us
    unnamed x224, local copies, waits for them, and re-layouts  27.1 us
  transfers between devices with their start and end apart: 5, of which 0 were waited for; matrix products, arithmetic and copies ran while one was open for 11% of the time, Pallas kernels for 43%

profile of v2, /device:TPU:0, one launch (start us, length us, event | category | flops | bytes accessed | tf_op | source)
XLA Modules:
  0.0 755.4 jit_solution(17564384854729909547)
XLA Ops:
  12.1 2.8 copy-done.5
  17.7 41.2 %shard_map.331 = (bf16[4,128,2048]{2,1,0:T(8,128)(2,1)S(1)}, bf16[2,1024,768]{2,1,0:T(8,128)(2,1)S(1)}, bf16[2,256,1024]{2,1,0:T(8,128)(2,1)S(1)}, bf16[2,1024,5...) custom-call(bf16[128,2048]{1,0:T(8,128)(2,1)S(1)} %copy-done, bf16[1024,3072]{1,0:T(8,128)(2,1)S(1)} %copy-done.5, ...), custom_call_target="tpu_custom_call" | custom-call | bytes 175000000 | tf_op jit(solution)/shard_map/pallas_call | solution.py:492
  64.2 2.2 shard_map.334
  66.4 4.2 all-to-all-start
  70.6 2.5 convert_element_type.225
  74.8 4.6 copy.147
  86.2 1.9 reshape.517
  89.0 2.8 fusion.4
  93.6 1.9 fusion.83
  98.5 2.3 fusion.81
  100.8 3.1 fusion.19
  104.3 3.0 convolution_convert_fusion.4
  107.3 27.8 %shard_map.332.attn = f32[128,2048]{1,0:T(8,128)S(1)} custom-call(bf16[4,128,2048]{2,1,0:T(8,128)(2,1)S(1)} %bitcast.170), custom_call_target="tpu_custom_call" | custom-call | bytes 56000000 | tf_op jit(solution)/shard_map/pallas_call | solution.py:639
  138.8 111.6 %shard_map.333 = (bf16[32,128,2048]{2,1,0:T(8,128)(2,1)}, f32[32,32,128]{2,1,0:T(8,128)}) custom-call(bf16[128,2048]{1,0:T(8,128)(2,1)} %copy-done.33, f32[32,128]{1,0:T(8,128)} %pad_maximum_fusion.7.t_ref), custom_call_target="tpu_custom_call" | custom-call | bytes 297500000 | tf_op jit(solution)/shard_map/pallas_call | solution.py:212
  252.6 3.3 constant_dynamic-slice_fusion
  257.8 124.6 %shard_map.335 = (bf16[16,128,2048]{2,1,0:T(8,128)(2,1)}, bf16[16,128,2048]{2,1,0:T(8,128)(2,1)}, bf16[32,128,2176]{2,1,0:T(8,128)(2,1)}, f32[704,2048]{1,0:T(8,...) custom-call(bf16[32,128,2048]{2,1,0:T(8,128)(2,1)} %get-tuple-element.51.nt_r, ...), custom_call_target="tpu_custom_call" | custom-call | bytes 385000000 | tf_op jit(solution)/shard_map/pallas_call | solution.py:1003
  382.5 87.0 %shard_map.336 = f32[128,2176]{1,0:T(8,128)S(1)} custom-call(bf16[32,128,2176]{2,1,0:T(8,128)(2,1)} %get-tuple-element.56.x_ref), custom_call_target="tpu_custom_call" | custom-call | bytes 297500000 | tf_op jit(solution)/shard_map/pallas_call | solution.py:347
  473.1 19.5 %shard_map.337 = bf16[4,128,2176]{2,1,0:T(8,128)(2,1)} custom-call(bf16[128,2176]{1,0:T(8,128)(2,1)} %fusion.35.x_ref), custom_call_target="tpu_custom_call" | custom-call | bytes 63000000 | tf_op jit(solution)/shard_map/pallas_call | solution.py:585
  492.6 3.5 fusion.14
  496.8 3.8 convolution_bitcast_fusion
  513.7 21.6 %shard_map.338 = f32[128,2048]{1,0:T(8,128)S(1)} custom-call(bf16[4,128,2048]{2,1,0:T(8,128)(2,1)S(1)} %bitcast.169), custom_call_target="tpu_custom_call" | custom-call | bytes 56000000 | tf_op jit(solution)/shard_map/pallas_call | solution.py:639
  535.3 3.8 all-to-all-start.1
  539.1 2.2 slice.127
  541.3 3.0 convolution_convert_fusion.6
  544.3 2.7 convolution_convert_fusion.3
  550.6 3.5 convolution_convert_fusion
  555.6 2.5 fusion.77
  563.4 5.0 convolution_convert_fusion.1
  568.4 162.9 %shard_map.339 = (bf16[128,2048]{1,0:T(8,128)(2,1)}, f32[64,3072]{1,0:T(8,128)}, f32[16,4096]{1,0:T(8,128)}, f32[64,2048]{1,0:T(8,128)}, f32[64,640]{1,0:T(8,128...) custom-call(bf16[16,128,2048]{2,1,0:T(8,128)(2,1)} %get-tuple-element.54.own, ...), custom_call_target="tpu_custom_call" | custom-call | bytes 455000000 | tf_op jit(solution)/shard_map/pallas_call | solution.py:890
  739.6 2.6 fusion.32
  742.2 1.9 shard_map.340
  744.0 1.9 copy.229
  (335 shorter events, 72.7 us)
Async XLA Ops:
  7.2 250.6 %all-gather.3.cloned.1.call-start = ((), (), s32[]{:S(2)}) async-start(), calls=%async_computation.2 | async-start | bytes 17301504 | tf_op jit(solution)/shard_map/all_gather | solution.py:1066
  61.9 21.9 %copy-start.13 = (bf16[2,256,1024]{2,1,0:T(8,128)(2,1)}, bf16[2,256,1024]{2,1,0:T(8,128)(2,1)S(1)}, u32[]{:S(2)}) copy-start(bf16[2,256,1024]{2,1,0:T(8,128)(2,1)S(1)} %get-tuple-element.50) | copy-start | bytes 3145732
  66.4 191.5 %all-to-all-start = ((bf16[32,64,256]{2,1,0:T(8,128)(2,1)}), bf16[32,64,256]{2,1,0:T(8,128)(2,1)}, u32[]{:S(2)}, u32[]{:S(2)}) async-start(bf16[32,64,256]{2,1,0:T(8,128)(2,1)} %shard_map.334), calls=%async_computation | async-start | bytes 2097152 | tf_op jit(solution)/shard_map/all_to_all | solution.py:1074
  79.5 56.6 %copy-start.83 = (f32[1,2048]{1,0:T(1,128)}, f32[1,2048]{1,0:T(1,128)S(1)}, u32[]{:S(2)}) copy-start(f32[1,2048]{1,0:T(1,128)S(1)} %get-tuple-element.185) | copy-start | bytes 24580
  79.6 176.4 %copy-start.74 = (f32[1,2048]{1,0:T(1,128)}, f32[1,2048]{1,0:T(1,128)S(1)}, u32[]{:S(2)}) copy-start(f32[1,2048]{1,0:T(1,128)S(1)} %get-tuple-element.186) | copy-start | bytes 24580
  89.0 6.4 copy-start.56
  107.3 27.8 %copy-start.1 = (bf16[128,2048]{1,0:T(8,128)(2,1)S(1)}, bf16[128,2048]{1,0:T(8,128)(2,1)}, u32[]{:S(2)}) copy-start(bf16[128,2048]{1,0:T(8,128)(2,1)} %stream.3) | copy-start | bytes 1572868
  135.5 115.0 %copy-start.73 = (bf16[88,2048]{1,0:T(8,128)(2,1)S(1)}, bf16[88,2048]{1,0:T(8,128)(2,1)}, u32[]{:S(2)}) copy-start(bf16[88,2048]{1,0:T(8,128)(2,1)} %param.36) | copy-start | bytes 1081348
  136.7 119.2 %copy-start.91 = (f32[128]{0:T(128)}, f32[128]{0:T(128)S(1)}, u32[]{:S(2)}) copy-start(f32[128]{0:T(128)S(1)} %get-tuple-element.212) | copy-start | bytes 1540
  136.8 119.1 %copy-start.42 = (f32[128,16]{1,0:T(8,128)}, f32[128,16]{1,0:T(8,128)S(1)}, u32[]{:S(2)}) copy-start(f32[128,16]{1,0:T(8,128)S(1)} %copy.155) | copy-start | bytes 24580
  137.0 119.0 %copy-start.52 = (f32[128,16]{1,0:T(8,128)}, f32[128,16]{1,0:T(8,128)S(1)}, u32[]{:S(2)}) copy-start(f32[128,16]{1,0:T(8,128)S(1)} %copy.154) | copy-start | bytes 24580
  137.1 118.8 %copy-start.54 = (f32[128,16]{1,0:T(8,128)}, f32[128,16]{1,0:T(8,128)S(1)}, u32[]{:S(2)}) copy-start(f32[128,16]{1,0:T(8,128)S(1)} %copy.153) | copy-start | bytes 24580
  137.3 118.7 %copy-start.93 = (f32[128]{0:T(128)}, f32[128]{0:T(128)S(1)}, u32[]{:S(2)}) copy-start(f32[128]{0:T(128)S(1)} %fusion.58) | copy-start | bytes 1540
  138.2 117.7 %copy-start.99 = (f32[128]{0:T(128)}, f32[128]{0:T(128)S(1)}, u32[]{:S(2)}) copy-start(f32[128]{0:T(128)S(1)} %get-tuple-element.172) | copy-start | bytes 1540
  382.4 87.4 %copy-start.55 = (f32[128,16]{1,0:T(8,128)S(1)}, f32[128,16]{1,0:T(8,128)}, u32[]{:S(2)}) copy-start(f32[128,16]{1,0:T(8,128)} %copy-done.54) | copy-start | bytes 24580
  382.4 87.4 %copy-start.81 = (f32[128,16]{1,0:T(8,128)S(1)}, f32[128,16]{1,0:T(8,128)}, u32[]{:S(2)}) copy-start(f32[128,16]{1,0:T(8,128)} %get-tuple-element.173) | copy-start | bytes 24580
  382.5 87.5 %copy-start.100 = (f32[128]{0:T(128)S(1)}, f32[128]{0:T(128)}, u32[]{:S(2)}) copy-start(f32[128]{0:T(128)} %copy-done.99) | copy-start | bytes 1540
  382.5 87.5 %copy-start.43 = (f32[128,16]{1,0:T(8,128)S(1)}, f32[128,16]{1,0:T(8,128)}, u32[]{:S(2)}) copy-start(f32[128,16]{1,0:T(8,128)} %copy-done.42) | copy-start | bytes 24580
  382.5 87.5 %copy-start.53 = (f32[128,16]{1,0:T(8,128)S(1)}, f32[128,16]{1,0:T(8,128)}, u32[]{:S(2)}) copy-start(f32[128,16]{1,0:T(8,128)} %copy-done.52) | copy-start | bytes 24580
  382.5 87.5 %copy-start.92 = (f32[128]{0:T(128)S(1)}, f32[128]{0:T(128)}, u32[]{:S(2)}) copy-start(f32[128]{0:T(128)} %copy-done.91) | copy-start | bytes 1540
  382.5 87.5 %copy-start.94 = (f32[128]{0:T(128)S(1)}, f32[128]{0:T(128)}, u32[]{:S(2)}) copy-start(f32[128]{0:T(128)} %copy-done.93) | copy-start | bytes 1540
  382.5 87.9 %copy-start.18 = (f32[128,2048]{1,0:T(8,128)S(1)}, f32[128,2048]{1,0:T(8,128)}, u32[]{:S(2)}) copy-start(f32[128,2048]{1,0:T(8,128)} %copy-done.17) | copy-start | bytes 3145732
  382.5 87.9 %copy-start.62 = (bf16[16,2048]{1,0:T(8,128)(2,1)S(1)}, bf16[16,2048]{1,0:T(8,128)(2,1)}, u32[]{:S(2)}) copy-start(bf16[16,2048]{1,0:T(8,128)(2,1)} %copy-done.61) | copy-start | bytes 196612
  382.5 87.9 %copy-start.84 = (f32[1,2048]{1,0:T(1,128)S(1)}, f32[1,2048]{1,0:T(1,128)}, u32[]{:S(2)}) copy-start(f32[1,2048]{1,0:T(1,128)} %copy-done.83) | copy-start | bytes 24580
  382.5 87.9 %copy-start.97 = (f32[128]{0:T(128)S(1)}, f32[128]{0:T(128)}, u32[]{:S(2)}) copy-start(f32[128]{0:T(128)} %copy-done.96) | copy-start | bytes 1540
  509.2 37.7 %collective-permute-start = (bf16[512,576]{0,1:T(8,128)(2,1)}, bf16[512,576]{0,1:T(8,128)(2,1)}, u32[]{:S(2)}, u32[]{:S(2)}) collective-permute-start(bf16[512,576]{0,1:T(8,128)(2,1)} %pad_maximum_fusion.2), channel_id=1, source_target_pairs={{1,0},{0,1},{3,2},{2,3},{5,4},{4,5},{7,6},{6,7},{9,8},{8,9},{11,10... | collective-permute-start | bytes 1769480 | tf_op jit(solution)/shard_map/ppermute | solution.py:1023
  535.3 206.8 %all-to-all-start.1 = ((bf16[32,64,256]{2,1,0:T(8,128)(2,1)}), bf16[32,64,256]{2,1,0:T(8,128)(2,1)S(1)}, u32[]{:S(2)}, u32[]{:S(2)}) async-start(bf16[32,64,256]{2,1,0:T(8,128)(2,1)} %bitcast.197), calls=%async_computation.1 | async-start | bytes 2097152 | tf_op jit(solution)/shard_map/all_to_all | solution.py:1118
  548.2 5.9 collective-permute-start.1
  568.4 171.1 %copy-start.3 = (bf16[128,2048]{1,0:T(8,128)(2,1)S(1)}, bf16[128,2048]{1,0:T(8,128)(2,1)}, u32[]{:S(2)}) copy-start(bf16[128,2048]{1,0:T(8,128)(2,1)} %stream.3) | copy-start | bytes 1572868
  568.4 171.1 %copy-start.38 = (f32[128,2048]{1,0:T(8,128)S(1)}, f32[128,2048]{1,0:T(8,128)}, u32[]{:S(2)}) copy-start(f32[128,2048]{1,0:T(8,128)} %get-tuple-element.169) | copy-start | bytes 3145732
  568.4 171.1 %copy-start.104 = (f32[128]{0:T(128)S(1)}, f32[128]{0:T(128)}, u32[]{:S(2)}) copy-start(f32[128]{0:T(128)} %get-tuple-element.204) | copy-start | bytes 1540
  739.6 6.3 copy-start.58
  (81 other events, 174.1 us)
Sparse Core Ops, SparseCore 0:
  62.0 174.0 all-gather.2

commit v3 on v2

--- a/solution.py
+++ b/solution.py
@@ -241,7 +241,9 @@
     lax.fori_loop(0, count // step, body, 0)
 
 
-def scatter_kernel(nz, lo, x_ref, o_ref, mine, core, one, two, line, load_sem, core_send, core_recv, one_send, one_recv, two_send, two_recv, line_send, line_recv):
+def scatter_kernel(nz, x_ref, rows_in, rows_grad, hid, dg, du, o_ref, dwg_o, dwu_o, dwd_o, mine, core, one, two, line,
+                   dwg, dwu, dwd, b_in, b_grad, b_hid, b_dg, b_du, load_sem, core_send, core_recv, one_send, one_recv,
+                   two_send, two_recv, line_send, line_recv, chunk_sem, out_sem):
     z, y, c, x = place()
     nbr = neighbours(nz)
     greet(nbr)
@@ -249,17 +251,60 @@
     half = T // 2
     rows = lambda h: pl.ds(h * half, half)
     place_of = lambda zb, yb, xb: (zb * 2 + yb) * 2 + xb
-    cols = pl.ds(lo, mine.shape[2])
+    count = b_in.shape[1]
+    chunks = rows_in.shape[0] // count
+
+    def chunk_copies(i):
+        r = pl.ds(i * count, count)
+        pairs = ((rows_in, b_in), (rows_grad, b_grad), (hid, b_hid), (dg, b_dg), (du, b_du))
+        return [pltpu.make_async_copy(a.at[r], b.at[i % 2], chunk_sem.at[i % 2, j]) for j, (a, b) in enumerate(pairs)]
+
+    def result(j):
+        out, b = ((dwg_o, b_in), (dwu_o, b_grad), (dwd_o, b_in))[j]
+        spans = [(k, lo, min(count, out.shape[0] - lo)) for k, lo in enumerate(range(0, out.shape[0], count))]
+        return spans, [
+            pltpu.make_async_copy(b.at[k, pl.ds(0, n)], out.at[pl.ds(lo, n)], out_sem.at[j, k]) for k, lo, n in spans
+        ]
+
+    def write(j):
+        total, b = ((dwg, b_in), (dwu, b_grad), (dwd, b_in))[j]
+        spans, copies = result(j)
+        for k, lo, n in spans:
+            b[k, 0:n] = total[lo : lo + n].astype(b.dtype)
+        for d in copies:
+            d.start()
+
+    def written(j):
+        for d in result(j)[1]:
+            d.wait()
+
+    def chunk(i):
+        if i >= chunks:
+            return
+        for d in chunk_copies(i):
+            d.wait()
+        k = i % 2
+        terms = ((dwd, b_hid, b_grad), (dwg, b_dg, b_in), (dwu, b_du, b_in))
+        for total, a, b in terms:
+            v = dot_tn(a[k], b[k])
+            total[...] = v if i == 0 else total[...] + v
+        if i + 2 < chunks:
+            for d in chunk_copies(i + 2):
+                d.start()
+        if i == chunks - 1:
+            write(0)
+            write(1)
+
     order = far_first(nz, z)
     combos = [(1 - y, 1 - x), (y, 1 - x), (1 - y, x), (y, x)]
 
     def core_copy(zb, yb, xb):
         k = place_of(zb, yb, xb)
-        return remote(x_ref.at[slot(zb, yb, 1 - c, xb), :, cols], core.at[k], core_send.at[k], core_recv.at[k], nbr["c"][0])
+        return remote(x_ref.at[slot(zb, yb, 1 - c, xb)], core.at[k], core_send.at[k], core_recv.at[k], nbr["c"][0])
 
     def load(zb, yb, xb):
         k = place_of(zb, yb, xb)
-        return pltpu.make_async_copy(x_ref.at[slot(zb, yb, c, xb), :, cols], mine.at[k], load_sem.at[k])
+        return pltpu.make_async_copy(x_ref.at[slot(zb, yb, c, xb)], mine.at[k], load_sem.at[k])
 
     def one_copy(h, zb, j):
         k = place_of(zb, j, 1 - x) if h == 0 else place_of(zb, 1 - y, j)
@@ -279,6 +324,9 @@
         for yb, xb in combos:
             core_copy(zb, yb, xb).start()
             load(zb, yb, xb).start()
+    for i in range(min(2, chunks)):
+        for d in chunk_copies(i):
+            d.start()
 
     def stage0(zb):
         for n, (yb, xb) in enumerate(combos):
@@ -315,9 +363,15 @@
             when(zb < z, lambda: line_copy(h, zb, False).start())
 
     for i in range(nz + 2):
-        if i < nz: stage0(order[i])
-        if 1 <= i < nz + 1: stage1(order[i - 1])
-        if 2 <= i: stage2(order[i - 2])
+        if i < nz:
+            stage0(order[i])
+        chunk(i)
+        if 1 <= i < nz + 1:
+            stage1(order[i - 1])
+        if 2 <= i:
+            stage2(order[i - 2])
+    written(0)
+    write(2)
     k = place_of(z, y, x)
     for h in (0, 1):
         lo = h * half
@@ -327,6 +381,8 @@
                 line_copy(h, z, d == 0).wait_recv()
                 o_ref[rows(h)] += line[d, h, z].astype(jnp.float32)
             when(ok, fin)
+    written(1)
+    written(2)
     for zb in order:
         for yb, xb in combos:
             core_copy(zb, yb, xb).wait_send()
@@ -337,32 +393,28 @@
             when(zb > z, lambda: line_copy(h, zb, True).wait_send())
             when(zb < z, lambda: line_copy(h, zb, False).wait_send())
 
-def reduce_scatter(x, nz, cid):
-    N, T, D = x.shape
-    sem = pltpu.SemaphoreType.DMA
-    bf = x.dtype
-    parts = max(1, N // 32)
-    W = D // parts
-    outs = [
-        pl.pallas_call(
-            functools.partial(scatter_kernel, nz, i * W),
-            out_shape=jax.ShapeDtypeStruct((T, W), jnp.float32),
-            in_specs=[pl.BlockSpec(memory_space=pl.ANY)],
-            out_specs=pl.BlockSpec(memory_space=pltpu.VMEM),
-            scratch_shapes=[
-                pltpu.VMEM((N // 2, T, W), bf), pltpu.VMEM((N // 2, T, W), bf),
-                pltpu.VMEM((2, 2 * nz, T // 2, W), bf), pltpu.VMEM((2, nz, T // 2, W), bf),
-                pltpu.VMEM((2, 2, nz, T // 2, W), bf),
-                sem((N // 2,)), sem((N // 2,)), sem((N // 2,)), sem((2, 2 * nz)), sem((2, 2 * nz)),
-                sem((2, nz)), sem((2, nz)), sem((2, nz)), sem((2, 2, nz))],
-            cost_estimate=lasting(85),
-        compiler_params=pltpu.CompilerParams(
-                collective_id=cid + i, has_side_effects=True, vmem_limit_bytes=48 << 20
-            ),
-        )(x)
-        for i in range(parts)
-    ]
-    return outs[0] if parts == 1 else jnp.concatenate(outs, axis=1)
+def reduce_scatter(v, rows_in, rows_grad, hid, dg, du, nz, cid):
+    n, tok, width = v.shape
+    rows, wide = rows_in.shape
+    f = hid.shape[1]
+    parts = next(k for k in (4, 2, 1) if rows % (k * 16) == 0)
+    b16, f32, sd = v.dtype, jnp.float32, jax.ShapeDtypeStruct
+    buf = lambda *shape: pltpu.VMEM(shape, b16)
+    grad = sd((f, wide), b16)
+    return pl.pallas_call(
+        functools.partial(scatter_kernel, nz),
+        out_shape=[sd((tok, width), f32), grad, grad, grad],
+        in_specs=[HBM] * 6,
+        out_specs=[pl.BlockSpec(memory_space=pltpu.VMEM), HBM, HBM, HBM],
+        scratch_shapes=[buf(n // 2, tok, width), buf(n // 2, tok, width), buf(2, 2 * nz, tok // 2, width),
+                        buf(2, nz, tok // 2, width), buf(2, 2, nz, tok // 2, width)]
+        + [pltpu.VMEM((f, wide), f32)] * 3
+        + [buf(2, rows // parts, k) for k in (wide, wide, f, f, f)]
+        + [SEM((n // 2,)), SEM((n // 2,)), SEM((n // 2,)), SEM((2, 2 * nz)), SEM((2, 2 * nz)), SEM((2, nz)), SEM((2, nz)),
+           SEM((2, nz)), SEM((2, 2, nz)), SEM((2, 5)), SEM((3, 2))],
+        cost_estimate=lasting(90),
+        compiler_params=pltpu.CompilerParams(collective_id=cid, has_side_effects=True, vmem_limit_bytes=64 << 20),
+    )(v, rows_in, rows_grad, hid, dg, du)
 
 
 def lasting(us):
@@ -649,8 +701,9 @@
     )(v)
 
 
-def finish_kernel(nz, na, own, far, stream, attn, mid, *refs):
+def finish_kernel(nz, na, there, own, far, stream, attn, mid, *refs):
     ins, refs = refs[:na], refs[na:]
+    others, refs = dict(zip(there, refs)), refs[len(there) :]
     (res_o, q_o, kv_o, out_o, lat_o, router_o, side_o, stat_o), refs = refs[:8], refs[8:]
     (t_mine, t_core, t_one, t_two, t_line, ffn), refs = refs[:6], refs[6:]
     mine, refs = refs[:na], refs[na:]
@@ -670,10 +723,10 @@
     away = target != linear
     nbr["to"] = ((target // 2, lax.rem(target, 2)), away)
     nbr["from"] = (source, away)
-    bits = [b for b in range(8) if 1 << b < nz]
-    for b in bits:
-        low = lax.rem(z // (1 << b), 2)
-        nbr["z%d" % b] = (device(z + (1 - 2 * low) * (1 << b), y, c, x), None)
+    here_q = z * 2 + y
+    for j in range(1, quads):
+        there = lax.rem(here_q + j, quads)
+        nbr["q%d" % j] = (device(there // 2, lax.rem(there, 2), c, x), None)
     greet(nbr)
     order = far_first(nz, z)
     xdev, cdev, ddev, ydev = (nbr[k][0] for k in ("x", "c", "d", "y"))
@@ -732,11 +785,15 @@
 
         on_line(zb, arrive, lambda right: tz_copy(zb, right).start())
 
+    apart = [a for a in range(na) if a not in others]
+
     def w_load(a, k):
         src = ins[a].at[k, c * 2 + x] if len(ins[a].shape) == 4 else ins[a].at[k]
         return pltpu.make_async_copy(src, mine[a].at[k], load.at[a, k])
 
     def wy_copy(a, zb):
+        if a in others:
+            return pltpu.make_async_copy(others[a].at[zb], one[a].at[zb], y_recv.at[a, zb])
         return remote(mine[a].at[zb * 2 + 1 - y], one[a].at[zb], y_send.at[a, zb], y_recv.at[a, zb], ydev)
 
     def wz_copy(a, zb, right):
@@ -744,7 +801,7 @@
         return remote(mine[a].at[zb * 2 + y], line[a].at[d, zb], z_send.at[a, zb], z_recv.at[d, a, zb], zdev(right))
 
     def w_stage0(zb):
-        for a in range(na):
+        for a in apart:
             w_load(a, zb * 2 + 1 - y).wait()
             wy_copy(a, zb).start()
 
@@ -752,7 +809,8 @@
         for a in range(na):
             total = mine[a].at[zb * 2 + y]
             w_load(a, zb * 2 + y).wait()
-            wy_copy(a, zb).wait_recv()
+            d = wy_copy(a, zb)
+            d.wait() if a in others else d.wait_recv()
             add(total, one[a].at[zb])
 
             def arrive(right):
@@ -766,9 +824,12 @@
             k = place_of(zb, yb, xb)
             t_core_copy(k).start()
             t_load_copy(k).start()
-        for yb in (1 - y, y):
-            for a in range(na):
-                w_load(a, zb * 2 + yb).start()
+        for a in apart:
+            w_load(a, zb * 2 + 1 - y).start()
+        for a in range(na):
+            w_load(a, zb * 2 + y).start()
+        for a in others:
+            wy_copy(a, zb).start()
     for i in range(nz):
         if i < 2:
             w_stage0(order[i])
@@ -802,19 +863,25 @@
 
     sums = lax.fori_loop(0, mid.shape[0] // rows, body, (jnp.zeros((1, 128), jnp.float32),) * 5)
     stat[...] = jnp.concatenate(sums + (jnp.zeros((3, 128), jnp.float32),), axis=0)
-    rounds = ["c", "x", "y"] + ["z%d" % b for b in bits]
-
-    def stat_copy(i):
-        return remote(stat, stat_in.at[i], st_send.at[i], st_recv.at[i], nbr[rounds[i]][0])
-
-    def stat_next(i):
-        if 0 < i <= len(rounds):
-            stat_copy(i - 1).wait()
-            stat[...] = stat[...] + stat_in[i - 1]
-        if i < len(rounds):
-            stat_copy(i).start()
-
-    stat_next(0)
+    near, wide = ["x", "c", "d"], ["q%d" % j for j in range(1, quads)]
+
+    def stat_copy(keys, key):
+        i = 3 * (keys is wide) + keys.index(key)
+        return remote(stat, stat_in.at[i], st_send.at[i], st_recv.at[i], nbr[key][0])
+
+    def stat_start(keys):
+        for key in keys:
+            stat_copy(keys, key).start()
+
+    def stat_end(keys):
+        for key in keys:
+            stat_copy(keys, key).wait()
+        total = stat[...]
+        for i in range(len(keys)):
+            total = total + stat_in[3 * (keys is wide) + i]
+        stat[...] = total
+
+    stat_start(near)
 
     k = z * 2 + y
     member, group = c * 2 + x, x * 2 + c
@@ -846,9 +913,10 @@
             when(away, lambda: to.start())
             when(jnp.logical_not(away), lambda: stay.start())
 
-        stat_next(n_done + 1)
-    for i in range(na + 1, len(rounds) + 1):
-        stat_next(i)
+        if n_done == 1:
+            stat_end(near)
+            stat_start(wide)
+    stat_end(wide)
     stat_o[...] = stat[...]
     router_o[...] = mine[4][k].astype(jnp.float32)
     lat_o[...] = mine[3][k].astype(jnp.float32)
@@ -871,11 +939,12 @@
         ty_copy(zb).wait_send()
         on_line(zb, lambda right: None, lambda right: tz_copy(zb, right).wait_send())
         for a in range(na):
-            wy_copy(a, zb).wait_send()
+            if a in apart:
+                wy_copy(a, zb).wait_send()
             on_line(zb, lambda right: None, lambda right: wz_copy(a, zb, right).wait_send())
 
 
-def finish(own, far, stream, attn, mid, arrays, nz, cid):
+def finish(own, far, stream, attn, mid, arrays, swapped, nz, cid):
     na = len(arrays)
     tok, width = mid.shape
     n, quads = 4 * nz, 2 * nz
@@ -888,9 +957,9 @@
     ]
     buf = lambda *shape: pltpu.VMEM(shape, b16)
     return pl.pallas_call(
-        functools.partial(finish_kernel, nz, na),
+        functools.partial(finish_kernel, nz, na, tuple(swapped)),
         out_shape=shapes,
-        in_specs=[HBM, HBM, vmem, vmem, vmem] + [HBM] * na,
+        in_specs=[HBM, HBM, vmem, vmem, vmem] + [HBM] * (na + len(swapped)),
         out_specs=[vmem] * 8,
         scratch_shapes=[buf(n, tok, width), buf(n, tok, width), buf(quads, tok, width), buf(nz, tok, width),
                         buf(2, nz, tok, width), pltpu.VMEM((8, 128), f32)]
@@ -898,13 +967,13 @@
         + [pltpu.VMEM((nz,) + v.shape[-2:], v.dtype) for v in arrays]
         + [pltpu.VMEM((2, nz) + v.shape[-2:], v.dtype) for v in arrays]
         + [buf(4, q.shape[1] // 4, q.shape[2]), buf(4, kv.shape[1] // 4, kv.shape[2]), buf(*out.shape[1:]),
-           pltpu.VMEM((4,) + side.shape[1:], f32), pltpu.VMEM((8, 128), f32), pltpu.VMEM((8, 8, 128), f32)]
+           pltpu.VMEM((4,) + side.shape[1:], f32), pltpu.VMEM((8, 128), f32), pltpu.VMEM((quads + 2, 8, 128), f32)]
         + [SEM((n,)), SEM((n,)), SEM((n,)), SEM((quads,)), SEM((quads,)), SEM((nz,)), SEM((nz,)), SEM((nz,)), SEM((2, nz)),
            SEM((na, quads)), SEM((na, nz)), SEM((na, nz)), SEM((na, nz)), SEM((2, na, nz)), SEM((na,)), SEM((na, 3)),
-           SEM((na, 3)), SEM, SEM, SEM((8,)), SEM((8,))],
+           SEM((na, 3)), SEM, SEM, SEM((quads + 2,)), SEM((quads + 2,))],
         cost_estimate=lasting(130),
         compiler_params=pltpu.CompilerParams(collective_id=cid, has_side_effects=True, vmem_limit_bytes=58 << 20),
-    )(own, far, stream, attn, mid, *arrays)
+    )(own, far, stream, attn, mid, *arrays, *swapped.values())
 
 
 def silu_parts(values):
@@ -913,13 +982,13 @@
 
 
 def experts_kernel(nt_ref, sg_ref, tail_ref, wg_ref, wu_ref, wd_ref, ws_ref, wsd_ref,
-                   own_ref, far_ref, ng_ref, dwg_hbm, dwu_hbm, dwd_hbm, dws_out, dsd_ref,
-                   dwg, dwu, dwd, dws_ref, sem, *, slots):
+                   own_ref, far_ref, ng_ref, x_ref, g_ref, hid_ref, dg_ref, du_ref, dws_out, dsd_ref,
+                   dws_ref, *, slots):
     f32, b16 = jnp.float32, jnp.bfloat16
     i = pl.program_id(0)
     @pl.when(i == 0)
     def _():
-        for r in (dwg, dwu, dwd, dws_ref, dsd_ref):
+        for r in (dws_ref, dsd_ref):
             r[...] = jnp.zeros_like(r)
     tokens = nt_ref.shape[0] * nt_ref.shape[1]
     width = nt_ref.shape[2]
@@ -938,9 +1007,11 @@
     hit = lax.broadcasted_iota(jnp.int32, (slots, tokens), 0) == in_row(place_of)
     pick = hit.astype(f32).astype(b16)
     x = wide_product(pick, nt).astype(b16)
+    x_ref[...] = x
     g0 = wide_product(pick, sg)
     gate = jnp.sum(jnp.where(hit, in_row(gate_row), 0.0), axis=1, keepdims=True)
     g = (gate * g0).astype(b16)
+    g_ref[...] = g
     gv = dot_nt(x, wg_ref[...])
     uv = dot_nt(x, wu_ref[...])
     act, slope = silu_parts(gv)
@@ -952,12 +1023,12 @@
     lane = lax.broadcasted_iota(jnp.int32, (slots, 128), 1)
     gg = jnp.where(lane == column, gg_high, jnp.where(lane == column + 1, gg - gg_high, 0.0)).astype(b16)
     e_out = (gate * part).astype(b16)
-    dwd[...] += dot_tn(hid, g)
+    hid_ref[...] = hid
     hg = dot_nt(g, wd_ref[...])
     dg = (hg * uv * slope).astype(b16)
     du = (hg * act).astype(b16)
-    dwg[...] += dot_tn(dg, x)
-    dwu[...] += dot_tn(du, x)
+    dg_ref[...] = dg
+    du_ref[...] = du
     ing = (wide_product(dg, wg_ref[...]) + wide_product(du, wu_ref[...])).astype(b16)
     fs = wsd_ref.shape[0]
     s = wide_product(nt, ws_ref[...])
@@ -983,10 +1054,7 @@
     ng_ref[:, :, width:] = dot_tn(pick, gg).astype(b16).reshape(ng_ref.shape[:2] + (128,))
     @pl.when(i == pl.num_programs(0) - 1)
     def _():
-        cs = [pltpu.make_async_copy(a, b, sem.at[j]) for j, (a, b) in enumerate(((dwg, dwg_hbm), (dwu, dwu_hbm), (dwd, dwd_hbm)))]
-        for c in cs: c.start()
         dws_out[...] = dws_ref[...].T.astype(b16)
-        for c in cs: c.wait()
 
 def experts_both(nt, sg, tails, wg, wu, wd, ws, wsd, capacity, blocks=4):
     n, tok, width = nt.shape
@@ -998,19 +1066,20 @@
     half = pl.BlockSpec((blocks // 2, tok, width), lambda i: (i, 0, 0))
     row = pl.BlockSpec((blocks,) + tails.shape[1:], lambda i: (i, 0, 0))
     sd = jax.ShapeDtypeStruct
-    anyspec = HBM
-    acc = pltpu.VMEM((f, width), f32)
+    kept = lambda k: pl.BlockSpec((blocks * capacity, k), lambda i: (i, 0))
     return pl.pallas_call(
         functools.partial(experts_kernel, slots=blocks * capacity),
         grid=(steps,),
         in_specs=[blk, blk, row] + [one(w) for w in (wg, wu, wd, ws, wsd)],
-        out_specs=[half, half, pl.BlockSpec((blocks, tok, width + 128), lambda i: (i, 0, 0)), anyspec, anyspec, anyspec,
-                   pl.BlockSpec((width, 2 * fs), lambda i: (0, 0)), pl.BlockSpec((fs, width), lambda i: (0, 0))],
-        out_shape=[sd((n // 2, tok, width), nt.dtype)] * 2 + [sd((n, tok, width + 128), nt.dtype),
-                   sd((f, width), f32), sd((f, width), f32), sd((f, width), f32),
-                   sd((width, 2 * fs), nt.dtype), sd((fs, width), f32)],
-        scratch_shapes=[acc, acc, acc, pltpu.VMEM((2 * fs, width), f32), SEM((3,))],
-        compiler_params=pltpu.CompilerParams(vmem_limit_bytes=64 << 20, dimension_semantics=("arbitrary",)),
+        out_specs=[half, half, pl.BlockSpec((blocks, tok, width + 128), lambda i: (i, 0, 0)), kept(width), kept(width)]
+        + [kept(f)] * 3
+        + [pl.BlockSpec((width, 2 * fs), lambda i: (0, 0)), pl.BlockSpec((fs, width), lambda i: (0, 0))],
+        out_shape=[sd((n // 2, tok, width), nt.dtype)] * 2
+        + [sd((n, tok, width + 128), nt.dtype)]
+        + [sd((n * capacity, k), nt.dtype) for k in (width, width, f, f, f)]
+        + [sd((width, 2 * fs), nt.dtype), sd((fs, width), f32)],
+        scratch_shapes=[pltpu.VMEM((2 * fs, width), f32)],
+        compiler_params=pltpu.CompilerParams(vmem_limit_bytes=62 << 20, dimension_semantics=("arbitrary",)),
         cost_estimate=lasting(110),
     )(nt, sg, tails, wg, wu, wd, ws, wsd)
 
@@ -1112,9 +1181,9 @@
     nt_all, tails = all_gather(normed_two, jnp.concatenate([gates.T, mask.T], axis=0), n_dev, nz, 4)
 
     mats = (jnp.swapaxes(expert_gate, 1, 2)[0], jnp.swapaxes(expert_up, 1, 2)[0], expert_down[0], w_s, w_sd)
-    out_own, out_far, n_grad, grad_eg, grad_eu, grad_ed, grad_s, grad_sd = experts_both(
+    out_own, out_far, n_grad, *kept, grad_s, grad_sd = experts_both(
         nt_all, grad_all, tails, *mats, capacity, 4)
-    n_grad = reduce_scatter(n_grad, nz, 16)
+    n_grad, grad_eg, grad_eu, grad_ed = reduce_scatter(n_grad, *kept, nz, 16)
     back = lax.all_to_all(grad_s.reshape(n_dev, own_w, 2 * lanes_s), both, split_axis=0, concat_axis=0, tiled=True)
     back = join_units(back, n_dev * fs, fs)
     gate_grad = jnp.sum(n_grad[:, width : width + 4 * experts].reshape(tok, experts, 4), axis=-1)
@@ -1135,6 +1204,14 @@
 
     att_grad = dot_nt(aog_all, mat_out).astype(b16)
     grad_out = dot_tn(attended, aog_all)
+    grad_out = grad_out.astype(b16).reshape(quads, -1, width)
+    y_of = lax.rem(rep // 2, 2)
+
+    def over_y(v):
+        far = lax.dynamic_index_in_dim(v.reshape((nz, 2) + v.shape[1:]), 1 - y_of, 1, False)
+        return swap(far, nz, lambda z, y, c, x: (z, 1 - y, c, x))
+
+    out_y = over_y(grad_out)
     att_grad = att_grad.reshape(2, seq, heads, DV)
     value_grad = jnp.swapaxes(contract(probs_low, att_grad, ((2,), (1,)), ((0, 1), (0, 2))), 1, 2)
     prob_grad_a = contract(att_grad, values, ((3,), (3,)), ((0, 2), (0, 2)))
@@ -1168,7 +1245,8 @@
     grad_stream = (mid_grad + attn_part).astype(b16)
 
     gq = dot_tn(normed, query_grad).astype(b16)
-    gkv = dot_tn(latent_normed, keyval_grad).astype(b16)
+    gkv = dot_tn(latent_normed, keyval_grad).astype(b16).reshape(quads, -1, kcols)
+    kv_y = over_y(gkv)
     nt_quad = lax.dynamic_slice_in_dim(nt_all, (rep // 2) * 4, 4, 0).reshape(4 * tok, width)
     lat_grad = jnp.pad(lat_grad, ((0, 0), (0, -lanes % 128)))
     glat = dot_tn(normed, lat_grad).astype(b16).reshape(quads, 4, own_w, -1)
@@ -1177,8 +1255,7 @@
     side = jnp.pad(side, ((0, 0), (0, 1024 - side.shape[1]))).reshape(quads, 8, 128)
     stream_out, o_q, o_kv, o_out, o_lat, o_router, o_side, o_stat = finish(
         out_own, out_far, stream_in, attn_out, mid,
-        [gq.reshape(quads, -1, qcols), gkv.reshape(quads, -1, kcols), grad_out.astype(b16).reshape(quads, -1, width), glat, grouter, side],
-        nz, 10)
+        [gq.reshape(quads, -1, qcols), gkv, grad_out, glat, grouter, side], {1: kv_y, 2: out_y}, nz, 10)
     o_side = o_side.reshape(-1)
     per = width // quads
     perl = kvr // quads
@@ -1188,7 +1265,7 @@
     stats = jnp.sqrt(jnp.sum(o_stat[:5], axis=1) / (tok * n_dev * width))
     return (
         stream_out, grad_stream, stats, ga, o_q, o_lat[:, :kvr], o_lat[:, kvr:lanes], gla, o_kv, o_out, gf,
-        o_router[:, :experts], back[0], back[1], grad_sd[:fs], jnp.swapaxes(grad_eg[None], 1, 2), jnp.swapaxes(grad_eu[None], 1, 2), grad_ed[None],
+        o_router[:, :experts], back[0], back[1], grad_sd[:fs], jnp.swapaxes(grad_eg.astype(f32)[None], 1, 2), jnp.swapaxes(grad_eu.astype(f32)[None], 1, 2), grad_ed.astype(f32)[None],
     )
 
 

time: 760 us -> 750 us (0.987)
  Pallas kernels: 600 us -> 556 us
  other arithmetic: 29.8 us -> 45.3 us
  waiting for transfers between devices: 0.03 us -> 9.06 us
    pallas_call x1, Pallas kernels: 125 us -> 98.5 us  [experts_both(): pl.pallas_call(functools.partial(experts_kernel, slots=blocks * capacity)...]
    pallas_call x2, Pallas kernels: 250 us -> 235 us  [the longest x1 147 us: finish(): pl.pallas_call(functools.partial(finish_kernel, nz, na, tuple(swapped)),...]
    ppermute x2 -> x4, waiting for transfers between devices: 0.01 us -> 9.04 us  [swap(): return lax.ppermute(v, ('rep', 'shard'), pairs)]
    transpose x0 -> x2, other arithmetic: none -> 8.57 us  [the longest x1 5.27 us: on_device(): jnp.swapaxes(grad_eu.astype(f32)[None], 1, 2)]
    unnamed x224 -> x208, local copies, waits for them, and re-layouts: 27.1 us -> 26.6 us
  transfers between devices with their start and end apart: 5 -> 7, of which waited for: 0 -> 1; matrix products, arithmetic and copies ran while one was open for 11% -> 13% of each run, Pallas kernels for 43% -> 41%
where the time goes in v3:
time: 750 us; the launch traced here: 741 us
  Pallas kernels  556 us (74%)
  local copies, waits for them, and re-layouts  57.7 us (8%)
  matrix products  46.2 us (6%)
  other arithmetic  45.3 us (6%)
  between operations  15.5 us (2%)
  starting transfers between devices  11.1 us (1%)
  waiting for transfers between devices  9.06 us (1%)
    pallas_call x1, Pallas kernels, finish(): pl.pallas_call(functools.partial(finish_kernel, nz, na, tuple(swapped)),...  147 us
    pallas_call x1, Pallas kernels, all_gather(): pl.pallas_call(functools.partial(gather_kernel, nz), out_shape=[jax.Shape...  112 us
    pallas_call x1, Pallas kernels, experts_both(): pl.pallas_call(functools.partial(experts_kernel, slots=blocks * capacity)...  98.5 us
    pallas_call x1, Pallas kernels, reduce_scatter(): pl.pallas_call(functools.partial(scatter_kernel, nz), out_shape=[sd((tok,...  88.3 us
    pallas_call x2, Pallas kernels, quad_scatter(): pl.pallas_call(quad_scatter_kernel, out_shape=jax.ShapeDtypeStruct((rows,...  46 us
    pallas_call x1, Pallas kernels, open_quad(): pl.pallas_call(functools.partial(open_kernel, nz), out_shape=[sd(shape, v...  41.2 us
    dot_general x20, matrix products, contract(): lax.dot_general(left, right, (over, batch), preferred_element_type=jnp.fl...  34.6 us
    unnamed x208, local copies, waits for them, and re-layouts  26.6 us
  transfers between devices with their start and end apart: 7, of which 1 were waited for; matrix products, arithmetic and copies ran while one was open for 13% of the time, Pallas kernels for 41%

profile of v3, /device:TPU:0, one launch (start us, length us, event | category | flops | bytes accessed | tf_op | source)
XLA Modules:
  0.0 740.6 jit_solution(17287055157085423460)
XLA Ops:
  12.1 2.8 copy-done.5
  17.7 41.2 %shard_map.331 = (bf16[4,128,2048]{2,1,0:T(8,128)(2,1)S(1)}, bf16[2,1024,768]{2,1,0:T(8,128)(2,1)S(1)}, bf16[2,256,1024]{2,1,0:T(8,128)(2,1)S(1)}, bf16[2,1024,5...) custom-call(bf16[128,2048]{1,0:T(8,128)(2,1)S(1)} %copy-done, bf16[1024,3072]{1,0:T(8,128)(2,1)S(1)} %copy-done.5, ...), custom_call_target="tpu_custom_call" | custom-call | bytes 175000000 | tf_op jit(solution)/shard_map/pallas_call | solution.py:544
  64.2 2.2 shard_map.334
  66.4 4.2 all-to-all-start
  70.6 2.5 convert_element_type.228
  74.8 4.6 copy.155
  89.1 2.8 fusion.4
  98.6 2.4 fusion.81
  101.0 3.1 fusion.19
  104.5 3.0 convolution_convert_fusion.4
  107.6 27.6 %shard_map.332.attn = f32[128,2048]{1,0:T(8,128)S(1)} custom-call(bf16[4,128,2048]{2,1,0:T(8,128)(2,1)S(1)} %bitcast.186), custom_call_target="tpu_custom_call" | custom-call | bytes 56000000 | tf_op jit(solution)/shard_map/pallas_call | solution.py:691
  138.9 111.6 %shard_map.333 = (bf16[32,128,2048]{2,1,0:T(8,128)(2,1)}, f32[32,32,128]{2,1,0:T(8,128)}) custom-call(bf16[128,2048]{1,0:T(8,128)(2,1)} %copy-done.34, f32[32,128]{1,0:T(8,128)} %pad_maximum_fusion.7.t_ref), custom_call_target="tpu_custom_call" | custom-call | bytes 297500000 | tf_op jit(solution)/shard_map/pallas_call | solution.py:212
  252.7 3.1 constant_dynamic-slice_fusion
  257.8 98.5 %shard_map.335 = (bf16[16,128,2048]{2,1,0:T(8,128)(2,1)}, bf16[16,128,2048]{2,1,0:T(8,128)(2,1)}, bf16[32,128,2176]{2,1,0:T(8,128)(2,1)}, bf16[1792,2048]{1,0:T(...) custom-call(bf16[32,128,2048]{2,1,0:T(8,128)(2,1)} %get-tuple-elemen, ...), custom_call_target="tpu_custom_call" | custom-call | bytes 385000000 | tf_op jit(solution)/shard_map/pallas_call | solution.py:1070
  356.3 88.3 %shard_map.336 = (f32[128,2176]{1,0:T(8,128)}, bf16[704,2048]{1,0:T(8,128)(2,1)}, bf16[704,2048]{1,0:T(8,128)(2,1)}, bf16[704,2048]{1,0:T(8,128)(2,1)}) custom-call(bf16[32,128,2176]{2,1,0:T(8,128)(2,1)} %get-tuple-element.62.x_ref, bf16[1792,2048]{1,0:T(8,128)(2,1)} %get-tuple-element.63.rows_in, bf16[1792,2048]{1,0:T(8,128)(2,1)} %get-tuple-element.64.rows_grad, ...), custom_call_target="tpu_custom_call" | custom-call | bytes 315000000 | tf_op jit(solution)/shard_map/pallas_call | solution.py:404
  449.5 2.1 multiply_reduce_fusion.2
  453.9 19.4 %shard_map.337 = bf16[4,128,2176]{2,1,0:T(8,128)(2,1)} custom-call(bf16[128,2176]{1,0:T(8,128)(2,1)} %fusion.35.x_ref), custom_call_target="tpu_custom_call" | custom-call | bytes 63000000 | tf_op jit(solution)/shard_map/pallas_call | solution.py:637
  473.3 3.5 fusion.14
  477.5 3.8 convolution_bitcast_fusion
  486.9 2.7 convolution_convert_fusion.3
  496.4 3.5 convolution_convert_fusion
  501.8 18.4 %shard_map.338 = f32[128,2048]{1,0:T(8,128)S(1)} custom-call(bf16[4,128,2048]{2,1,0:T(8,128)(2,1)S(1)} %bitcast.185), custom_call_target="tpu_custom_call" | custom-call | bytes 56000000 | tf_op jit(solution)/shard_map/pallas_call | solution.py:691
  520.2 3.3 convolution_convert_fusion.5
  527.4 3.3 bitcast_convert_fusion
  530.7 3.7 all-to-all-start.1
  536.4 5.3 convert_bitcast_fusion
  543.3 3.3 convert_bitcast_fusion.1
  548.1 2.5 fusion.77
  555.9 5.0 convolution_convert_fusion.1
  560.9 9.0 %collective-permute-done.2.refs_6_ = bf16[4,64,1024]{2,1,0:T(8,128)(2,1)} collective-permute-done((bf16[4,64,1024]{2,1,0:T(8,128)(2,1)}, bf16[4,64,1024]{2,1,0:T(8,128)(2,1)}, u32[]{:S(2)}, u32[]{:S(2)}) %collective-permute-start.2) | collective-permute-done | bytes 524320 | tf_op jit(solution)/shard_map/ppermute | solution.py:1092
  570.0 146.6 %shard_map.339 = (bf16[128,2048]{1,0:T(8,128)(2,1)}, f32[64,3072]{1,0:T(8,128)}, f32[16,4096]{1,0:T(8,128)}, f32[64,2048]{1,0:T(8,128)}, f32[64,640]{1,0:T(8,128...) custom-call(bf16[16,128,2048]{2,1,0:T(8,128)(2,1)} %get-tuple-element.60.own, ...), custom_call_target="tpu_custom_call" | custom-call | bytes 455000000 | tf_op jit(solution)/shard_map/pallas_call | solution.py:959
  724.9 2.6 fusion.32
  (328 shorter events, 89.2 us)
Async XLA Ops:
  7.2 250.6 %all-gather.3.cloned.1.call-start = ((), (), s32[]{:S(2)}) async-start(), calls=%async_computation.2 | async-start | bytes 17301504 | tf_op jit(solution)/shard_map/all_gather | solution.py:1135
  61.9 21.9 %copy-start.13 = (bf16[2,256,1024]{2,1,0:T(8,128)(2,1)}, bf16[2,256,1024]{2,1,0:T(8,128)(2,1)S(1)}, u32[]{:S(2)}) copy-start(bf16[2,256,1024]{2,1,0:T(8,128)(2,1)S(1)} %get-tuple-element.56) | copy-start | bytes 3145732
  66.4 191.3 %all-to-all-start = ((bf16[32,64,256]{2,1,0:T(8,128)(2,1)}), bf16[32,64,256]{2,1,0:T(8,128)(2,1)}, u32[]{:S(2)}, u32[]{:S(2)}) async-start(bf16[32,64,256]{2,1,0:T(8,128)(2,1)} %shard_map.334), calls=%async_computation | async-start | bytes 2097152 | tf_op jit(solution)/shard_map/all_to_all | solution.py:1143
  79.6 56.6 %copy-start.78 = (f32[1,2048]{1,0:T(1,128)}, f32[1,2048]{1,0:T(1,128)S(1)}, u32[]{:S(2)}) copy-start(f32[1,2048]{1,0:T(1,128)S(1)} %get-tuple-element.197) | copy-start | bytes 24580
  79.6 176.3 %copy-start.70 = (f32[1,2048]{1,0:T(1,128)}, f32[1,2048]{1,0:T(1,128)S(1)}, u32[]{:S(2)}) copy-start(f32[1,2048]{1,0:T(1,128)S(1)} %get-tuple-element.198) | copy-start | bytes 24580
  89.1 6.4 copy-start.55
  107.5 27.6 %copy-start.1 = (bf16[128,2048]{1,0:T(8,128)(2,1)S(1)}, bf16[128,2048]{1,0:T(8,128)(2,1)}, u32[]{:S(2)}) copy-start(bf16[128,2048]{1,0:T(8,128)(2,1)} %stream.3) | copy-start | bytes 1572868
  135.5 115.0 %copy-start.69 = (bf16[88,2048]{1,0:T(8,128)(2,1)S(1)}, bf16[88,2048]{1,0:T(8,128)(2,1)}, u32[]{:S(2)}) copy-start(bf16[88,2048]{1,0:T(8,128)(2,1)} %param.36) | copy-start | bytes 1081348
  136.8 119.0 %copy-start.86 = (f32[128]{0:T(128)}, f32[128]{0:T(128)S(1)}, u32[]{:S(2)}) copy-start(f32[128]{0:T(128)S(1)} %get-tuple-element.224) | copy-start | bytes 1540
  136.9 118.9 %copy-start.44 = (f32[128,16]{1,0:T(8,128)}, f32[128,16]{1,0:T(8,128)S(1)}, u32[]{:S(2)}) copy-start(f32[128,16]{1,0:T(8,128)S(1)} %copy.163) | copy-start | bytes 24580
  137.0 118.8 %copy-start.53 = (f32[128,16]{1,0:T(8,128)}, f32[128,16]{1,0:T(8,128)S(1)}, u32[]{:S(2)}) copy-start(f32[128,16]{1,0:T(8,128)S(1)} %copy.162) | copy-start | bytes 24580
  137.1 118.7 %copy-start.54 = (f32[128,16]{1,0:T(8,128)}, f32[128,16]{1,0:T(8,128)S(1)}, u32[]{:S(2)}) copy-start(f32[128,16]{1,0:T(8,128)S(1)} %copy.161) | copy-start | bytes 24580
  137.3 118.5 %copy-start.87 = (f32[128]{0:T(128)}, f32[128]{0:T(128)S(1)}, u32[]{:S(2)}) copy-start(f32[128]{0:T(128)S(1)} %fusion.58) | copy-start | bytes 1540
  138.2 117.6 %copy-start.92 = (f32[128]{0:T(128)}, f32[128]{0:T(128)S(1)}, u32[]{:S(2)}) copy-start(f32[128]{0:T(128)S(1)} %get-tuple-element.184) | copy-start | bytes 1540
  445.4 6.2 copy-start.18
  445.4 6.2 copy-start.45
  445.4 6.2 copy-start.79
  445.4 6.2 copy-start.90
  445.4 6.2 copy-start.97
  493.1 32.0 %copy-start.24 = (bf16[512,1024]{1,0:T(8,128)(2,1)}, bf16[512,1024]{1,0:T(8,128)(2,1)S(1)}, u32[]{:S(2)}) copy-start(bf16[512,1024]{1,0:T(8,128)(2,1)S(1)} %convolution_convert_fusion.6) | copy-start | bytes 3145732
  494.0 47.6 %collective-permute-start = (bf16[512,576]{0,1:T(8,128)(2,1)}, bf16[512,576]{0,1:T(8,128)(2,1)}, u32[]{:S(2)}, u32[]{:S(2)}) collective-permute-start(bf16[512,576]{0,1:T(8,128)(2,1)} %pad_maximum_fusion.2), channel_id=1, source_target_pairs={{1,0},{0,1},{3,2},{2,3},{5,4},{4,5},{7,6},{6,7},{9,8},{8,9},{11,10... | collective-permute-start | bytes 1769480 | tf_op jit(solution)/shard_map/ppermute | solution.py:1092
  524.5 45.4 %collective-permute-start.3 = (bf16[4,64,2048]{2,1,0:T(8,128)(2,1)}, bf16[4,64,2048]{2,1,0:T(8,128)(2,1)}, u32[]{:S(2)}, u32[]{:S(2)}) collective-permute-start(bf16[4,64,2048]{2,1,0:T(8,128)(2,1)} %dynamic-slice_bitcast_fusion), channel_id=1, source_target_pairs={{4,0},{5,1},{6,2},{7,3},{0,4},{1,5},{2,6},{3,7},{12,8},{13,9},{14,... | collective-permute-start | bytes 3145736 | tf_op jit(solution)/shard_map/ppermute | solution.py:1092
  525.9 44.0 %collective-permute-start.2 = (bf16[4,64,1024]{2,1,0:T(8,128)(2,1)}, bf16[4,64,1024]{2,1,0:T(8,128)(2,1)}, u32[]{:S(2)}, u32[]{:S(2)}) collective-permute-start(bf16[4,64,1024]{2,1,0:T(8,128)(2,1)} %dynamic-slice_bitcast_fusion.1), channel_id=1, source_target_pairs={{4,0},{5,1},{6,2},{7,3},{0,4},{1,5},{2,6},{3,7},{12,8},{13,9},{14,... | collective-permute-start | bytes 1572872 | tf_op jit(solution)/shard_map/ppermute | solution.py:1092
  530.7 196.8 %all-to-all-start.1 = ((bf16[32,64,256]{2,1,0:T(8,128)(2,1)}), bf16[32,64,256]{2,1,0:T(8,128)(2,1)S(1)}, u32[]{:S(2)}, u32[]{:S(2)}) async-start(bf16[32,64,256]{2,1,0:T(8,128)(2,1)} %bitcast.215), calls=%async_computation.1 | async-start | bytes 2097152 | tf_op jit(solution)/shard_map/all_to_all | solution.py:1187
  536.4 5.3 copy-start.47
  536.4 6.9 copy-start.41
  542.9 3.7 collective-permute-start.1
  569.9 154.9 %copy-start.3 = (bf16[128,2048]{1,0:T(8,128)(2,1)S(1)}, bf16[128,2048]{1,0:T(8,128)(2,1)}, u32[]{:S(2)}) copy-start(bf16[128,2048]{1,0:T(8,128)(2,1)} %stream.3) | copy-start | bytes 1572868
  569.9 154.9 %copy-start.39 = (f32[128,2048]{1,0:T(8,128)S(1)}, f32[128,2048]{1,0:T(8,128)}, u32[]{:S(2)}) copy-start(f32[128,2048]{1,0:T(8,128)} %get-tuple-element.181) | copy-start | bytes 3145732
  569.9 154.9 %copy-start.96 = (f32[128]{0:T(128)S(1)}, f32[128]{0:T(128)}, u32[]{:S(2)}) copy-start(f32[128]{0:T(128)} %get-tuple-element.216) | copy-start | bytes 1540
  724.9 6.3 copy-start.57
  727.4 5.4 copy-start.61
  (75 other events, 142.0 us)
Sparse Core Ops, SparseCore 0:
  62.1 173.3 all-gather.2

commit v4 on v3

--- a/solution.py
+++ b/solution.py
@@ -239,6 +239,12 @@
         return carry
 
     lax.fori_loop(0, count // step, body, 0)
+
+
+SCATTERING = [
+    ("s0", 0), ("s0", 1), ("n", 0), ("c", 0), ("f", 0), ("c", 1), ("c", 2), ("f", 1), ("s0", 2), ("s2", 0), ("n", 1), ("f", 2),
+    ("s0", 3), ("s2", 1), ("n", 2), ("s2", 2), ("f", 3), ("n", 3), ("c", 3), ("s2", 3),
+]
 
 
 def scatter_kernel(nz, x_ref, rows_in, rows_grad, hid, dg, du, o_ref, dwg_o, dwu_o, dwd_o, mine, core, one, two, line,
@@ -339,15 +345,14 @@
             if n in (0, 2):
                 one_copy(1, zb, xb).start()
 
-    def stage1(zb):
-        for far in (True, False):
-            for h in (0, 1):
-                j = (1 - y if far else y) if h == 0 else (1 - x if far else x)
-                one_copy(h, zb, j).wait_recv()
-                k = place_of(zb, j, x) if h == 0 else place_of(zb, y, j)
-                add_rows(mine.at[k], one.at[h, zb * 2 + j], h * half, 0, half)
-                if far:
-                    two_copy(h, zb).start()
+    def stage1(zb, far):
+        for h in (0, 1):
+            j = (1 - y if far else y) if h == 0 else (1 - x if far else x)
+            one_copy(h, zb, j).wait_recv()
+            k = place_of(zb, j, x) if h == 0 else place_of(zb, y, j)
+            add_rows(mine.at[k], one.at[h, zb * 2 + j], h * half, 0, half)
+            if far:
+                two_copy(h, zb).start()
 
     def stage2(zb):
         k = place_of(zb, y, x)
@@ -362,14 +367,10 @@
             when(zb > z, lambda: line_copy(h, zb, True).start())
             when(zb < z, lambda: line_copy(h, zb, False).start())
 
-    for i in range(nz + 2):
-        if i < nz:
-            stage0(order[i])
-        chunk(i)
-        if 1 <= i < nz + 1:
-            stage1(order[i - 1])
-        if 2 <= i:
-            stage2(order[i - 2])
+    stages = dict(s0=stage0, f=lambda zb: stage1(zb, True), n=lambda zb: stage1(zb, False), s2=stage2)
+    plain = [(n, i) for i in range(max(nz, chunks)) for n in ("s0", "c", "f", "n", "s2") if n == "c" or i < nz]
+    for name, i in SCATTERING if nz == chunks == 4 else plain:
+        chunk(i) if name == "c" else stages[name](order[i])
     written(0)
     write(2)
     k = place_of(z, y, x)
@@ -701,6 +702,13 @@
     )(v)
 
 
+CLOSING = [
+    ("w0", 0), ("t0", 0), ("wa", 0), ("w0", 1), ("wb", 0), ("w0", 2), ("t0", 1), ("wb", 1), ("t1", 0), ("wa", 1), ("wa", 2),
+    ("w0", 3), ("t0", 2), ("t1", 1), ("t2", 0), ("wa", 3), ("wb", 2), ("t1", 2), ("t0", 3), ("t2", 1), ("t2", 2), ("t1", 3),
+    ("wb", 3), ("t2", 3),
+]
+
+
 def finish_kernel(nz, na, there, own, far, stream, attn, mid, *refs):
     ins, refs = refs[:na], refs[na:]
     others, refs = dict(zip(there, refs)), refs[len(there) :]
@@ -725,8 +733,8 @@
     nbr["from"] = (source, away)
     here_q = z * 2 + y
     for j in range(1, quads):
-        there = lax.rem(here_q + j, quads)
-        nbr["q%d" % j] = (device(there // 2, lax.rem(there, 2), c, x), None)
+        to_q = lax.rem(here_q + j, quads)
+        nbr["q%d" % j] = (device(to_q // 2, lax.rem(to_q, 2), c, x), None)
     greet(nbr)
     order = far_first(nz, z)
     xdev, cdev, ddev, ydev = (nbr[k][0] for k in ("x", "c", "d", "y"))
@@ -805,8 +813,8 @@
             w_load(a, zb * 2 + 1 - y).wait()
             wy_copy(a, zb).start()
 
-    def w_stage1(zb):
-        for a in range(na):
+    def w_stage1(zb, some):
+        for a in some:
             total = mine[a].at[zb * 2 + y]
             w_load(a, zb * 2 + y).wait()
             d = wy_copy(a, zb)
@@ -830,16 +838,12 @@
             w_load(a, zb * 2 + y).start()
         for a in others:
             wy_copy(a, zb).start()
-    for i in range(nz):
-        if i < 2:
-            w_stage0(order[i])
-        t_stage0(order[i])
-    for i in range(nz):
-        t_stage1(order[i])
-        if i + 2 < nz:
-            w_stage0(order[i + 2])
-        w_stage1(order[i])
-        t_stage2(order[i])
+    stages = dict(
+        w0=w_stage0, t0=t_stage0, t1=t_stage1, t2=t_stage2,
+        wa=lambda zb: w_stage1(zb, there), wb=lambda zb: w_stage1(zb, apart),
+    )
+    for name, i in CLOSING if nz == 4 else [(n, i) for i in range(nz) for n in ("w0", "t0", "wa", "wb", "t1", "t2")]:
+        stages[name](order[i])
 
     here = t_mine.at[place_of(z, y, x)]
     for right, ok in ((True, z >= 1), (False, z + 1 < nz)):

time: 750 us -> 723 us (0.964)
  Pallas kernels: 556 us -> 527 us
    pallas_call x1, Pallas kernels: 147 us -> 124 us  [finish(): pl.pallas_call(functools.partial(finish_kernel, nz, na, tuple(swapped)),...]
  transfers between devices with their start and end apart: 7 -> 7, of which waited for: 1 -> 1; matrix products, arithmetic and copies ran while one was open for 13% -> 13% of each run, Pallas kernels for 41% -> 40%
where the time goes in v4:
time: 723 us; the launch traced here: 712 us
  Pallas kernels  527 us (73%)
  local copies, waits for them, and re-layouts  57.7 us (8%)
  matrix products  46.3 us (6%)
  other arithmetic  45.3 us (6%)
  between operations  15.5 us (2%)
  starting transfers between devices  11.3 us (2%)
  waiting for transfers between devices  8.96 us (1%)
    pallas_call x1, Pallas kernels, finish(): pl.pallas_call(functools.partial(finish_kernel, nz, na, tuple(swapped)),...  124 us
    pallas_call x1, Pallas kernels, all_gather(): pl.pallas_call(functools.partial(gather_kernel, nz), out_shape=[jax.Shape...  112 us
    pallas_call x1, Pallas kernels, experts_both(): pl.pallas_call(functools.partial(experts_kernel, slots=blocks * capacity)...  98.5 us
    pallas_call x1, Pallas kernels, reduce_scatter(): pl.pallas_call(functools.partial(scatter_kernel, nz), out_shape=[sd((tok,...  82.3 us
    pallas_call x2, Pallas kernels, quad_scatter(): pl.pallas_call(quad_scatter_kernel, out_shape=jax.ShapeDtypeStruct((rows,...  46.1 us
    pallas_call x1, Pallas kernels, open_quad(): pl.pallas_call(functools.partial(open_kernel, nz), out_shape=[sd(shape, v...  41.2 us
    dot_general x20, matrix products, contract(): lax.dot_general(left, right, (over, batch), preferred_element_type=jnp.fl...  34.6 us
    unnamed x208, local copies, waits for them, and re-layouts  26.6 us
  transfers between devices with their start and end apart: 7, of which 1 were waited for; matrix products, arithmetic and copies ran while one was open for 13% of the time, Pallas kernels for 40%

profile of v4, /device:TPU:0, one launch (start us, length us, event | category | flops | bytes accessed | tf_op | source)
XLA Modules:
  0.0 712.0 jit_solution(15487556016235026326)
XLA Ops:
  12.1 2.8 copy-done.5
  17.7 41.2 %shard_map.331 = (bf16[4,128,2048]{2,1,0:T(8,128)(2,1)S(1)}, bf16[2,1024,768]{2,1,0:T(8,128)(2,1)S(1)}, bf16[2,256,1024]{2,1,0:T(8,128)(2,1)S(1)}, bf16[2,1024,5...) custom-call(bf16[128,2048]{1,0:T(8,128)(2,1)S(1)} %copy-done, bf16[1024,3072]{1,0:T(8,128)(2,1)S(1)} %copy-done.5, ...), custom_call_target="tpu_custom_call" | custom-call | bytes 175000000 | tf_op jit(solution)/shard_map/pallas_call | solution.py:545
  64.2 2.2 shard_map.334
  66.4 4.2 all-to-all-start
  70.6 2.5 convert_element_type.228
  74.8 4.6 copy.155
  89.1 2.8 fusion.4
  98.6 2.4 fusion.81
  101.0 3.1 fusion.19
  104.5 3.0 convolution_convert_fusion.4
  107.6 27.6 %shard_map.332.attn = f32[128,2048]{1,0:T(8,128)S(1)} custom-call(bf16[4,128,2048]{2,1,0:T(8,128)(2,1)S(1)} %bitcast.186), custom_call_target="tpu_custom_call" | custom-call | bytes 56000000 | tf_op jit(solution)/shard_map/pallas_call | solution.py:692
  138.9 111.6 %shard_map.333 = (bf16[32,128,2048]{2,1,0:T(8,128)(2,1)}, f32[32,32,128]{2,1,0:T(8,128)}) custom-call(bf16[128,2048]{1,0:T(8,128)(2,1)} %copy-done.34, f32[32,128]{1,0:T(8,128)} %pad_maximum_fusion.7.t_ref), custom_call_target="tpu_custom_call" | custom-call | bytes 297500000 | tf_op jit(solution)/shard_map/pallas_call | solution.py:212
  252.7 3.1 constant_dynamic-slice_fusion
  257.8 98.5 %shard_map.335 = (bf16[16,128,2048]{2,1,0:T(8,128)(2,1)}, bf16[16,128,2048]{2,1,0:T(8,128)(2,1)}, bf16[32,128,2176]{2,1,0:T(8,128)(2,1)}, bf16[1792,2048]{1,0:T(...) custom-call(bf16[32,128,2048]{2,1,0:T(8,128)(2,1)} %get-tuple-elemen, ...), custom_call_target="tpu_custom_call" | custom-call | bytes 385000000 | tf_op jit(solution)/shard_map/pallas_call | solution.py:1074
  356.3 82.3 %shard_map.336 = (f32[128,2176]{1,0:T(8,128)}, bf16[704,2048]{1,0:T(8,128)(2,1)}, bf16[704,2048]{1,0:T(8,128)(2,1)}, bf16[704,2048]{1,0:T(8,128)(2,1)}) custom-call(bf16[32,128,2176]{2,1,0:T(8,128)(2,1)} %get-tuple-element.62.x_ref, bf16[1792,2048]{1,0:T(8,128)(2,1)} %get-tuple-element.63.rows_in, bf16[1792,2048]{1,0:T(8,128)(2,1)} %get-tuple-element.64.rows_grad, ...), custom_call_target="tpu_custom_call" | custom-call | bytes 315000000 | tf_op jit(solution)/shard_map/pallas_call | solution.py:405
  443.6 2.1 multiply_reduce_fusion.2
  447.9 19.5 %shard_map.337 = bf16[4,128,2176]{2,1,0:T(8,128)(2,1)} custom-call(bf16[128,2176]{1,0:T(8,128)(2,1)} %fusion.35.x_ref), custom_call_target="tpu_custom_call" | custom-call | bytes 63000000 | tf_op jit(solution)/shard_map/pallas_call | solution.py:638
  467.4 3.5 fusion.14
  471.6 3.8 convolution_bitcast_fusion
  481.0 2.7 convolution_convert_fusion.3
  490.5 3.5 convolution_convert_fusion
  495.8 18.5 %shard_map.338 = f32[128,2048]{1,0:T(8,128)S(1)} custom-call(bf16[4,128,2048]{2,1,0:T(8,128)(2,1)S(1)} %bitcast.185), custom_call_target="tpu_custom_call" | custom-call | bytes 56000000 | tf_op jit(solution)/shard_map/pallas_call | solution.py:692
  514.4 3.3 convolution_convert_fusion.5
  521.6 3.3 bitcast_convert_fusion
  524.9 3.9 all-to-all-start.1
  530.8 5.3 convert_bitcast_fusion
  537.7 3.3 convert_bitcast_fusion.1
  542.5 2.5 fusion.77
  550.3 5.0 convolution_convert_fusion.1
  555.3 8.9 %collective-permute-done.2.refs_6_ = bf16[4,64,1024]{2,1,0:T(8,128)(2,1)} collective-permute-done((bf16[4,64,1024]{2,1,0:T(8,128)(2,1)}, bf16[4,64,1024]{2,1,0:T(8,128)(2,1)}, u32[]{:S(2)}, u32[]{:S(2)}) %collective-permute-start.2) | collective-permute-done | bytes 524320 | tf_op jit(solution)/shard_map/ppermute | solution.py:1096
  564.3 123.7 %shard_map.339 = (bf16[128,2048]{1,0:T(8,128)(2,1)}, f32[64,3072]{1,0:T(8,128)}, f32[16,4096]{1,0:T(8,128)}, f32[64,2048]{1,0:T(8,128)}, f32[64,640]{1,0:T(8,128...) custom-call(bf16[16,128,2048]{2,1,0:T(8,128)(2,1)} %get-tuple-element.60.own, ...), custom_call_target="tpu_custom_call" | custom-call | bytes 455000000 | tf_op jit(solution)/shard_map/pallas_call | solution.py:963
  696.3 2.6 fusion.32
  (328 shorter events, 89.1 us)
Async XLA Ops:
  7.2 250.6 %all-gather.3.cloned.1.call-start = ((), (), s32[]{:S(2)}) async-start(), calls=%async_computation.2 | async-start | bytes 17301504 | tf_op jit(solution)/shard_map/all_gather | solution.py:1139
  61.9 21.9 %copy-start.13 = (bf16[2,256,1024]{2,1,0:T(8,128)(2,1)}, bf16[2,256,1024]{2,1,0:T(8,128)(2,1)S(1)}, u32[]{:S(2)}) copy-start(bf16[2,256,1024]{2,1,0:T(8,128)(2,1)S(1)} %get-tuple-element.56) | copy-start | bytes 3145732
  66.4 191.3 %all-to-all-start = ((bf16[32,64,256]{2,1,0:T(8,128)(2,1)}), bf16[32,64,256]{2,1,0:T(8,128)(2,1)}, u32[]{:S(2)}, u32[]{:S(2)}) async-start(bf16[32,64,256]{2,1,0:T(8,128)(2,1)} %shard_map.334), calls=%async_computation | async-start | bytes 2097152 | tf_op jit(solution)/shard_map/all_to_all | solution.py:1147
  79.6 56.6 %copy-start.78 = (f32[1,2048]{1,0:T(1,128)}, f32[1,2048]{1,0:T(1,128)S(1)}, u32[]{:S(2)}) copy-start(f32[1,2048]{1,0:T(1,128)S(1)} %get-tuple-element.197) | copy-start | bytes 24580
  79.6 176.3 %copy-start.70 = (f32[1,2048]{1,0:T(1,128)}, f32[1,2048]{1,0:T(1,128)S(1)}, u32[]{:S(2)}) copy-start(f32[1,2048]{1,0:T(1,128)S(1)} %get-tuple-element.198) | copy-start | bytes 24580
  89.1 6.4 copy-start.55
  107.5 27.6 %copy-start.1 = (bf16[128,2048]{1,0:T(8,128)(2,1)S(1)}, bf16[128,2048]{1,0:T(8,128)(2,1)}, u32[]{:S(2)}) copy-start(bf16[128,2048]{1,0:T(8,128)(2,1)} %stream.3) | copy-start | bytes 1572868
  135.5 115.0 %copy-start.69 = (bf16[88,2048]{1,0:T(8,128)(2,1)S(1)}, bf16[88,2048]{1,0:T(8,128)(2,1)}, u32[]{:S(2)}) copy-start(bf16[88,2048]{1,0:T(8,128)(2,1)} %param.36) | copy-start | bytes 1081348
  136.8 119.0 %copy-start.86 = (f32[128]{0:T(128)}, f32[128]{0:T(128)S(1)}, u32[]{:S(2)}) copy-start(f32[128]{0:T(128)S(1)} %get-tuple-element.224) | copy-start | bytes 1540
  136.9 118.9 %copy-start.44 = (f32[128,16]{1,0:T(8,128)}, f32[128,16]{1,0:T(8,128)S(1)}, u32[]{:S(2)}) copy-start(f32[128,16]{1,0:T(8,128)S(1)} %copy.163) | copy-start | bytes 24580
  137.0 118.8 %copy-start.53 = (f32[128,16]{1,0:T(8,128)}, f32[128,16]{1,0:T(8,128)S(1)}, u32[]{:S(2)}) copy-start(f32[128,16]{1,0:T(8,128)S(1)} %copy.162) | copy-start | bytes 24580
  137.1 118.7 %copy-start.54 = (f32[128,16]{1,0:T(8,128)}, f32[128,16]{1,0:T(8,128)S(1)}, u32[]{:S(2)}) copy-start(f32[128,16]{1,0:T(8,128)S(1)} %copy.161) | copy-start | bytes 24580
  137.3 118.5 %copy-start.87 = (f32[128]{0:T(128)}, f32[128]{0:T(128)S(1)}, u32[]{:S(2)}) copy-start(f32[128]{0:T(128)S(1)} %fusion.58) | copy-start | bytes 1540
  138.2 117.6 %copy-start.92 = (f32[128]{0:T(128)}, f32[128]{0:T(128)S(1)}, u32[]{:S(2)}) copy-start(f32[128]{0:T(128)S(1)} %get-tuple-element.184) | copy-start | bytes 1540
  439.4 6.2 copy-start.18
  439.4 6.2 copy-start.45
  439.5 6.2 copy-start.79
  439.5 6.2 copy-start.90
  439.5 6.2 copy-start.97
  487.2 32.7 %copy-start.24 = (bf16[512,1024]{1,0:T(8,128)(2,1)}, bf16[512,1024]{1,0:T(8,128)(2,1)S(1)}, u32[]{:S(2)}) copy-start(bf16[512,1024]{1,0:T(8,128)(2,1)S(1)} %convolution_convert_fusion.6) | copy-start | bytes 3145732
  488.1 48.0 %collective-permute-start = (bf16[512,576]{0,1:T(8,128)(2,1)}, bf16[512,576]{0,1:T(8,128)(2,1)}, u32[]{:S(2)}, u32[]{:S(2)}) collective-permute-start(bf16[512,576]{0,1:T(8,128)(2,1)} %pad_maximum_fusion.2), channel_id=1, source_target_pairs={{1,0},{0,1},{3,2},{2,3},{5,4},{4,5},{7,6},{6,7},{9,8},{8,9},{11,10... | collective-permute-start | bytes 1769480 | tf_op jit(solution)/shard_map/ppermute | solution.py:1096
  518.7 45.6 %collective-permute-start.3 = (bf16[4,64,2048]{2,1,0:T(8,128)(2,1)}, bf16[4,64,2048]{2,1,0:T(8,128)(2,1)}, u32[]{:S(2)}, u32[]{:S(2)}) collective-permute-start(bf16[4,64,2048]{2,1,0:T(8,128)(2,1)} %dynamic-slice_bitcast_fusion), channel_id=1, source_target_pairs={{4,0},{5,1},{6,2},{7,3},{0,4},{1,5},{2,6},{3,7},{12,8},{13,9},{14,... | collective-permute-start | bytes 3145736 | tf_op jit(solution)/shard_map/ppermute | solution.py:1096
  520.7 43.5 %collective-permute-start.2 = (bf16[4,64,1024]{2,1,0:T(8,128)(2,1)}, bf16[4,64,1024]{2,1,0:T(8,128)(2,1)}, u32[]{:S(2)}, u32[]{:S(2)}) collective-permute-start(bf16[4,64,1024]{2,1,0:T(8,128)(2,1)} %dynamic-slice_bitcast_fusion.1), channel_id=1, source_target_pairs={{4,0},{5,1},{6,2},{7,3},{0,4},{1,5},{2,6},{3,7},{12,8},{13,9},{14,... | collective-permute-start | bytes 1572872 | tf_op jit(solution)/shard_map/ppermute | solution.py:1096
  524.9 174.0 %all-to-all-start.1 = ((bf16[32,64,256]{2,1,0:T(8,128)(2,1)}), bf16[32,64,256]{2,1,0:T(8,128)(2,1)S(1)}, u32[]{:S(2)}, u32[]{:S(2)}) async-start(bf16[32,64,256]{2,1,0:T(8,128)(2,1)} %bitcast.215), calls=%async_computation.1 | async-start | bytes 2097152 | tf_op jit(solution)/shard_map/all_to_all | solution.py:1191
  530.8 5.3 copy-start.47
  530.8 6.9 copy-start.41
  537.3 3.7 collective-permute-start.1
  564.3 132.0 %copy-start.3 = (bf16[128,2048]{1,0:T(8,128)(2,1)S(1)}, bf16[128,2048]{1,0:T(8,128)(2,1)}, u32[]{:S(2)}) copy-start(bf16[128,2048]{1,0:T(8,128)(2,1)} %stream.3) | copy-start | bytes 1572868
  564.3 132.0 %copy-start.39 = (f32[128,2048]{1,0:T(8,128)S(1)}, f32[128,2048]{1,0:T(8,128)}, u32[]{:S(2)}) copy-start(f32[128,2048]{1,0:T(8,128)} %get-tuple-element.181) | copy-start | bytes 3145732
  564.3 132.0 %copy-start.96 = (f32[128]{0:T(128)S(1)}, f32[128]{0:T(128)}, u32[]{:S(2)}) copy-start(f32[128]{0:T(128)} %get-tuple-element.216) | copy-start | bytes 1540
  696.3 6.3 copy-start.57
  698.9 5.4 copy-start.61
  (75 other events, 141.8 us)
Sparse Core Ops, SparseCore 0:
  62.1 173.3 all-gather.2
